TPU v7x, 256 devices: a whole 4x4x8 slice. The times are simulated.
256 devices in a mesh: frames: 32 (over y_hi, z, core), heads: 8 (over x, y_lo).
Axes of the slice: x: 4, y: 4 (y_hi: 2, y_lo: 2; y = y_hi * 2 + y_lo), z: 8, core: 2. Of those that a mesh axis runs over, the one named last changes fastest.
Arguments:
- tokens: bfloat16 [16384, 1024], P('frames', 'heads'), may hold values from -5 to 5
- norm_gain: float32 [1024], replicated, may hold values from 0.5 to 1.5
- norm_bias: float32 [1024], replicated, may hold values from -2.5 to 2.5
- w_query: bfloat16 [1024, 1024], P(None, 'heads'), may hold values from -0.375 to 0.375
- w_key: bfloat16 [1024, 1024], P(None, 'heads'), may hold values from -3.225 to 3.225
- w_value: bfloat16 [1024, 1024], P(None, 'heads'), may hold values from -0.1875 to 0.1875
- w_out: bfloat16 [1024, 1024], P('heads'), may hold values from -0.1875 to 0.1875
- layer_scale: float32 [1024], P('heads'), may hold values from 0.3 to 3
Outputs:
- layer_out: bfloat16 [16384, 1024], P('frames', 'heads')
All inputs are finite; a program needn't handle non-finite values.
Results may differ from a plain program's by a relative error of at most 0.0092.
Values may be sent and summed in bfloat16 or wider, within the bound.
No kernel may reach another device: no remote copies, remote signals or barrier semaphores. Data moves between devices by JAX's collectives and lax.ppermute only.
A program may use at most 64 MiB of HBM per device.

v0:
```python
import functools

import jax
import jax.numpy as jnp
from jax import lax
from jax.experimental import pallas as pl
from jax.experimental.pallas import tpu as pltpu
from jax.sharding import PartitionSpec as P

HEAD_DIM = 64
HALF = 512
BLOCK = 1024
TILE = 512
FEATURES = 1024
LOG2E = 1.4426950408889634
SCORE_SCALE = HEAD_DIM ** (-0.5) * LOG2E
PACK_ROWS = 80

Y_HI, Z, CORE = 2, 8, 2


def frames_shift(dy, dz, dc):
    pairs = []
    for y in range(Y_HI):
        for z in range(Z):
            for c in range(CORE):
                source = (y * Z + z) * CORE + c
                target = ((y ^ dy) * Z + (z + dz) % Z) * CORE + (c ^ dc)
                pairs.append((source, target))
    return pairs


def send(array, dy, dz, dc):
    return lax.ppermute(array, "frames", frames_shift(dy, dz, dc))


X, Y_LO = 4, 2
STEPS = ((0, 0), (0, 1), (1, 0), (3, 0), (2, 0), (1, 1), (3, 1), (2, 1))


def heads_shift(dx, dy):
    return [
        (x * Y_LO + y, ((x + dx) % X) * Y_LO + (y ^ dy)) for x in range(X) for y in range(Y_LO)
    ]


def send_heads(array, step):
    return lax.ppermute(array, "heads", heads_shift(*step))


def params(limit=48):
    return pltpu.CompilerParams(vmem_limit_bytes=limit * 2**20)


def whole(count):
    return [pl.BlockSpec(memory_space=pltpu.VMEM)] * count


def prepare_kernel(
    place_ref, wq_hbm, wk_hbm, wv_hbm, w_out_hbm, gain_hbm, bias_hbm, scale_hbm,
    w_ref, out_ref, vectors_ref,
    wq_ref, wk_ref, wv_ref, w_out_ref, gain_ref, bias_ref, scale_ref, flipped_ref, done,
):
    pairs = (
        (wq_hbm, wq_ref), (wk_hbm, wk_ref), (wv_hbm, wv_ref), (w_out_hbm, w_out_ref),
        (gain_hbm, gain_ref), (bias_hbm, bias_ref), (scale_hbm, scale_ref),
    )
    copies = [pltpu.make_async_copy(a, b, done.at[n]) for n, (a, b) in enumerate(pairs)]
    for copy in copies:
        copy.start()
    for copy in copies:
        copy.wait()
    core = place_ref[0]
    heads = [pl.ds(pl.multiple_of(h * HEAD_DIM, HEAD_DIM), HEAD_DIM) for h in (core, 1 - core)]
    count = len(STEPS)
    width = FEATURES // count

    def columns(n):
        return pl.ds(pl.multiple_of(place_ref[n] * width, width), width)

    for k, ref in enumerate((wq_ref, wk_ref, wv_ref)):
        flipped_ref[...] = ref[...].T
        for h, rows in enumerate(heads):
            at = (3 * h + k) * HEAD_DIM
            for n in range(count):
                w_ref[at : at + HEAD_DIM, n * width : (n + 1) * width] = flipped_ref[
                    rows, columns(1 + n)
                ]
    for h, rows in enumerate(heads):
        for n in range(count):
            out_ref[h * HEAD_DIM : (h + 1) * HEAD_DIM, n * width : (n + 1) * width] = w_out_ref[
                rows, columns(1 + count + n)
            ]
    for n in range(count):
        j = place_ref[1 + n]
        vectors_ref[n : n + 1, :] = gain_ref[pl.ds(j, 1), :]
        vectors_ref[count + n : count + n + 1, :] = bias_ref[pl.ds(j, 1), :]
    vectors_ref[2 * count : 3 * count, :] = jnp.broadcast_to(scale_ref[...], (count, width))


def prepare(place, wq, wk, wv, w_out, gain, bias, scale):
    return pl.pallas_call(
        prepare_kernel,
        out_shape=(
            jax.ShapeDtypeStruct((6 * HEAD_DIM, FEATURES), jnp.bfloat16),
            jax.ShapeDtypeStruct((2 * HEAD_DIM, FEATURES), jnp.bfloat16),
            jax.ShapeDtypeStruct((3 * len(STEPS), FEATURES // len(STEPS)), jnp.float32),
        ),
        in_specs=[pl.BlockSpec(memory_space=pltpu.SMEM)]
        + [pl.BlockSpec(memory_space=pltpu.MemorySpace.HBM)] * 7,
        out_specs=tuple(whole(3)),
        scratch_shapes=[
            pltpu.VMEM(a.shape, a.dtype) for a in (wq, wk, wv, w_out, gain, bias, scale)
        ]
        + [pltpu.VMEM((2 * HEAD_DIM, FEATURES), jnp.bfloat16), pltpu.SemaphoreType.DMA((7,))],
        compiler_params=params(),
        name="prepare",
        cost_estimate=pl.CostEstimate(
            flops=2 * HALF * FEATURES * 384, bytes_accessed=4 * 2**20, transcendentals=0
        ),
    )(place, wq, wk, wv, w_out, gain, bias, scale)


def project_kernel(*refs):
    x_refs = refs[:8]
    vectors_ref, w_ref, keep, give, normed_ref = refs[8:]
    count = len(x_refs)
    width = x_refs[0].shape[1]
    total = jnp.zeros((HALF, width), jnp.float32)
    for x_ref in x_refs:
        total = total + x_ref[...].astype(jnp.float32)
    mean = jnp.sum(total, axis=1, keepdims=True) * (1.0 / FEATURES)
    squares = jnp.zeros((HALF, width), jnp.float32)
    for x_ref in x_refs:
        centred = x_ref[...].astype(jnp.float32) - mean
        squares = squares + centred * centred
    variance = jnp.sum(squares, axis=1, keepdims=True) * (1.0 / FEATURES)
    inverse = lax.rsqrt(variance + 1e-06)
    for n, x_ref in enumerate(x_refs):
        centred = x_ref[...].astype(jnp.float32) - mean
        gain = vectors_ref[n : n + 1, :]
        bias = vectors_ref[count + n : count + n + 1, :]
        normed = centred * inverse * gain + bias
        normed_ref[:, n * width : (n + 1) * width] = normed.astype(jnp.bfloat16)
    for h, out in enumerate((keep, give)):
        out[...] = lax.dot_general(
            w_ref[h * 3 * HEAD_DIM : (h + 1) * 3 * HEAD_DIM, :],
            normed_ref[...],
            (((1,), (1,)), ((), ())),
            preferred_element_type=jnp.float32,
        ).astype(jnp.bfloat16)


def project(blocks, vectors, w):
    shape = jax.ShapeDtypeStruct((3 * HEAD_DIM, HALF), jnp.bfloat16)
    return pl.pallas_call(
        project_kernel,
        out_shape=(shape, shape),
        in_specs=whole(10),
        out_specs=tuple(whole(2)),
        scratch_shapes=[pltpu.VMEM((HALF, FEATURES), jnp.bfloat16)],
        compiler_params=params(),
        name="norm_project",
        cost_estimate=pl.CostEstimate(
            flops=2 * HALF * FEATURES * 384, bytes_accessed=2 * 2**20, transcendentals=HALF
        ),
    )(*blocks, vectors, w)


def join_kernel(keep, taken, q_ref, kv_ref):
    for ref, columns in ((keep, slice(0, HALF)), (taken, slice(HALF, 2 * HALF))):
        q_ref[:, columns] = ref[0:HEAD_DIM, :]
        kv_ref[:, columns] = ref[HEAD_DIM:, :]


def join(keep, taken):
    return pl.pallas_call(
        join_kernel,
        out_shape=(
            jax.ShapeDtypeStruct((HEAD_DIM, 2 * HALF), jnp.bfloat16),
            jax.ShapeDtypeStruct((2 * HEAD_DIM, 2 * HALF), jnp.bfloat16),
        ),
        in_specs=whole(2),
        out_specs=tuple(whole(2)),
        compiler_params=params(),
        name="join",
    )(keep, taken)


def attend_kernel(*refs, blocks, sets, work, fresh, pack):
    kv = refs[:blocks]
    queries = refs[blocks : blocks + sets]
    at = blocks + sets
    old = None
    if not fresh:
        old = refs[at : at + 3 * sets]
        at += 3 * sets
    new = None
    packs = refs[at : at + len(pack)]
    at += len(pack)
    if len(pack) < BLOCK // TILE:
        new = refs[at : at + 3 * sets]
        at += 3 * sets
    k_ref, s_ref = refs[at:]
    for b in range(blocks):
        k_ref[b * BLOCK : (b + 1) * BLOCK, :] = kv[b][0:HEAD_DIM, :].T

    steps = [
        (which, b, n == 0, n == len(chosen) - 1)
        for which, chosen in work
        for n, b in enumerate(chosen)
    ]
    tiles = BLOCK // TILE

    def score(step, columns, slot):
        which, b = step[:2]
        s = jnp.dot(
            k_ref[b * BLOCK : (b + 1) * BLOCK, :],
            queries[which][:, columns],
            preferred_element_type=jnp.float32,
        )
        s_ref[slot] = s
        return jnp.max(s, axis=0, keepdims=True)

    def one_tile(columns, next_columns, top, slot, packed):
        for n, (which, b, first, last) in enumerate(steps):
            if first:
                if fresh:
                    m = jnp.full((1, TILE), -jnp.inf, jnp.float32)
                    l = jnp.zeros((1, TILE), jnp.float32)
                    acc = jnp.zeros((HEAD_DIM, TILE), jnp.float32)
                else:
                    m, l, acc = (old[3 * which + i][:, columns] for i in range(3))
            newest = jnp.maximum(m, top)
            factor = jnp.exp2((m - newest) * SCORE_SCALE)
            if n + 1 < len(steps):
                top = score(steps[n + 1], columns, 1 - slot)
            elif next_columns is not None:
                top = score(steps[0], next_columns, 1 - slot)
            weights = jnp.exp2((s_ref[slot] - newest) * SCORE_SCALE)
            slot = 1 - slot
            l = l * factor + jnp.sum(weights, axis=0, keepdims=True)
            acc = acc * factor + jnp.dot(
                kv[b][HEAD_DIM:, :],
                weights.astype(jnp.bfloat16),
                preferred_element_type=jnp.float32,
            )
            m = newest
            if last and packed is None:
                new[3 * which][:, columns] = m
                new[3 * which + 1][:, columns] = l
                new[3 * which + 2][:, columns] = acc
            elif last:
                packed[0:HEAD_DIM, :] = (acc / l).astype(jnp.bfloat16)
                lse = m * SCORE_SCALE + jnp.log2(l)
                high = lse.astype(jnp.bfloat16).astype(jnp.float32)
                middle = (lse - high).astype(jnp.bfloat16).astype(jnp.float32)
                low = lse - high - middle
                row = lax.broadcasted_iota(jnp.int32, (PACK_ROWS - HEAD_DIM, TILE), 0)
                rows = jnp.where(row == 0, high, jnp.where(row == 1, middle, low))
                packed[HEAD_DIM:PACK_ROWS, :] = rows.astype(jnp.bfloat16)
        return top, slot

    if len(steps) % 2 == 0 and len(steps) > 2:

        def body(i, top):
            here = pl.ds(pl.multiple_of(i * TILE, TILE), TILE)
            after = pl.ds(pl.multiple_of(lax.rem(i + 1, tiles) * TILE, TILE), TILE)
            return one_tile(here, after, top, 0, None)[0]

        lax.fori_loop(0, tiles, body, score(steps[0], slice(0, TILE), 0))
    else:
        top, slot = score(steps[0], slice(0, TILE), 0), 0
        for i in range(tiles):
            here = slice(i * TILE, (i + 1) * TILE)
            after = slice((i + 1) * TILE, (i + 2) * TILE) if i + 1 < tiles else None
            packed = packs[pack.index(i)] if i in pack else None
            top, slot = one_tile(here, after, top, slot, packed)


def attend(kv, queries, states, work, pack=()):
    sets = len(queries)
    fresh = states is None
    width = BLOCK if not pack else TILE
    out_shape = [jax.ShapeDtypeStruct((PACK_ROWS, TILE), jnp.bfloat16)] * len(pack)
    if len(pack) < BLOCK // TILE:
        out_shape += [
            jax.ShapeDtypeStruct((1, width), jnp.float32),
            jax.ShapeDtypeStruct((1, width), jnp.float32),
            jax.ShapeDtypeStruct((HEAD_DIM, width), jnp.float32),
        ] * sets
    operands = list(kv) + list(queries) + ([] if fresh else list(states))
    count = sum(len(chosen) for _, chosen in work)
    return pl.pallas_call(
        functools.partial(
            attend_kernel, blocks=len(kv), sets=sets, work=work, fresh=fresh, pack=pack
        ),
        out_shape=tuple(out_shape),
        in_specs=whole(len(operands)),
        out_specs=tuple(whole(len(out_shape))),
        scratch_shapes=[
            pltpu.VMEM((len(kv) * BLOCK, HEAD_DIM), jnp.bfloat16),
            pltpu.VMEM((2, BLOCK, TILE), jnp.float32),
        ],
        compiler_params=params(),
        name="attend",
        cost_estimate=pl.CostEstimate(
            flops=count * 4 * BLOCK * BLOCK * HEAD_DIM * 4,
            bytes_accessed=2**20,
            transcendentals=count * BLOCK * BLOCK,
        ),
    )(*operands)


def unpack(pack_ref):
    split = pack_ref[HEAD_DIM:PACK_ROWS, :].astype(jnp.float32)
    return pack_ref[0:HEAD_DIM, :].astype(jnp.float32), split[0:1] + split[1:2] + split[2:3]


def merge(first, first_lse, second, second_lse):
    top = jnp.maximum(first_lse, second_lse)
    a = jnp.exp2(first_lse - top)
    b = jnp.exp2(second_lse - top)
    inverse = 1.0 / (a + b)
    return (first * (a * inverse) + second * (b * inverse)).astype(jnp.bfloat16)


def output_kernel(m_ref, l_ref, acc_ref, mine_ref, core_ref, diagonal_ref, w_ref, *out_refs):
    total = l_ref[...]
    here = merge(
        acc_ref[...] / total, m_ref[...] * SCORE_SCALE + jnp.log2(total), *unpack(mine_ref)
    )
    other = merge(*unpack(core_ref), *unpack(diagonal_ref))
    attended = jnp.concatenate([here, other], axis=0).T
    width = out_refs[0].shape[1]
    for n, out_ref in enumerate(out_refs):
        out_ref[...] = jnp.dot(
            attended,
            w_ref[:, n * width : (n + 1) * width],
            preferred_element_type=jnp.float32,
        ).astype(jnp.bfloat16)


def output(state, mine, core, diagonal, w_out):
    shape = jax.ShapeDtypeStruct((HALF, FEATURES // len(STEPS)), jnp.bfloat16)
    return pl.pallas_call(
        output_kernel,
        out_shape=(shape,) * len(STEPS),
        in_specs=whole(7),
        out_specs=tuple(whole(len(STEPS))),
        compiler_params=params(),
        name="output_project",
    )(*state, mine, core, diagonal, w_out)


def add_kernel(*refs):
    total = refs[0][...].astype(jnp.float32)
    for ref in refs[1:-1]:
        total = total + ref[...].astype(jnp.float32)
    refs[-1][...] = total.astype(jnp.bfloat16)


def add(*terms):
    return pl.pallas_call(
        add_kernel,
        out_shape=jax.ShapeDtypeStruct(terms[0].shape, jnp.bfloat16),
        in_specs=whole(len(terms)),
        out_specs=whole(1)[0],
        compiler_params=params(),
        name="add",
    )(*terms)


def finish_kernel(tokens_ref, vectors_ref, *refs):
    out_ref = refs[-1]
    total = refs[0][...].astype(jnp.float32)
    for part_ref in refs[1:-1]:
        total = total + part_ref[...].astype(jnp.float32)
    scale = vectors_ref[2 * len(STEPS) : 2 * len(STEPS) + 1, :]
    out_ref[...] = (tokens_ref[...].astype(jnp.float32) + scale * total).astype(jnp.bfloat16)


def finish(parts, tokens, vectors):
    return pl.pallas_call(
        finish_kernel,
        out_shape=jax.ShapeDtypeStruct(tokens.shape, jnp.bfloat16),
        in_specs=whole(2 + len(parts)),
        out_specs=whole(1)[0],
        compiler_params=params(),
        name="finish",
    )(tokens, vectors, *parts)


def per_device(tokens, norm_gain, norm_bias, w_query, w_key, w_value, w_out, layer_scale):
    groups = lax.axis_size("heads")
    width = FEATURES // groups
    core = lax.axis_index("frames") % CORE
    x, y = lax.axis_index("heads") // Y_LO, lax.axis_index("heads") % Y_LO
    sources = [((x - dx) % X) * Y_LO + (y ^ dy) for dx, dy in STEPS]
    targets = [((x + dx) % X) * Y_LO + (y ^ dy) for dx, dy in STEPS]
    place = jnp.stack([core, *sources, *targets]).astype(jnp.int32)

    across = send_heads(tokens, (2, 0))
    beside = send_heads(tokens, (0, 1))
    blocks = [tokens, beside, send_heads(tokens, (1, 0)), send_heads(tokens, (3, 0)), across]
    blocks += [send_heads(beside, (1, 0)), send_heads(beside, (3, 0)), send_heads(across, (0, 1))]
    w_all, w_last, vectors = prepare(
        place,
        w_query,
        w_key,
        w_value,
        w_out,
        norm_gain.reshape(groups, width),
        norm_bias.reshape(groups, width),
        layer_scale.reshape(1, width),
    )
    keep, give = project(blocks, vectors, w_all)
    queries, own = join(keep, send(give, 0, 0, 1))
    right, left = own, own
    mine, theirs = None, None
    for step in range(4):
        near = (right, left)
        right = send(right, 0, 1, 0)
        if step < 3:
            left = send(left, 0, -1, 0)
        if step == 0:
            partner = send(queries, 1, 0, 0)
            mine = attend([own], [queries], None, ((0, (0,)),))
        elif step == 1:
            late = near[1]
            theirs = attend([own, *near], [partner], None, ((0, (0, 1, 2)),))
            mine = attend(near[:1], [queries], mine, ((0, (0,)),))
        else:
            both = attend(
                near, [queries, partner], mine + theirs, ((0, (0, 1)), (1, (0, 1)))
            )
            mine, theirs = both[:3], both[3:]
    for_mine, for_other = attend([right], [partner], theirs, ((0, (0,)),), pack=(0, 1))
    from_partner = send(for_mine, 1, 0, 0)
    from_diagonal = send(for_other, 1, 0, 1)
    for_core, *state = attend([late, right], [queries], mine, ((0, (0, 1)),), pack=(1,))
    from_core = send(for_core, 0, 0, 1)
    terms = dict(zip(STEPS, output(state, from_partner, from_core, from_diagonal, w_last)))
    by_partner = send_heads(terms[2, 1], (0, 1))
    by_column = [send_heads(terms[1, 1], (1, 0)), send_heads(terms[3, 1], (3, 0))]
    parts = [send_heads(add(terms[2, 0], by_partner), (2, 0))]
    parts += [send_heads(add(terms[0, 1], *by_column), (0, 1))]
    parts += [send_heads(terms[1, 0], (1, 0)), send_heads(terms[3, 0], (3, 0)), terms[0, 0]]
    return finish(parts, tokens, vectors)


def solution(mesh):
    in_specs = (
        P("frames", "heads"),
        P(),
        P(),
        P(None, "heads"),
        P(None, "heads"),
        P(None, "heads"),
        P("heads", None),
        P("heads"),
    )
    out_specs = P("frames", "heads")
    return jax.shard_map(
        per_device, mesh=mesh, in_specs=in_specs, out_specs=out_specs, check_vma=False
    )
```

profile of v0, /device:TPU:8, one launch (start us, length us, event | category | flops | bytes accessed | tf_op | source)
XLA Modules:
  0.0 84.1 jit_solution(703992717370138538)
XLA Ops:
  0.0 2.2 %collective-permute-start = (bf16[512,128]{1,0:T(8,128)(2,1)}, bf16[512,128]{1,0:T(8,128)(2,1)S(1)}, u32[]{:S(2)}, u32[]{:S(2)}) collective-permute-start(bf16[512,128]{1,0:T(8,128)(2,1)} %tokens_ref.1), channel_id=1, source_target_pairs={{0,1},{1,0},{2,3},{3,2},{4,5},{5,4},{6,7},{7,6},{8,9},{9,8},{10,11... | collective-permute-start | bytes 393224 | tf_op jit(solution)/shard_map/ppermute | solution.py:48
  2.2 1.3 %collective-permute-start.3 = (bf16[512,128]{1,0:T(8,128)(2,1)}, bf16[512,128]{1,0:T(8,128)(2,1)S(1)}, u32[]{:S(2)}, u32[]{:S(2)}) collective-permute-start(bf16[512,128]{1,0:T(8,128)(2,1)} %tokens_ref.1), channel_id=1, source_target_pairs={{0,4},{1,5},{2,6},{3,7},{4,0},{5,1},{6,2},{7,3},{8,12},{9,13},{10,... | collective-permute-start | bytes 393224 | tf_op jit(solution)/shard_map/ppermute | solution.py:48
  4.1 2.6 %collective-permute-start.2 = (bf16[512,128]{1,0:T(8,128)(2,1)}, bf16[512,128]{1,0:T(8,128)(2,1)S(1)}, u32[]{:S(2)}, u32[]{:S(2)}) collective-permute-start(bf16[512,128]{1,0:T(8,128)(2,1)} %tokens_ref.1), channel_id=1, source_target_pairs={{0,6},{1,7},{2,0},{3,1},{4,2},{5,3},{6,4},{7,5},{8,14},{9,15},{10,... | collective-permute-start | bytes 393224 | tf_op jit(solution)/shard_map/ppermute | solution.py:48
  6.9 3.0 %collective-permute-start.5 = (bf16[512,128]{1,0:T(8,128)(2,1)S(1)}, bf16[512,128]{1,0:T(8,128)(2,1)S(1)}, u32[]{:S(2)}, u32[]{:S(2)}) collective-permute-start(bf16[512,128]{1,0:T(8,128)(2,1)S(1)} %collective-permute-done.refs_1_), channel_id=1, source_target_pairs={{0,6},{1,7},{2,0},{3,1},{4,2},{5,3},{6,4},{7,5},{8,14},{9,15},{10,... | collective-permute-start | bytes 393224 | tf_op jit(solution)/shard_map/ppermute | solution.py:48
  10.0 1.6 %collective-permute-start.6 = (bf16[512,128]{1,0:T(8,128)(2,1)S(1)}, bf16[512,128]{1,0:T(8,128)(2,1)S(1)}, u32[]{:S(2)}, u32[]{:S(2)}) collective-permute-start(bf16[512,128]{1,0:T(8,128)(2,1)S(1)} %collective-permute-done.3.refs_4_), channel_id=1, source_target_pairs={{0,1},{1,0},{2,3},{3,2},{4,5},{5,4},{6,7},{7,6},{8,9},{9,8},{10,11... | collective-permute-start | bytes 393224 | tf_op jit(solution)/shard_map/ppermute | solution.py:48
  12.3 0.9 %copy-done.2 = bf16[1024,128]{1,0:T(8,128)(2,1)S(1)} copy-done((bf16[1024,128]{1,0:T(8,128)(2,1)S(1)}, bf16[1024,128]{1,0:T(8,128)(2,1)}, u32[]{:S(2)}) %copy-start.2) | copy-done | bytes 262168
  15.2 1.1 %prepare.1 = (bf16[384,1024]{1,0:T(8,128)(2,1)S(1)}, bf16[128,1024]{1,0:T(8,128)(2,1)S(1)}, f32[24,128]{1,0:T(8,128)S(1)}) custom-call(s32[17]{0:T(128)S(1)} %stack.65.place_ref, bf16[1024,128]{1,0:T(8,128)(2,1)S(1)} %copy-done.1, bf16[1024,128]{1,0:T(8,128)(2,1)S(1)} %copy-done.2, bf16[1024,128]{1,0:T(8,128)(2,1)S(1)} %copy-done.3, ...), custom_call_target="tpu_custom_call" | custom-call | flops 402653184 | bytes 4194304 | tf_op jit(solution)/shard_map/prepare/pallas_call | solution.py:102
  16.4 1.7 %norm_project.1 = (bf16[192,512]{1,0:T(8,128)(2,1)S(1)}, bf16[192,512]{1,0:T(8,128)(2,1)S(1)}) custom-call(bf16[512,128]{1,0:T(8,128)(2,1)S(1)} %copy-done, bf16[512,128]{1,0:T(8,128)(2,1)S(1)} %collective-permute-done.refs_1_, bf16[512,128]{1,0:T(8,128)(2,1)S(1)} %collective-permute-done.1.refs_2_, bf16[512,128]{1,0:T(8,128)(2,1)S(1)} %collective-permute-done.2.refs_3_, ...), custom_call_target="tpu_custom_call" | custom-call | flops 402653184 | bytes 2097152 | tf_op jit(solution)/shard_map/norm_project/pallas_call | solution.py:156
  18.2 1.4 %collective-permute-done.7.taken = bf16[192,512]{1,0:T(8,128)(2,1)S(1)} collective-permute-done((bf16[192,512]{1,0:T(8,128)(2,1)S(1)}, bf16[192,512]{1,0:T(8,128)(2,1)S(1)}, u32[]{:S(2)}, u32[]{:S(2)}) %collective-permute-start.7) | collective-permute-done | bytes 196640 | tf_op jit(solution)/shard_map/ppermute | solution.py:34
  19.6 2.0 %collective-permute-start.9 = (bf16[128,1024]{1,0:T(8,128)(2,1)S(1)}, bf16[128,1024]{1,0:T(8,128)(2,1)S(1)}, u32[]{:S(2)}, u32[]{:S(2)}) collective-permute-start(bf16[128,1024]{1,0:T(8,128)(2,1)S(1)} %get-tuple-element.51.refs_0_), channel_id=1, source_target_pairs={{0,16},{8,24},{16,32},{24,40},{32,48},{40,56},{48,64},{56,72},{64,... | collective-permute-start | bytes 786440 | tf_op jit(solution)/shard_map/ppermute | solution.py:34
  21.6 4.0 %collective-permute-start.8 = (bf16[128,1024]{1,0:T(8,128)(2,1)S(1)}, bf16[128,1024]{1,0:T(8,128)(2,1)S(1)}, u32[]{:S(2)}, u32[]{:S(2)}) collective-permute-start(bf16[128,1024]{1,0:T(8,128)(2,1)S(1)} %get-tuple-element.51.refs_0_), channel_id=1, source_target_pairs={{0,112},{8,120},{16,0},{24,8},{32,16},{40,24},{48,32},{56,40},{64,... | collective-permute-start | bytes 786440 | tf_op jit(solution)/shard_map/ppermute | solution.py:34
  25.7 2.3 %collective-permute-start.15 = (bf16[64,1024]{1,0:T(8,128)(2,1)S(1)}, bf16[64,1024]{1,0:T(8,128)(2,1)S(1)}, u32[]{:S(2)}, u32[]{:S(2)}) collective-permute-start(bf16[64,1024]{1,0:T(8,128)(2,1)S(1)} %get-tuple-element.52.refs_1_.refs_2_), channel_id=1, source_target_pairs={{0,128},{8,136},{16,144},{24,152},{32,160},{40,168},{48,176},{56,1... | collective-permute-start | bytes 393224 | tf_op jit(solution)/shard_map/ppermute | solution.py:34
  28.0 1.8 %attend.7 = (f32[1,1024]{1,0:T(1,128)S(1)}, f32[1,1024]{1,0:T(1,128)S(1)}, f32[64,1024]{1,0:T(8,128)S(1)}) custom-call(bf16[128,1024]{1,0:T(8,128)(2,1)S(1)} %get-tuple-element.51.refs_0_, bf16[64,1024]{1,0:T(8,128)(2,1)S(1)} %get-tuple-element.52.refs_1_.refs_2_), custom_call_target="tpu_custom_call" | custom-call | flops 1073741824 | bytes 1048576 | tf_op jit(solution)/shard_map/attend/pallas_call | solution.py:294
  29.7 2.4 %collective-permute-done.9.refs_0_.refs_1_ = bf16[128,1024]{1,0:T(8,128)(2,1)S(1)} collective-permute-done((bf16[128,1024]{1,0:T(8,128)(2,1)S(1)}, bf16[128,1024]{1,0:T(8,128)(2,1)S(1)}, u32[]{:S(2)}, u32[]{:S(2)}) %collective-permute-start.9) | collective-permute-done | bytes 262176 | tf_op jit(solution)/shard_map/ppermute | solution.py:34
  32.2 3.2 %collective-permute-start.13 = (bf16[128,1024]{1,0:T(8,128)(2,1)S(1)}, bf16[128,1024]{1,0:T(8,128)(2,1)S(1)}, u32[]{:S(2)}, u32[]{:S(2)}) collective-permute-start(bf16[128,1024]{1,0:T(8,128)(2,1)S(1)} %collective-permute-done.8.refs_2_.refs_0_), channel_id=1, source_target_pairs={{0,112},{8,120},{16,0},{24,8},{32,16},{40,24},{48,32},{56,40},{64,... | collective-permute-start | bytes 786440 | tf_op jit(solution)/shard_map/ppermute | solution.py:34
  35.4 1.8 %attend.8 = (f32[1,1024]{1,0:T(1,128)S(1)}, f32[1,1024]{1,0:T(1,128)S(1)}, f32[64,1024]{1,0:T(8,128)S(1)}) custom-call(bf16[128,1024]{1,0:T(8,128)(2,1)S(1)} %collective-permute-done.9.refs_0_.refs_1_, bf16[64,1024]{1,0:T(8,128)(2,1)S(1)} %get-tuple-element.52.refs_1_.refs_2_, f32[1,1024]{1,0:T(1,128)S(1)} %get-tuple-element.53.refs_2_, ...), custom_call_target="tpu_custom_call" | custom-call | flops 1073741824 | bytes 1048576 | tf_op jit(solution)/shard_map/attend/pallas_call | solution.py:294
  37.2 4.1 %attend.9 = (f32[1,1024]{1,0:T(1,128)S(1)}, f32[1,1024]{1,0:T(1,128)S(1)}, f32[64,1024]{1,0:T(8,128)S(1)}) custom-call(bf16[128,1024]{1,0:T(8,128)(2,1)S(1)} %get-tuple-element.51.refs_0_, bf16[128,1024]{1,0:T(8,128)(2,1)S(1)} %collective-permute-done.9.refs_0_.refs_1_, bf16[128,1024]{1,0:T(8,128)(2,1)S(1)} %collective-permute-done.8.refs_2_.refs_0_, ...), custom_call_target="tpu_custom_call" | custom-call | flops 3221225472 | bytes 1048576 | tf_op jit(solution)/shard_map/attend/pallas_call | solution.py:294
  41.4 3.2 %collective-permute-start.14 = (bf16[128,1024]{1,0:T(8,128)(2,1)S(1)}, bf16[128,1024]{1,0:T(8,128)(2,1)S(1)}, u32[]{:S(2)}, u32[]{:S(2)}) collective-permute-start(bf16[128,1024]{1,0:T(8,128)(2,1)S(1)} %collective-permute-done.13.refs_1_), channel_id=1, source_target_pairs={{0,112},{8,120},{16,0},{24,8},{32,16},{40,24},{48,32},{56,40},{64,... | collective-permute-start | bytes 786440 | tf_op jit(solution)/shard_map/ppermute | solution.py:34
  44.7 5.0 %attend.10 = (f32[1,1024]{1,0:T(1,128)S(1)}, f32[1,1024]{1,0:T(1,128)S(1)}, f32[64,1024]{1,0:T(8,128)S(1)}, f32[1,1024]{1,0:T(1,128)S(1)}, f32[1,1024]{1,0:T(1,128)S(1)}, /*index=5*/f32[64,1024]{1,0:T(8,128)S(1)}) custom-call(bf16[128,1024]{1,0:T(8,128)(2,1)S(1)} %collective-permute-done.10.refs_0_, bf16[128,1024]{1,0:T(8,128)(2,1)S(1)} %collective-permute-done.13.refs_1_, ...), custom_call_target="tpu_custom_call" | custom-call | flops 4294967296 | bytes 1048576 | tf_op jit(solution)/shard_map/attend/pallas_call | solution.py:294
  50.0 5.0 %attend.11 = (f32[1,1024]{1,0:T(1,128)S(1)}, f32[1,1024]{1,0:T(1,128)S(1)}, f32[64,1024]{1,0:T(8,128)S(1)}, f32[1,1024]{1,0:T(1,128)S(1)}, f32[1,1024]{1,0:T(1,128)S(1)}, /*index=5*/f32[64,1024]{1,0:T(8,128)S(1)}) custom-call(bf16[128,1024]{1,0:T(8,128)(2,1)S(1)} %collective-permute-done.11.refs_0_, bf16[128,1024]{1,0:T(8,128)(2,1)S(1)} %collective-permute-done.14.refs_1_, ...), custom_call_target="tpu_custom_call" | custom-call | flops 4294967296 | bytes 1048576 | tf_op jit(solution)/shard_map/attend/pallas_call | solution.py:294
  55.0 2.9 %collective-permute-done.12.refs_1_.refs_0_ = bf16[128,1024]{1,0:T(8,128)(2,1)S(1)} collective-permute-done((bf16[128,1024]{1,0:T(8,128)(2,1)S(1)}, bf16[128,1024]{1,0:T(8,128)(2,1)S(1)}, u32[]{:S(2)}, u32[]{:S(2)}) %collective-permute-start.12) | collective-permute-done | bytes 262176 | tf_op jit(solution)/shard_map/ppermute | solution.py:34
  57.9 1.8 %attend.13 = (bf16[80,512]{1,0:T(8,128)(2,1)S(1)}, bf16[80,512]{1,0:T(8,128)(2,1)S(1)}) custom-call(bf16[128,1024]{1,0:T(8,128)(2,1)S(1)} %collective-permute-done.12.refs_1_.refs_0_, bf16[64,1024]{1,0:T(8,128)(2,1)S(1)} %collective-permute-done.15.refs_3_.refs_1_, f32[1,1024]{1,0:T(1,128)S(1)} %get-tuple-element.74.refs_2_, ...), custom_call_target="tpu_custom_call" | custom-call | flops 1073741824 | bytes 1048576 | tf_op jit(solution)/shard_map/attend/pallas_call | solution.py:294
  59.7 2.4 %collective-permute-start.16 = (bf16[80,512]{1,0:T(8,128)(2,1)S(1)}, bf16[80,512]{1,0:T(8,128)(2,1)S(1)}, u32[]{:S(2)}, u32[]{:S(2)}) collective-permute-start(bf16[80,512]{1,0:T(8,128)(2,1)S(1)} %get-tuple-element.77), channel_id=1, source_target_pairs={{0,128},{8,136},{16,144},{24,152},{32,160},{40,168},{48,176},{56,1... | collective-permute-start | bytes 245768 | tf_op jit(solution)/shard_map/ppermute | solution.py:34
  62.1 3.1 %attend.12 = (bf16[80,512]{1,0:T(8,128)(2,1)S(1)}, f32[1,512]{1,0:T(1,128)S(1)}, f32[1,512]{1,0:T(1,128)S(1)}, f32[64,512]{1,0:T(8,128)S(1)}) custom-call(bf16[128,1024]{1,0:T(8,128)(2,1)S(1)} %collective-permute-done.8.refs_2_.refs_0_, bf16[128,1024]{1,0:T(8,128)(2,1)S(1)} %collective-permute-done.12.refs_1_.refs_0_, ...), custom_call_target="tpu_custom_call" | custom-call | flops 2147483648 | bytes 1048576 | tf_op jit(solution)/shard_map/attend/pallas_call | solution.py:294
  65.1 1.4 %collective-permute-start.17 = (bf16[80,512]{1,0:T(8,128)(2,1)S(1)}, bf16[80,512]{1,0:T(8,128)(2,1)S(1)}, u32[]{:S(2)}, u32[]{:S(2)}) collective-permute-start(bf16[80,512]{1,0:T(8,128)(2,1)S(1)} %get-tuple-element.78), channel_id=1, source_target_pairs={{0,8},{8,0},{16,24},{24,16},{32,40},{40,32},{48,56},{56,48},{64,72... | collective-permute-start | bytes 245768 | tf_op jit(solution)/shard_map/ppermute | solution.py:34
  68.1 3.2 %collective-permute-start.22 = (bf16[512,128]{1,0:T(8,128)(2,1)S(1)}, bf16[512,128]{1,0:T(8,128)(2,1)S(1)}, u32[]{:S(2)}, u32[]{:S(2)}) collective-permute-start(bf16[512,128]{1,0:T(8,128)(2,1)S(1)} %get-tuple-element.85), channel_id=1, source_target_pairs={{0,6},{1,7},{2,0},{3,1},{4,2},{5,3},{6,4},{7,5},{8,14},{9,15},{10,... | collective-permute-start | bytes 393224 | tf_op jit(solution)/shard_map/ppermute | solution.py:48
  71.3 1.3 %collective-permute-start.19 = (bf16[512,128]{1,0:T(8,128)(2,1)S(1)}, bf16[512,128]{1,0:T(8,128)(2,1)S(1)}, u32[]{:S(2)}, u32[]{:S(2)}) collective-permute-start(bf16[512,128]{1,0:T(8,128)(2,1)S(1)} %get-tuple-element.82), channel_id=1, source_target_pairs={{0,1},{1,0},{2,3},{3,2},{4,5},{5,4},{6,7},{7,6},{8,9},{9,8},{10,11... | collective-permute-start | bytes 393224 | tf_op jit(solution)/shard_map/ppermute | solution.py:48
  72.6 3.2 %collective-permute-start.25 = (bf16[512,128]{1,0:T(8,128)(2,1)S(1)}, bf16[512,128]{1,0:T(8,128)(2,1)S(1)}, u32[]{:S(2)}, u32[]{:S(2)}) collective-permute-start(bf16[512,128]{1,0:T(8,128)(2,1)S(1)} %get-tuple-element.87), channel_id=1, source_target_pairs={{0,6},{1,7},{2,0},{3,1},{4,2},{5,3},{6,4},{7,5},{8,14},{9,15},{10,... | collective-permute-start | bytes 393224 | tf_op jit(solution)/shard_map/ppermute | solution.py:48
  77.4 1.4 %collective-permute-done.24.refs_2_ = bf16[512,128]{1,0:T(8,128)(2,1)S(1)} collective-permute-done((bf16[512,128]{1,0:T(8,128)(2,1)S(1)}, bf16[512,128]{1,0:T(8,128)(2,1)S(1)}, u32[]{:S(2)}, u32[]{:S(2)}) %collective-permute-start.24) | collective-permute-done | bytes 131104 | tf_op jit(solution)/shard_map/ppermute | solution.py:48
  78.8 1.0 %collective-permute-done.25.refs_3_ = bf16[512,128]{1,0:T(8,128)(2,1)S(1)} collective-permute-done((bf16[512,128]{1,0:T(8,128)(2,1)S(1)}, bf16[512,128]{1,0:T(8,128)(2,1)S(1)}, u32[]{:S(2)}, u32[]{:S(2)}) %collective-permute-start.25) | collective-permute-done | bytes 131104 | tf_op jit(solution)/shard_map/ppermute | solution.py:48
  79.8 1.2 %collective-permute-done.23.refs_1_ = bf16[512,128]{1,0:T(8,128)(2,1)S(1)} collective-permute-done((bf16[512,128]{1,0:T(8,128)(2,1)S(1)}, bf16[512,128]{1,0:T(8,128)(2,1)S(1)}, u32[]{:S(2)}, u32[]{:S(2)}) %collective-permute-start.23) | collective-permute-done | bytes 131104 | tf_op jit(solution)/shard_map/ppermute | solution.py:48
  81.0 2.4 %collective-permute-done.20.refs_0_ = bf16[512,128]{1,0:T(8,128)(2,1)S(1)} collective-permute-done((bf16[512,128]{1,0:T(8,128)(2,1)S(1)}, bf16[512,128]{1,0:T(8,128)(2,1)S(1)}, u32[]{:S(2)}, u32[]{:S(2)}) %collective-permute-start.20) | collective-permute-done | bytes 131104 | tf_op jit(solution)/shard_map/ppermute | solution.py:48
  (51 shorter events, 7.8 us)
Async XLA Ops:
  0.0 11.7 %copy-start.1 = (bf16[1024,128]{1,0:T(8,128)(2,1)S(1)}, bf16[1024,128]{1,0:T(8,128)(2,1)}, u32[]{:S(2)}) copy-start(bf16[1024,128]{1,0:T(8,128)(2,1)} %wq_hbm.1) | copy-start | bytes 786436
  0.0 6.7 %collective-permute-start = (bf16[512,128]{1,0:T(8,128)(2,1)}, bf16[512,128]{1,0:T(8,128)(2,1)S(1)}, u32[]{:S(2)}, u32[]{:S(2)}) collective-permute-start(bf16[512,128]{1,0:T(8,128)(2,1)} %tokens_ref.1), channel_id=1, source_target_pairs={{0,1},{1,0},{2,3},{3,2},{4,5},{5,4},{6,7},{7,6},{8,9},{9,8},{10,11... | collective-permute-start | bytes 393224 | tf_op jit(solution)/shard_map/ppermute | solution.py:48
  2.2 7.8 %collective-permute-start.3 = (bf16[512,128]{1,0:T(8,128)(2,1)}, bf16[512,128]{1,0:T(8,128)(2,1)S(1)}, u32[]{:S(2)}, u32[]{:S(2)}) collective-permute-start(bf16[512,128]{1,0:T(8,128)(2,1)} %tokens_ref.1), channel_id=1, source_target_pairs={{0,4},{1,5},{2,6},{3,7},{4,0},{5,1},{6,2},{7,3},{8,12},{9,13},{10,... | collective-permute-start | bytes 393224 | tf_op jit(solution)/shard_map/ppermute | solution.py:48
  3.5 12.8 %collective-permute-start.1 = (bf16[512,128]{1,0:T(8,128)(2,1)}, bf16[512,128]{1,0:T(8,128)(2,1)S(1)}, u32[]{:S(2)}, u32[]{:S(2)}) collective-permute-start(bf16[512,128]{1,0:T(8,128)(2,1)} %tokens_ref.1), channel_id=1, source_target_pairs={{0,2},{1,3},{2,4},{3,5},{4,6},{5,7},{6,0},{7,1},{8,10},{9,11},{10,... | collective-permute-start | bytes 393224 | tf_op jit(solution)/shard_map/ppermute | solution.py:48
  4.1 12.3 %collective-permute-start.2 = (bf16[512,128]{1,0:T(8,128)(2,1)}, bf16[512,128]{1,0:T(8,128)(2,1)S(1)}, u32[]{:S(2)}, u32[]{:S(2)}) collective-permute-start(bf16[512,128]{1,0:T(8,128)(2,1)} %tokens_ref.1), channel_id=1, source_target_pairs={{0,6},{1,7},{2,0},{3,1},{4,2},{5,3},{6,4},{7,5},{8,14},{9,15},{10,... | collective-permute-start | bytes 393224 | tf_op jit(solution)/shard_map/ppermute | solution.py:48
  6.7 9.6 %collective-permute-start.4 = (bf16[512,128]{1,0:T(8,128)(2,1)S(1)}, bf16[512,128]{1,0:T(8,128)(2,1)S(1)}, u32[]{:S(2)}, u32[]{:S(2)}) collective-permute-start(bf16[512,128]{1,0:T(8,128)(2,1)S(1)} %collective-permute-done.refs_1_), channel_id=1, source_target_pairs={{0,2},{1,3},{2,4},{3,5},{4,6},{5,7},{6,0},{7,1},{8,10},{9,11},{10,... | collective-permute-start | bytes 393224 | tf_op jit(solution)/shard_map/ppermute | solution.py:48
  6.9 9.4 %collective-permute-start.5 = (bf16[512,128]{1,0:T(8,128)(2,1)S(1)}, bf16[512,128]{1,0:T(8,128)(2,1)S(1)}, u32[]{:S(2)}, u32[]{:S(2)}) collective-permute-start(bf16[512,128]{1,0:T(8,128)(2,1)S(1)} %collective-permute-done.refs_1_), channel_id=1, source_target_pairs={{0,6},{1,7},{2,0},{3,1},{4,2},{5,3},{6,4},{7,5},{8,14},{9,15},{10,... | collective-permute-start | bytes 393224 | tf_op jit(solution)/shard_map/ppermute | solution.py:48
  10.0 6.4 %collective-permute-start.6 = (bf16[512,128]{1,0:T(8,128)(2,1)S(1)}, bf16[512,128]{1,0:T(8,128)(2,1)S(1)}, u32[]{:S(2)}, u32[]{:S(2)}) collective-permute-start(bf16[512,128]{1,0:T(8,128)(2,1)S(1)} %collective-permute-done.3.refs_4_), channel_id=1, source_target_pairs={{0,1},{1,0},{2,3},{3,2},{4,5},{5,4},{6,7},{7,6},{8,9},{9,8},{10,11... | collective-permute-start | bytes 393224 | tf_op jit(solution)/shard_map/ppermute | solution.py:48
  11.6 0.7 copy-start.5
  12.3 1.0 %copy-start.2 = (bf16[1024,128]{1,0:T(8,128)(2,1)S(1)}, bf16[1024,128]{1,0:T(8,128)(2,1)}, u32[]{:S(2)}) copy-start(bf16[1024,128]{1,0:T(8,128)(2,1)} %wk_hbm.1) | copy-start | bytes 786436
  13.3 0.9 %copy-start.3 = (bf16[1024,128]{1,0:T(8,128)(2,1)S(1)}, bf16[1024,128]{1,0:T(8,128)(2,1)}, u32[]{:S(2)}) copy-start(bf16[1024,128]{1,0:T(8,128)(2,1)} %wv_hbm.1) | copy-start | bytes 786436
  14.2 0.9 %copy-start.4 = (bf16[128,1024]{1,0:T(8,128)(2,1)S(1)}, bf16[128,1024]{1,0:T(8,128)(2,1)}, u32[]{:S(2)}) copy-start(bf16[128,1024]{1,0:T(8,128)(2,1)} %w_out_hbm.1) | copy-start | bytes 786436
  15.2 1.2 %copy-start = (bf16[512,128]{1,0:T(8,128)(2,1)S(1)}, bf16[512,128]{1,0:T(8,128)(2,1)}, u32[]{:S(2)}) copy-start(bf16[512,128]{1,0:T(8,128)(2,1)} %tokens_ref.1) | copy-start | bytes 393220
  18.1 1.5 %collective-permute-start.7 = (bf16[192,512]{1,0:T(8,128)(2,1)S(1)}, bf16[192,512]{1,0:T(8,128)(2,1)S(1)}, u32[]{:S(2)}, u32[]{:S(2)}) collective-permute-start(bf16[192,512]{1,0:T(8,128)(2,1)S(1)} %get-tuple-element.50), channel_id=1, source_target_pairs={{0,8},{8,0},{16,24},{24,16},{32,40},{40,32},{48,56},{56,48},{64,72... | collective-permute-start | bytes 589832 | tf_op jit(solution)/shard_map/ppermute | solution.py:34
  19.6 12.5 %collective-permute-start.9 = (bf16[128,1024]{1,0:T(8,128)(2,1)S(1)}, bf16[128,1024]{1,0:T(8,128)(2,1)S(1)}, u32[]{:S(2)}, u32[]{:S(2)}) collective-permute-start(bf16[128,1024]{1,0:T(8,128)(2,1)S(1)} %get-tuple-element.51.refs_0_), channel_id=1, source_target_pairs={{0,16},{8,24},{16,32},{24,40},{32,48},{40,56},{48,64},{56,72},{64,... | collective-permute-start | bytes 786440 | tf_op jit(solution)/shard_map/ppermute | solution.py:34
  21.6 10.6 %collective-permute-start.8 = (bf16[128,1024]{1,0:T(8,128)(2,1)S(1)}, bf16[128,1024]{1,0:T(8,128)(2,1)S(1)}, u32[]{:S(2)}, u32[]{:S(2)}) collective-permute-start(bf16[128,1024]{1,0:T(8,128)(2,1)S(1)} %get-tuple-element.51.refs_0_), channel_id=1, source_target_pairs={{0,112},{8,120},{16,0},{24,8},{32,16},{40,24},{48,32},{56,40},{64,... | collective-permute-start | bytes 786440 | tf_op jit(solution)/shard_map/ppermute | solution.py:34
  25.7 11.5 %collective-permute-start.15 = (bf16[64,1024]{1,0:T(8,128)(2,1)S(1)}, bf16[64,1024]{1,0:T(8,128)(2,1)S(1)}, u32[]{:S(2)}, u32[]{:S(2)}) collective-permute-start(bf16[64,1024]{1,0:T(8,128)(2,1)S(1)} %get-tuple-element.52.refs_1_.refs_2_), channel_id=1, source_target_pairs={{0,128},{8,136},{16,144},{24,152},{32,160},{40,168},{48,176},{56,1... | collective-permute-start | bytes 393224 | tf_op jit(solution)/shard_map/ppermute | solution.py:34
  32.2 9.2 %collective-permute-start.10 = (bf16[128,1024]{1,0:T(8,128)(2,1)S(1)}, bf16[128,1024]{1,0:T(8,128)(2,1)S(1)}, u32[]{:S(2)}, u32[]{:S(2)}) collective-permute-start(bf16[128,1024]{1,0:T(8,128)(2,1)S(1)} %collective-permute-done.9.refs_0_.refs_1_), channel_id=1, source_target_pairs={{0,16},{8,24},{16,32},{24,40},{32,48},{40,56},{48,64},{56,72},{64,... | collective-permute-start | bytes 786440 | tf_op jit(solution)/shard_map/ppermute | solution.py:34
  32.2 9.2 %collective-permute-start.13 = (bf16[128,1024]{1,0:T(8,128)(2,1)S(1)}, bf16[128,1024]{1,0:T(8,128)(2,1)S(1)}, u32[]{:S(2)}, u32[]{:S(2)}) collective-permute-start(bf16[128,1024]{1,0:T(8,128)(2,1)S(1)} %collective-permute-done.8.refs_2_.refs_0_), channel_id=1, source_target_pairs={{0,112},{8,120},{16,0},{24,8},{32,16},{40,24},{48,32},{56,40},{64,... | collective-permute-start | bytes 786440 | tf_op jit(solution)/shard_map/ppermute | solution.py:34
  41.3 8.6 %collective-permute-start.11 = (bf16[128,1024]{1,0:T(8,128)(2,1)S(1)}, bf16[128,1024]{1,0:T(8,128)(2,1)S(1)}, u32[]{:S(2)}, u32[]{:S(2)}) collective-permute-start(bf16[128,1024]{1,0:T(8,128)(2,1)S(1)} %collective-permute-done.10.refs_0_), channel_id=1, source_target_pairs={{0,16},{8,24},{16,32},{24,40},{32,48},{40,56},{48,64},{56,72},{64,... | collective-permute-start | bytes 786440 | tf_op jit(solution)/shard_map/ppermute | solution.py:34
  41.4 8.5 %collective-permute-start.14 = (bf16[128,1024]{1,0:T(8,128)(2,1)S(1)}, bf16[128,1024]{1,0:T(8,128)(2,1)S(1)}, u32[]{:S(2)}, u32[]{:S(2)}) collective-permute-start(bf16[128,1024]{1,0:T(8,128)(2,1)S(1)} %collective-permute-done.13.refs_1_), channel_id=1, source_target_pairs={{0,112},{8,120},{16,0},{24,8},{32,16},{40,24},{48,32},{56,40},{64,... | collective-permute-start | bytes 786440 | tf_op jit(solution)/shard_map/ppermute | solution.py:34
  49.9 8.0 %collective-permute-start.12 = (bf16[128,1024]{1,0:T(8,128)(2,1)S(1)}, bf16[128,1024]{1,0:T(8,128)(2,1)S(1)}, u32[]{:S(2)}, u32[]{:S(2)}) collective-permute-start(bf16[128,1024]{1,0:T(8,128)(2,1)S(1)} %collective-permute-done.11.refs_0_), channel_id=1, source_target_pairs={{0,16},{8,24},{16,32},{24,40},{32,48},{40,56},{48,64},{56,72},{64,... | collective-permute-start | bytes 786440 | tf_op jit(solution)/shard_map/ppermute | solution.py:34
  59.7 6.9 %collective-permute-start.16 = (bf16[80,512]{1,0:T(8,128)(2,1)S(1)}, bf16[80,512]{1,0:T(8,128)(2,1)S(1)}, u32[]{:S(2)}, u32[]{:S(2)}) collective-permute-start(bf16[80,512]{1,0:T(8,128)(2,1)S(1)} %get-tuple-element.77), channel_id=1, source_target_pairs={{0,128},{8,136},{16,144},{24,152},{32,160},{40,168},{48,176},{56,1... | collective-permute-start | bytes 245768 | tf_op jit(solution)/shard_map/ppermute | solution.py:34
  62.1 5.4 %collective-permute-start.18 = (bf16[80,512]{1,0:T(8,128)(2,1)S(1)}, bf16[80,512]{1,0:T(8,128)(2,1)S(1)}, u32[]{:S(2)}, u32[]{:S(2)}) collective-permute-start(bf16[80,512]{1,0:T(8,128)(2,1)S(1)} %get-tuple-element.79), channel_id=1, source_target_pairs={{0,136},{8,128},{16,152},{24,144},{32,168},{40,160},{48,184},{56,1... | collective-permute-start | bytes 245768 | tf_op jit(solution)/shard_map/ppermute | solution.py:34
  65.1 2.4 %collective-permute-start.17 = (bf16[80,512]{1,0:T(8,128)(2,1)S(1)}, bf16[80,512]{1,0:T(8,128)(2,1)S(1)}, u32[]{:S(2)}, u32[]{:S(2)}) collective-permute-start(bf16[80,512]{1,0:T(8,128)(2,1)S(1)} %get-tuple-element.78), channel_id=1, source_target_pairs={{0,8},{8,0},{16,24},{24,16},{32,40},{40,32},{48,56},{56,48},{64,72... | collective-permute-start | bytes 245768 | tf_op jit(solution)/shard_map/ppermute | solution.py:34
  68.0 7.8 %collective-permute-start.21 = (bf16[512,128]{1,0:T(8,128)(2,1)S(1)}, bf16[512,128]{1,0:T(8,128)(2,1)S(1)}, u32[]{:S(2)}, u32[]{:S(2)}) collective-permute-start(bf16[512,128]{1,0:T(8,128)(2,1)S(1)} %get-tuple-element.84), channel_id=1, source_target_pairs={{0,2},{1,3},{2,4},{3,5},{4,6},{5,7},{6,0},{7,1},{8,10},{9,11},{10,... | collective-permute-start | bytes 393224 | tf_op jit(solution)/shard_map/ppermute | solution.py:48
  68.1 7.7 %collective-permute-start.22 = (bf16[512,128]{1,0:T(8,128)(2,1)S(1)}, bf16[512,128]{1,0:T(8,128)(2,1)S(1)}, u32[]{:S(2)}, u32[]{:S(2)}) collective-permute-start(bf16[512,128]{1,0:T(8,128)(2,1)S(1)} %get-tuple-element.85), channel_id=1, source_target_pairs={{0,6},{1,7},{2,0},{3,1},{4,2},{5,3},{6,4},{7,5},{8,14},{9,15},{10,... | collective-permute-start | bytes 393224 | tf_op jit(solution)/shard_map/ppermute | solution.py:48
  71.3 5.4 %collective-permute-start.19 = (bf16[512,128]{1,0:T(8,128)(2,1)S(1)}, bf16[512,128]{1,0:T(8,128)(2,1)S(1)}, u32[]{:S(2)}, u32[]{:S(2)}) collective-permute-start(bf16[512,128]{1,0:T(8,128)(2,1)S(1)} %get-tuple-element.82), channel_id=1, source_target_pairs={{0,1},{1,0},{2,3},{3,2},{4,5},{5,4},{6,7},{7,6},{8,9},{9,8},{10,11... | collective-permute-start | bytes 393224 | tf_op jit(solution)/shard_map/ppermute | solution.py:48
  72.6 6.2 %collective-permute-start.24 = (bf16[512,128]{1,0:T(8,128)(2,1)S(1)}, bf16[512,128]{1,0:T(8,128)(2,1)S(1)}, u32[]{:S(2)}, u32[]{:S(2)}) collective-permute-start(bf16[512,128]{1,0:T(8,128)(2,1)S(1)} %get-tuple-element.86), channel_id=1, source_target_pairs={{0,2},{1,3},{2,4},{3,5},{4,6},{5,7},{6,0},{7,1},{8,10},{9,11},{10,... | collective-permute-start | bytes 393224 | tf_op jit(solution)/shard_map/ppermute | solution.py:48
  72.6 7.2 %collective-permute-start.25 = (bf16[512,128]{1,0:T(8,128)(2,1)S(1)}, bf16[512,128]{1,0:T(8,128)(2,1)S(1)}, u32[]{:S(2)}, u32[]{:S(2)}) collective-permute-start(bf16[512,128]{1,0:T(8,128)(2,1)S(1)} %get-tuple-element.87), channel_id=1, source_target_pairs={{0,6},{1,7},{2,0},{3,1},{4,2},{5,3},{6,4},{7,5},{8,14},{9,15},{10,... | collective-permute-start | bytes 393224 | tf_op jit(solution)/shard_map/ppermute | solution.py:48
  75.9 5.1 %collective-permute-start.23 = (bf16[512,128]{1,0:T(8,128)(2,1)S(1)}, bf16[512,128]{1,0:T(8,128)(2,1)S(1)}, u32[]{:S(2)}, u32[]{:S(2)}) collective-permute-start(bf16[512,128]{1,0:T(8,128)(2,1)S(1)} %add.126), channel_id=1, source_target_pairs={{0,1},{1,0},{2,3},{3,2},{4,5},{5,4},{6,7},{7,6},{8,9},{9,8},{10,11... | collective-permute-start | bytes 393224 | tf_op jit(solution)/shard_map/ppermute | solution.py:48
  76.8 6.6 %collective-permute-start.20 = (bf16[512,128]{1,0:T(8,128)(2,1)S(1)}, bf16[512,128]{1,0:T(8,128)(2,1)S(1)}, u32[]{:S(2)}, u32[]{:S(2)}) collective-permute-start(bf16[512,128]{1,0:T(8,128)(2,1)S(1)} %add.125), channel_id=1, source_target_pairs={{0,4},{1,5},{2,6},{3,7},{4,0},{5,1},{6,2},{7,3},{8,12},{9,13},{10,... | collective-permute-start | bytes 393224 | tf_op jit(solution)/shard_map/ppermute | solution.py:48
  (2 other events, 1.4 us)
where the time goes:
time: 84.5 us; the launch traced here: 84.1 us
  starting transfers between devices  39.6 us (47%)
  Pallas kernels  26.7 us (32%)
  waiting for transfers between devices  14 us (17%)
  local copies, waits for them, and re-layouts  3.62 us (4%)
    pallas_call x7, Pallas kernels, attend(): pl.pallas_call(functools.partial(attend_kernel, blocks=len(kv), sets=sets...  22.5 us
    ppermute x14, starting transfers between devices, send_heads(): return lax.ppermute(array, 'heads', heads_shift(*step))  20.8 us
    ppermute x12, starting transfers between devices, send(): return lax.ppermute(array, 'frames', frames_shift(dy, dz, dc))  18.8 us
    ppermute x12, waiting for transfers between devices, send(): return lax.ppermute(array, 'frames', frames_shift(dy, dz, dc))  7.96 us
    ppermute x14, waiting for transfers between devices, send_heads(): return lax.ppermute(array, 'heads', heads_shift(*step))  6.02 us
    unnamed x16, local copies, waits for them, and re-layouts  3.53 us
    pallas_call x1, Pallas kernels, project(): pl.pallas_call(project_kernel, out_shape=(shape, shape), in_specs=whole(1...  1.69 us
  transfers between devices with their start and end apart: 26, of which 9 were waited for; matrix products, arithmetic and copies ran while one was open for 0% of the time, Pallas kernels for 26%

commit v1 on v0

--- a/solution.py
+++ b/solution.py
@@ -191,17 +191,13 @@
     kv = refs[:blocks]
     queries = refs[blocks : blocks + sets]
     at = blocks + sets
-    old = None
-    if not fresh:
-        old = refs[at : at + 3 * sets]
-        at += 3 * sets
-    new = None
-    packs = refs[at : at + len(pack)]
-    at += len(pack)
-    if len(pack) < BLOCK // TILE:
-        new = refs[at : at + 3 * sets]
-        at += 3 * sets
-    k_ref, s_ref = refs[at:]
+    old = {}
+    for which in range(sets):
+        if which not in fresh:
+            old[which] = refs[at : at + 3]
+            at += 3
+    k_ref, s_ref = refs[-2:]
+    packs, new = refs[at : at + len(pack)], refs[at + len(pack) : -2]
     for b in range(blocks):
         k_ref[b * BLOCK : (b + 1) * BLOCK, :] = kv[b][0:HEAD_DIM, :].T
 
@@ -222,15 +218,15 @@
         s_ref[slot] = s
         return jnp.max(s, axis=0, keepdims=True)
 
-    def one_tile(columns, next_columns, top, slot, packed):
+    def one_tile(tile, columns, next_columns, top, slot):
         for n, (which, b, first, last) in enumerate(steps):
             if first:
-                if fresh:
+                if which in fresh:
                     m = jnp.full((1, TILE), -jnp.inf, jnp.float32)
                     l = jnp.zeros((1, TILE), jnp.float32)
                     acc = jnp.zeros((HEAD_DIM, TILE), jnp.float32)
                 else:
-                    m, l, acc = (old[3 * which + i][:, columns] for i in range(3))
+                    m, l, acc = (ref[:, columns] for ref in old[which])
             newest = jnp.maximum(m, top)
             factor = jnp.exp2((m - newest) * SCORE_SCALE)
             if n + 1 < len(steps):
@@ -246,27 +242,28 @@
                 preferred_element_type=jnp.float32,
             )
             m = newest
-            if last and packed is None:
+            if last and tile not in pack:
                 new[3 * which][:, columns] = m
                 new[3 * which + 1][:, columns] = l
                 new[3 * which + 2][:, columns] = acc
             elif last:
-                packed[0:HEAD_DIM, :] = (acc / l).astype(jnp.bfloat16)
+                pack_ref = packs[pack.index(tile)]
+                pack_ref[0:HEAD_DIM, :] = (acc / l).astype(jnp.bfloat16)
                 lse = m * SCORE_SCALE + jnp.log2(l)
                 high = lse.astype(jnp.bfloat16).astype(jnp.float32)
                 middle = (lse - high).astype(jnp.bfloat16).astype(jnp.float32)
                 low = lse - high - middle
                 row = lax.broadcasted_iota(jnp.int32, (PACK_ROWS - HEAD_DIM, TILE), 0)
                 rows = jnp.where(row == 0, high, jnp.where(row == 1, middle, low))
-                packed[HEAD_DIM:PACK_ROWS, :] = rows.astype(jnp.bfloat16)
+                pack_ref[HEAD_DIM:PACK_ROWS, :] = rows.astype(jnp.bfloat16)
         return top, slot
 
-    if len(steps) % 2 == 0 and len(steps) > 2:
+    if len(steps) % 2 == 0 and not pack:
 
         def body(i, top):
             here = pl.ds(pl.multiple_of(i * TILE, TILE), TILE)
             after = pl.ds(pl.multiple_of(lax.rem(i + 1, tiles) * TILE, TILE), TILE)
-            return one_tile(here, after, top, 0, None)[0]
+            return one_tile(-1, here, after, top, 0)[0]
 
         lax.fori_loop(0, tiles, body, score(steps[0], slice(0, TILE), 0))
     else:
@@ -274,22 +271,23 @@
         for i in range(tiles):
             here = slice(i * TILE, (i + 1) * TILE)
             after = slice((i + 1) * TILE, (i + 2) * TILE) if i + 1 < tiles else None
-            packed = packs[pack.index(i)] if i in pack else None
-            top, slot = one_tile(here, after, top, slot, packed)
+            top, slot = one_tile(i, here, after, top, slot)
 
 
 def attend(kv, queries, states, work, pack=()):
     sets = len(queries)
-    fresh = states is None
-    width = BLOCK if not pack else TILE
+    fresh = tuple(n for n, state in enumerate(states) if state is None)
+    width = BLOCK - TILE * len(pack)
     out_shape = [jax.ShapeDtypeStruct((PACK_ROWS, TILE), jnp.bfloat16)] * len(pack)
-    if len(pack) < BLOCK // TILE:
+    if width > 0:
         out_shape += [
             jax.ShapeDtypeStruct((1, width), jnp.float32),
             jax.ShapeDtypeStruct((1, width), jnp.float32),
             jax.ShapeDtypeStruct((HEAD_DIM, width), jnp.float32),
         ] * sets
-    operands = list(kv) + list(queries) + ([] if fresh else list(states))
+    operands = list(kv) + list(queries)
+    for state in states:
+        operands += [] if state is None else list(state)
     count = sum(len(chosen) for _, chosen in work)
     return pl.pallas_call(
         functools.partial(
@@ -425,26 +423,25 @@
             left = send(left, 0, -1, 0)
         if step == 0:
             partner = send(queries, 1, 0, 0)
-            mine = attend([own], [queries], None, ((0, (0,)),))
-        elif step == 1:
-            late = near[1]
-            theirs = attend([own, *near], [partner], None, ((0, (0, 1, 2)),))
-            mine = attend(near[:1], [queries], mine, ((0, (0,)),))
+            mine = attend([own], [queries], [None], ((0, (0,)),))
         else:
-            both = attend(
-                near, [queries, partner], mine + theirs, ((0, (0, 1)), (1, (0, 1)))
-            )
+            if step == 1:
+                late = near[1]
+                blocks, work = (own, *near), ((1, (0, 1, 2)), (0, (1,)))
+            else:
+                blocks, work = near, ((0, (0, 1)), (1, (0, 1)))
+            both = attend(blocks, [queries, partner], [mine, theirs], work)
             mine, theirs = both[:3], both[3:]
-    for_mine, for_other = attend([right], [partner], theirs, ((0, (0,)),), pack=(0, 1))
+    for_mine, for_other = attend([right], [partner], [theirs], ((0, (0,)),), pack=(0, 1))
     from_partner = send(for_mine, 1, 0, 0)
     from_diagonal = send(for_other, 1, 0, 1)
-    for_core, *state = attend([late, right], [queries], mine, ((0, (0, 1)),), pack=(1,))
+    for_core, *state = attend([late, right], [queries], [mine], ((0, (0, 1)),), pack=(1,))
     from_core = send(for_core, 0, 0, 1)
     terms = dict(zip(STEPS, output(state, from_partner, from_core, from_diagonal, w_last)))
+    by_column = [send_heads(terms[1, 1], (1, 0)), send_heads(terms[3, 1], (3, 0))]
+    parts = [send_heads(add(terms[0, 1], *by_column), (0, 1))]
     by_partner = send_heads(terms[2, 1], (0, 1))
-    by_column = [send_heads(terms[1, 1], (1, 0)), send_heads(terms[3, 1], (3, 0))]
-    parts = [send_heads(add(terms[2, 0], by_partner), (2, 0))]
-    parts += [send_heads(add(terms[0, 1], *by_column), (0, 1))]
+    parts += [send_heads(add(terms[2, 0], by_partner), (2, 0))]
     parts += [send_heads(terms[1, 0], (1, 0)), send_heads(terms[3, 0], (3, 0)), terms[0, 0]]
     return finish(parts, tokens, vectors)
 

time: 84.5 us -> 82.8 us (0.980)
  Pallas kernels: 26.7 us -> 25.6 us
    pallas_call x7 -> x6, Pallas kernels: 22.5 us -> 21.4 us  [attend(): pl.pallas_call(functools.partial(attend_kernel, blocks=len(kv), sets=sets...]
  transfers between devices with their start and end apart: 26 -> 26, of which waited for: 9 -> 8; matrix products, arithmetic and copies ran while one was open for 0% -> 0% of each run, Pallas kernels for 26% -> 25%
where the time goes in v1:
time: 82.8 us; the launch traced here: 82.4 us
  starting transfers between devices  39.1 us (47%)
  Pallas kernels  25.6 us (31%)
  waiting for transfers between devices  13.9 us (17%)
  local copies, waits for them, and re-layouts  3.62 us (4%)
    pallas_call x6, Pallas kernels, attend(): pl.pallas_call(functools.partial(attend_kernel, blocks=len(kv), sets=sets...  21.4 us
    ppermute x14, starting transfers between devices, send_heads(): return lax.ppermute(array, 'heads', heads_shift(*step))  20.3 us
    ppermute x12, starting transfers between devices, send(): return lax.ppermute(array, 'frames', frames_shift(dy, dz, dc))  18.8 us
    ppermute x12, waiting for transfers between devices, send(): return lax.ppermute(array, 'frames', frames_shift(dy, dz, dc))  8.35 us
    ppermute x14, waiting for transfers between devices, send_heads(): return lax.ppermute(array, 'heads', heads_shift(*step))  5.54 us
    unnamed x16, local copies, waits for them, and re-layouts  3.53 us
    pallas_call x1, Pallas kernels, project(): pl.pallas_call(project_kernel, out_shape=(shape, shape), in_specs=whole(1...  1.69 us
  transfers between devices with their start and end apart: 26, of which 8 were waited for; matrix products, arithmetic and copies ran while one was open for 0% of the time, Pallas kernels for 25%

profile of v1, /device:TPU:8, one launch (start us, length us, event | category | flops | bytes accessed | tf_op | source)
XLA Modules:
  0.0 82.4 jit_solution(17802632941106737820)
XLA Ops:
  0.0 2.2 %collective-permute-start = (bf16[512,128]{1,0:T(8,128)(2,1)}, bf16[512,128]{1,0:T(8,128)(2,1)S(1)}, u32[]{:S(2)}, u32[]{:S(2)}) collective-permute-start(bf16[512,128]{1,0:T(8,128)(2,1)} %tokens_ref.1), channel_id=1, source_target_pairs={{0,1},{1,0},{2,3},{3,2},{4,5},{5,4},{6,7},{7,6},{8,9},{9,8},{10,11... | collective-permute-start | bytes 393224 | tf_op jit(solution)/shard_map/ppermute | solution.py:48
  2.2 1.3 %collective-permute-start.3 = (bf16[512,128]{1,0:T(8,128)(2,1)}, bf16[512,128]{1,0:T(8,128)(2,1)S(1)}, u32[]{:S(2)}, u32[]{:S(2)}) collective-permute-start(bf16[512,128]{1,0:T(8,128)(2,1)} %tokens_ref.1), channel_id=1, source_target_pairs={{0,4},{1,5},{2,6},{3,7},{4,0},{5,1},{6,2},{7,3},{8,12},{9,13},{10,... | collective-permute-start | bytes 393224 | tf_op jit(solution)/shard_map/ppermute | solution.py:48
  4.1 2.6 %collective-permute-start.2 = (bf16[512,128]{1,0:T(8,128)(2,1)}, bf16[512,128]{1,0:T(8,128)(2,1)S(1)}, u32[]{:S(2)}, u32[]{:S(2)}) collective-permute-start(bf16[512,128]{1,0:T(8,128)(2,1)} %tokens_ref.1), channel_id=1, source_target_pairs={{0,6},{1,7},{2,0},{3,1},{4,2},{5,3},{6,4},{7,5},{8,14},{9,15},{10,... | collective-permute-start | bytes 393224 | tf_op jit(solution)/shard_map/ppermute | solution.py:48
  6.9 3.0 %collective-permute-start.5 = (bf16[512,128]{1,0:T(8,128)(2,1)S(1)}, bf16[512,128]{1,0:T(8,128)(2,1)S(1)}, u32[]{:S(2)}, u32[]{:S(2)}) collective-permute-start(bf16[512,128]{1,0:T(8,128)(2,1)S(1)} %collective-permute-done.refs_1_), channel_id=1, source_target_pairs={{0,6},{1,7},{2,0},{3,1},{4,2},{5,3},{6,4},{7,5},{8,14},{9,15},{10,... | collective-permute-start | bytes 393224 | tf_op jit(solution)/shard_map/ppermute | solution.py:48
  10.0 1.6 %collective-permute-start.6 = (bf16[512,128]{1,0:T(8,128)(2,1)S(1)}, bf16[512,128]{1,0:T(8,128)(2,1)S(1)}, u32[]{:S(2)}, u32[]{:S(2)}) collective-permute-start(bf16[512,128]{1,0:T(8,128)(2,1)S(1)} %collective-permute-done.3.refs_4_), channel_id=1, source_target_pairs={{0,1},{1,0},{2,3},{3,2},{4,5},{5,4},{6,7},{7,6},{8,9},{9,8},{10,11... | collective-permute-start | bytes 393224 | tf_op jit(solution)/shard_map/ppermute | solution.py:48
  12.3 0.9 %copy-done.2 = bf16[1024,128]{1,0:T(8,128)(2,1)S(1)} copy-done((bf16[1024,128]{1,0:T(8,128)(2,1)S(1)}, bf16[1024,128]{1,0:T(8,128)(2,1)}, u32[]{:S(2)}) %copy-start.2) | copy-done | bytes 262168
  13.3 0.9 %copy-done.3 = bf16[1024,128]{1,0:T(8,128)(2,1)S(1)} copy-done((bf16[1024,128]{1,0:T(8,128)(2,1)S(1)}, bf16[1024,128]{1,0:T(8,128)(2,1)}, u32[]{:S(2)}) %copy-start.3) | copy-done | bytes 262168
  14.2 0.9 %copy-done.4 = bf16[128,1024]{1,0:T(8,128)(2,1)S(1)} copy-done((bf16[128,1024]{1,0:T(8,128)(2,1)S(1)}, bf16[128,1024]{1,0:T(8,128)(2,1)}, u32[]{:S(2)}) %copy-start.4) | copy-done | bytes 262168
  15.2 1.1 %prepare.1 = (bf16[384,1024]{1,0:T(8,128)(2,1)S(1)}, bf16[128,1024]{1,0:T(8,128)(2,1)S(1)}, f32[24,128]{1,0:T(8,128)S(1)}) custom-call(s32[17]{0:T(128)S(1)} %stack.65.place_ref, bf16[1024,128]{1,0:T(8,128)(2,1)S(1)} %copy-done.1, bf16[1024,128]{1,0:T(8,128)(2,1)S(1)} %copy-done.2, bf16[1024,128]{1,0:T(8,128)(2,1)S(1)} %copy-done.3, ...), custom_call_target="tpu_custom_call" | custom-call | flops 402653184 | bytes 4194304 | tf_op jit(solution)/shard_map/prepare/pallas_call | solution.py:102
  16.4 1.7 %norm_project.1 = (bf16[192,512]{1,0:T(8,128)(2,1)S(1)}, bf16[192,512]{1,0:T(8,128)(2,1)S(1)}) custom-call(bf16[512,128]{1,0:T(8,128)(2,1)S(1)} %copy-done, bf16[512,128]{1,0:T(8,128)(2,1)S(1)} %collective-permute-done.refs_1_, bf16[512,128]{1,0:T(8,128)(2,1)S(1)} %collective-permute-done.1.refs_2_, bf16[512,128]{1,0:T(8,128)(2,1)S(1)} %collective-permute-done.2.refs_3_, ...), custom_call_target="tpu_custom_call" | custom-call | flops 402653184 | bytes 2097152 | tf_op jit(solution)/shard_map/norm_project/pallas_call | solution.py:156
  18.2 1.4 %collective-permute-done.7.taken = bf16[192,512]{1,0:T(8,128)(2,1)S(1)} collective-permute-done((bf16[192,512]{1,0:T(8,128)(2,1)S(1)}, bf16[192,512]{1,0:T(8,128)(2,1)S(1)}, u32[]{:S(2)}, u32[]{:S(2)}) %collective-permute-start.7) | collective-permute-done | bytes 196640 | tf_op jit(solution)/shard_map/ppermute | solution.py:34
  19.6 2.0 %collective-permute-start.9 = (bf16[128,1024]{1,0:T(8,128)(2,1)S(1)}, bf16[128,1024]{1,0:T(8,128)(2,1)S(1)}, u32[]{:S(2)}, u32[]{:S(2)}) collective-permute-start(bf16[128,1024]{1,0:T(8,128)(2,1)S(1)} %get-tuple-element.51.refs_0_), channel_id=1, source_target_pairs={{0,16},{8,24},{16,32},{24,40},{32,48},{40,56},{48,64},{56,72},{64,... | collective-permute-start | bytes 786440 | tf_op jit(solution)/shard_map/ppermute | solution.py:34
  21.6 4.0 %collective-permute-start.8 = (bf16[128,1024]{1,0:T(8,128)(2,1)S(1)}, bf16[128,1024]{1,0:T(8,128)(2,1)S(1)}, u32[]{:S(2)}, u32[]{:S(2)}) collective-permute-start(bf16[128,1024]{1,0:T(8,128)(2,1)S(1)} %get-tuple-element.51.refs_0_), channel_id=1, source_target_pairs={{0,112},{8,120},{16,0},{24,8},{32,16},{40,24},{48,32},{56,40},{64,... | collective-permute-start | bytes 786440 | tf_op jit(solution)/shard_map/ppermute | solution.py:34
  25.7 2.3 %collective-permute-start.15 = (bf16[64,1024]{1,0:T(8,128)(2,1)S(1)}, bf16[64,1024]{1,0:T(8,128)(2,1)S(1)}, u32[]{:S(2)}, u32[]{:S(2)}) collective-permute-start(bf16[64,1024]{1,0:T(8,128)(2,1)S(1)} %get-tuple-element.52.refs_1_.refs_3_.refs_2_), channel_id=1, source_target_pairs={{0,128},{8,136},{16,144},{24,152},{32,160},{40,168},{48,176},{56,1... | collective-permute-start | bytes 393224 | tf_op jit(solution)/shard_map/ppermute | solution.py:34
  28.0 1.8 %attend.6 = (f32[1,1024]{1,0:T(1,128)S(1)}, f32[1,1024]{1,0:T(1,128)S(1)}, f32[64,1024]{1,0:T(8,128)S(1)}) custom-call(bf16[128,1024]{1,0:T(8,128)(2,1)S(1)} %get-tuple-element.51.refs_0_, bf16[64,1024]{1,0:T(8,128)(2,1)S(1)} %get-tuple-element.52.refs_1_.refs_3_.refs_2_), custom_call_target="tpu_custom_call" | custom-call | flops 1073741824 | bytes 1048576 | tf_op jit(solution)/shard_map/attend/pallas_call | solution.py:292
  29.7 2.5 %collective-permute-done.9.refs_1_ = bf16[128,1024]{1,0:T(8,128)(2,1)S(1)} collective-permute-done((bf16[128,1024]{1,0:T(8,128)(2,1)S(1)}, bf16[128,1024]{1,0:T(8,128)(2,1)S(1)}, u32[]{:S(2)}, u32[]{:S(2)}) %collective-permute-start.9) | collective-permute-done | bytes 262176 | tf_op jit(solution)/shard_map/ppermute | solution.py:34
  32.2 3.2 %collective-permute-start.13 = (bf16[128,1024]{1,0:T(8,128)(2,1)S(1)}, bf16[128,1024]{1,0:T(8,128)(2,1)S(1)}, u32[]{:S(2)}, u32[]{:S(2)}) collective-permute-start(bf16[128,1024]{1,0:T(8,128)(2,1)S(1)} %collective-permute-done.8.refs_2_.refs_0_), channel_id=1, source_target_pairs={{0,112},{8,120},{16,0},{24,8},{32,16},{40,24},{48,32},{56,40},{64,... | collective-permute-start | bytes 786440 | tf_op jit(solution)/shard_map/ppermute | solution.py:34
  35.4 4.9 %attend.7 = (f32[1,1024]{1,0:T(1,128)S(1)}, f32[1,1024]{1,0:T(1,128)S(1)}, f32[64,1024]{1,0:T(8,128)S(1)}, f32[1,1024]{1,0:T(1,128)S(1)}, f32[1,1024]{1,0:T(1,128)S(1)}, /*index=5*/f32[64,1024]{1,0:T(8,128)S(1)}) custom-call(bf16[128,1024]{1,0:T(8,128)(2,1)S(1)} %get-tuple-element.51.refs_0_, bf16[128,1024]{1,0:T(8,128)(2,1)S(1)} %collective-permute-done.9.refs_1_, ...), custom_call_target="tpu_custom_call" | custom-call | flops 4294967296 | bytes 1048576 | tf_op jit(solution)/shard_map/attend/pallas_call | solution.py:292
  41.2 3.2 %collective-permute-start.14 = (bf16[128,1024]{1,0:T(8,128)(2,1)S(1)}, bf16[128,1024]{1,0:T(8,128)(2,1)S(1)}, u32[]{:S(2)}, u32[]{:S(2)}) collective-permute-start(bf16[128,1024]{1,0:T(8,128)(2,1)S(1)} %collective-permute-done.13.refs_1_), channel_id=1, source_target_pairs={{0,112},{8,120},{16,0},{24,8},{32,16},{40,24},{48,32},{56,40},{64,... | collective-permute-start | bytes 786440 | tf_op jit(solution)/shard_map/ppermute | solution.py:34
  44.5 4.9 %attend.8 = (f32[1,1024]{1,0:T(1,128)S(1)}, f32[1,1024]{1,0:T(1,128)S(1)}, f32[64,1024]{1,0:T(8,128)S(1)}, f32[1,1024]{1,0:T(1,128)S(1)}, f32[1,1024]{1,0:T(1,128)S(1)}, /*index=5*/f32[64,1024]{1,0:T(8,128)S(1)}) custom-call(bf16[128,1024]{1,0:T(8,128)(2,1)S(1)} %collective-permute-done.10.refs_0_, bf16[128,1024]{1,0:T(8,128)(2,1)S(1)} %collective-permute-done.13.refs_1_, ...), custom_call_target="tpu_custom_call" | custom-call | flops 4294967296 | bytes 1048576 | tf_op jit(solution)/shard_map/attend/pallas_call | solution.py:292
  49.5 4.9 %attend.9 = (f32[1,1024]{1,0:T(1,128)S(1)}, f32[1,1024]{1,0:T(1,128)S(1)}, f32[64,1024]{1,0:T(8,128)S(1)}, f32[1,1024]{1,0:T(1,128)S(1)}, f32[1,1024]{1,0:T(1,128)S(1)}, /*index=5*/f32[64,1024]{1,0:T(8,128)S(1)}) custom-call(bf16[128,1024]{1,0:T(8,128)(2,1)S(1)} %collective-permute-done.11.refs_0_, bf16[128,1024]{1,0:T(8,128)(2,1)S(1)} %collective-permute-done.14.refs_1_, ...), custom_call_target="tpu_custom_call" | custom-call | flops 4294967296 | bytes 1048576 | tf_op jit(solution)/shard_map/attend/pallas_call | solution.py:292
  54.5 2.6 %collective-permute-done.12.refs_1_.refs_0_ = bf16[128,1024]{1,0:T(8,128)(2,1)S(1)} collective-permute-done((bf16[128,1024]{1,0:T(8,128)(2,1)S(1)}, bf16[128,1024]{1,0:T(8,128)(2,1)S(1)}, u32[]{:S(2)}, u32[]{:S(2)}) %collective-permute-start.12) | collective-permute-done | bytes 262176 | tf_op jit(solution)/shard_map/ppermute | solution.py:34
  57.1 1.8 %attend.11 = (bf16[80,512]{1,0:T(8,128)(2,1)S(1)}, bf16[80,512]{1,0:T(8,128)(2,1)S(1)}) custom-call(bf16[128,1024]{1,0:T(8,128)(2,1)S(1)} %collective-permute-done.12.refs_1_.refs_0_, bf16[64,1024]{1,0:T(8,128)(2,1)S(1)} %collective-permute-done.15.refs_4_.refs_3_.refs_1_, f32[1,1024]{1,0:T(1,128)S(1)} %get-tuple-element.74.refs_2_, ...), custom_call_target="tpu_custom_call" | custom-call | flops 1073741824 | bytes 1048576 | tf_op jit(solution)/shard_map/attend/pallas_call | solution.py:292
  58.9 2.4 %collective-permute-start.16 = (bf16[80,512]{1,0:T(8,128)(2,1)S(1)}, bf16[80,512]{1,0:T(8,128)(2,1)S(1)}, u32[]{:S(2)}, u32[]{:S(2)}) collective-permute-start(bf16[80,512]{1,0:T(8,128)(2,1)S(1)} %get-tuple-element.77), channel_id=1, source_target_pairs={{0,128},{8,136},{16,144},{24,152},{32,160},{40,168},{48,176},{56,1... | collective-permute-start | bytes 245768 | tf_op jit(solution)/shard_map/ppermute | solution.py:34
  61.3 3.1 %attend.10 = (bf16[80,512]{1,0:T(8,128)(2,1)S(1)}, f32[1,512]{1,0:T(1,128)S(1)}, f32[1,512]{1,0:T(1,128)S(1)}, f32[64,512]{1,0:T(8,128)S(1)}) custom-call(bf16[128,1024]{1,0:T(8,128)(2,1)S(1)} %collective-permute-done.8.refs_2_.refs_0_, bf16[128,1024]{1,0:T(8,128)(2,1)S(1)} %collective-permute-done.12.refs_1_.refs_0_, ...), custom_call_target="tpu_custom_call" | custom-call | flops 2147483648 | bytes 1048576 | tf_op jit(solution)/shard_map/attend/pallas_call | solution.py:292
  64.3 1.4 %collective-permute-start.17 = (bf16[80,512]{1,0:T(8,128)(2,1)S(1)}, bf16[80,512]{1,0:T(8,128)(2,1)S(1)}, u32[]{:S(2)}, u32[]{:S(2)}) collective-permute-start(bf16[80,512]{1,0:T(8,128)(2,1)S(1)} %get-tuple-element.78), channel_id=1, source_target_pairs={{0,8},{8,0},{16,24},{24,16},{32,40},{40,32},{48,56},{56,48},{64,72... | collective-permute-start | bytes 245768 | tf_op jit(solution)/shard_map/ppermute | solution.py:34
  65.8 0.9 %collective-permute-done.18.diagonal_ref = bf16[80,512]{1,0:T(8,128)(2,1)S(1)} collective-permute-done((bf16[80,512]{1,0:T(8,128)(2,1)S(1)}, bf16[80,512]{1,0:T(8,128)(2,1)S(1)}, u32[]{:S(2)}, u32[]{:S(2)}) %collective-permute-start.18) | collective-permute-done | bytes 81952 | tf_op jit(solution)/shard_map/ppermute | solution.py:34
  67.2 1.4 %collective-permute-start.22 = (bf16[512,128]{1,0:T(8,128)(2,1)S(1)}, bf16[512,128]{1,0:T(8,128)(2,1)S(1)}, u32[]{:S(2)}, u32[]{:S(2)}) collective-permute-start(bf16[512,128]{1,0:T(8,128)(2,1)S(1)} %get-tuple-element.85), channel_id=1, source_target_pairs={{0,1},{1,0},{2,3},{3,2},{4,5},{5,4},{6,7},{7,6},{8,9},{9,8},{10,11... | collective-permute-start | bytes 393224 | tf_op jit(solution)/shard_map/ppermute | solution.py:48
  68.6 3.2 %collective-permute-start.20 = (bf16[512,128]{1,0:T(8,128)(2,1)S(1)}, bf16[512,128]{1,0:T(8,128)(2,1)S(1)}, u32[]{:S(2)}, u32[]{:S(2)}) collective-permute-start(bf16[512,128]{1,0:T(8,128)(2,1)S(1)} %get-tuple-element.83), channel_id=1, source_target_pairs={{0,6},{1,7},{2,0},{3,1},{4,2},{5,3},{6,4},{7,5},{8,14},{9,15},{10,... | collective-permute-start | bytes 393224 | tf_op jit(solution)/shard_map/ppermute | solution.py:48
  71.8 3.2 %collective-permute-start.25 = (bf16[512,128]{1,0:T(8,128)(2,1)S(1)}, bf16[512,128]{1,0:T(8,128)(2,1)S(1)}, u32[]{:S(2)}, u32[]{:S(2)}) collective-permute-start(bf16[512,128]{1,0:T(8,128)(2,1)S(1)} %get-tuple-element.87), channel_id=1, source_target_pairs={{0,6},{1,7},{2,0},{3,1},{4,2},{5,3},{6,4},{7,5},{8,14},{9,15},{10,... | collective-permute-start | bytes 393224 | tf_op jit(solution)/shard_map/ppermute | solution.py:48
  76.2 3.2 %collective-permute-done.24.refs_2_ = bf16[512,128]{1,0:T(8,128)(2,1)S(1)} collective-permute-done((bf16[512,128]{1,0:T(8,128)(2,1)S(1)}, bf16[512,128]{1,0:T(8,128)(2,1)S(1)}, u32[]{:S(2)}, u32[]{:S(2)}) %collective-permute-start.24) | collective-permute-done | bytes 131104 | tf_op jit(solution)/shard_map/ppermute | solution.py:48
  79.9 1.7 %collective-permute-done.23.refs_1_ = bf16[512,128]{1,0:T(8,128)(2,1)S(1)} collective-permute-done((bf16[512,128]{1,0:T(8,128)(2,1)S(1)}, bf16[512,128]{1,0:T(8,128)(2,1)S(1)}, u32[]{:S(2)}, u32[]{:S(2)}) %collective-permute-start.23) | collective-permute-done | bytes 131104 | tf_op jit(solution)/shard_map/ppermute | solution.py:48
  (50 shorter events, 5.7 us)
Async XLA Ops:
  0.0 11.7 %copy-start.1 = (bf16[1024,128]{1,0:T(8,128)(2,1)S(1)}, bf16[1024,128]{1,0:T(8,128)(2,1)}, u32[]{:S(2)}) copy-start(bf16[1024,128]{1,0:T(8,128)(2,1)} %wq_hbm.1) | copy-start | bytes 786436
  0.0 6.7 %collective-permute-start = (bf16[512,128]{1,0:T(8,128)(2,1)}, bf16[512,128]{1,0:T(8,128)(2,1)S(1)}, u32[]{:S(2)}, u32[]{:S(2)}) collective-permute-start(bf16[512,128]{1,0:T(8,128)(2,1)} %tokens_ref.1), channel_id=1, source_target_pairs={{0,1},{1,0},{2,3},{3,2},{4,5},{5,4},{6,7},{7,6},{8,9},{9,8},{10,11... | collective-permute-start | bytes 393224 | tf_op jit(solution)/shard_map/ppermute | solution.py:48
  2.2 7.8 %collective-permute-start.3 = (bf16[512,128]{1,0:T(8,128)(2,1)}, bf16[512,128]{1,0:T(8,128)(2,1)S(1)}, u32[]{:S(2)}, u32[]{:S(2)}) collective-permute-start(bf16[512,128]{1,0:T(8,128)(2,1)} %tokens_ref.1), channel_id=1, source_target_pairs={{0,4},{1,5},{2,6},{3,7},{4,0},{5,1},{6,2},{7,3},{8,12},{9,13},{10,... | collective-permute-start | bytes 393224 | tf_op jit(solution)/shard_map/ppermute | solution.py:48
  3.5 12.8 %collective-permute-start.1 = (bf16[512,128]{1,0:T(8,128)(2,1)}, bf16[512,128]{1,0:T(8,128)(2,1)S(1)}, u32[]{:S(2)}, u32[]{:S(2)}) collective-permute-start(bf16[512,128]{1,0:T(8,128)(2,1)} %tokens_ref.1), channel_id=1, source_target_pairs={{0,2},{1,3},{2,4},{3,5},{4,6},{5,7},{6,0},{7,1},{8,10},{9,11},{10,... | collective-permute-start | bytes 393224 | tf_op jit(solution)/shard_map/ppermute | solution.py:48
  4.1 12.3 %collective-permute-start.2 = (bf16[512,128]{1,0:T(8,128)(2,1)}, bf16[512,128]{1,0:T(8,128)(2,1)S(1)}, u32[]{:S(2)}, u32[]{:S(2)}) collective-permute-start(bf16[512,128]{1,0:T(8,128)(2,1)} %tokens_ref.1), channel_id=1, source_target_pairs={{0,6},{1,7},{2,0},{3,1},{4,2},{5,3},{6,4},{7,5},{8,14},{9,15},{10,... | collective-permute-start | bytes 393224 | tf_op jit(solution)/shard_map/ppermute | solution.py:48
  6.7 9.6 %collective-permute-start.4 = (bf16[512,128]{1,0:T(8,128)(2,1)S(1)}, bf16[512,128]{1,0:T(8,128)(2,1)S(1)}, u32[]{:S(2)}, u32[]{:S(2)}) collective-permute-start(bf16[512,128]{1,0:T(8,128)(2,1)S(1)} %collective-permute-done.refs_1_), channel_id=1, source_target_pairs={{0,2},{1,3},{2,4},{3,5},{4,6},{5,7},{6,0},{7,1},{8,10},{9,11},{10,... | collective-permute-start | bytes 393224 | tf_op jit(solution)/shard_map/ppermute | solution.py:48
  6.9 9.4 %collective-permute-start.5 = (bf16[512,128]{1,0:T(8,128)(2,1)S(1)}, bf16[512,128]{1,0:T(8,128)(2,1)S(1)}, u32[]{:S(2)}, u32[]{:S(2)}) collective-permute-start(bf16[512,128]{1,0:T(8,128)(2,1)S(1)} %collective-permute-done.refs_1_), channel_id=1, source_target_pairs={{0,6},{1,7},{2,0},{3,1},{4,2},{5,3},{6,4},{7,5},{8,14},{9,15},{10,... | collective-permute-start | bytes 393224 | tf_op jit(solution)/shard_map/ppermute | solution.py:48
  10.0 6.4 %collective-permute-start.6 = (bf16[512,128]{1,0:T(8,128)(2,1)S(1)}, bf16[512,128]{1,0:T(8,128)(2,1)S(1)}, u32[]{:S(2)}, u32[]{:S(2)}) collective-permute-start(bf16[512,128]{1,0:T(8,128)(2,1)S(1)} %collective-permute-done.3.refs_4_), channel_id=1, source_target_pairs={{0,1},{1,0},{2,3},{3,2},{4,5},{5,4},{6,7},{7,6},{8,9},{9,8},{10,11... | collective-permute-start | bytes 393224 | tf_op jit(solution)/shard_map/ppermute | solution.py:48
  11.6 0.7 copy-start.5
  12.3 1.0 %copy-start.2 = (bf16[1024,128]{1,0:T(8,128)(2,1)S(1)}, bf16[1024,128]{1,0:T(8,128)(2,1)}, u32[]{:S(2)}) copy-start(bf16[1024,128]{1,0:T(8,128)(2,1)} %wk_hbm.1) | copy-start | bytes 786436
  13.3 0.9 %copy-start.3 = (bf16[1024,128]{1,0:T(8,128)(2,1)S(1)}, bf16[1024,128]{1,0:T(8,128)(2,1)}, u32[]{:S(2)}) copy-start(bf16[1024,128]{1,0:T(8,128)(2,1)} %wv_hbm.1) | copy-start | bytes 786436
  14.2 0.9 %copy-start.4 = (bf16[128,1024]{1,0:T(8,128)(2,1)S(1)}, bf16[128,1024]{1,0:T(8,128)(2,1)}, u32[]{:S(2)}) copy-start(bf16[128,1024]{1,0:T(8,128)(2,1)} %w_out_hbm.1) | copy-start | bytes 786436
  15.2 1.2 %copy-start = (bf16[512,128]{1,0:T(8,128)(2,1)S(1)}, bf16[512,128]{1,0:T(8,128)(2,1)}, u32[]{:S(2)}) copy-start(bf16[512,128]{1,0:T(8,128)(2,1)} %tokens_ref.1) | copy-start | bytes 393220
  18.1 1.5 %collective-permute-start.7 = (bf16[192,512]{1,0:T(8,128)(2,1)S(1)}, bf16[192,512]{1,0:T(8,128)(2,1)S(1)}, u32[]{:S(2)}, u32[]{:S(2)}) collective-permute-start(bf16[192,512]{1,0:T(8,128)(2,1)S(1)} %get-tuple-element.50), channel_id=1, source_target_pairs={{0,8},{8,0},{16,24},{24,16},{32,40},{40,32},{48,56},{56,48},{64,72... | collective-permute-start | bytes 589832 | tf_op jit(solution)/shard_map/ppermute | solution.py:34
  19.6 12.5 %collective-permute-start.9 = (bf16[128,1024]{1,0:T(8,128)(2,1)S(1)}, bf16[128,1024]{1,0:T(8,128)(2,1)S(1)}, u32[]{:S(2)}, u32[]{:S(2)}) collective-permute-start(bf16[128,1024]{1,0:T(8,128)(2,1)S(1)} %get-tuple-element.51.refs_0_), channel_id=1, source_target_pairs={{0,16},{8,24},{16,32},{24,40},{32,48},{40,56},{48,64},{56,72},{64,... | collective-permute-start | bytes 786440 | tf_op jit(solution)/shard_map/ppermute | solution.py:34
  21.6 10.5 %collective-permute-start.8 = (bf16[128,1024]{1,0:T(8,128)(2,1)S(1)}, bf16[128,1024]{1,0:T(8,128)(2,1)S(1)}, u32[]{:S(2)}, u32[]{:S(2)}) collective-permute-start(bf16[128,1024]{1,0:T(8,128)(2,1)S(1)} %get-tuple-element.51.refs_0_), channel_id=1, source_target_pairs={{0,112},{8,120},{16,0},{24,8},{32,16},{40,24},{48,32},{56,40},{64,... | collective-permute-start | bytes 786440 | tf_op jit(solution)/shard_map/ppermute | solution.py:34
  25.7 9.8 %collective-permute-start.15 = (bf16[64,1024]{1,0:T(8,128)(2,1)S(1)}, bf16[64,1024]{1,0:T(8,128)(2,1)S(1)}, u32[]{:S(2)}, u32[]{:S(2)}) collective-permute-start(bf16[64,1024]{1,0:T(8,128)(2,1)S(1)} %get-tuple-element.52.refs_1_.refs_3_.refs_2_), channel_id=1, source_target_pairs={{0,128},{8,136},{16,144},{24,152},{32,160},{40,168},{48,176},{56,1... | collective-permute-start | bytes 393224 | tf_op jit(solution)/shard_map/ppermute | solution.py:34
  32.2 9.0 %collective-permute-start.10 = (bf16[128,1024]{1,0:T(8,128)(2,1)S(1)}, bf16[128,1024]{1,0:T(8,128)(2,1)S(1)}, u32[]{:S(2)}, u32[]{:S(2)}) collective-permute-start(bf16[128,1024]{1,0:T(8,128)(2,1)S(1)} %collective-permute-done.9.refs_1_), channel_id=1, source_target_pairs={{0,16},{8,24},{16,32},{24,40},{32,48},{40,56},{48,64},{56,72},{64,... | collective-permute-start | bytes 786440 | tf_op jit(solution)/shard_map/ppermute | solution.py:34
  32.2 9.0 %collective-permute-start.13 = (bf16[128,1024]{1,0:T(8,128)(2,1)S(1)}, bf16[128,1024]{1,0:T(8,128)(2,1)S(1)}, u32[]{:S(2)}, u32[]{:S(2)}) collective-permute-start(bf16[128,1024]{1,0:T(8,128)(2,1)S(1)} %collective-permute-done.8.refs_2_.refs_0_), channel_id=1, source_target_pairs={{0,112},{8,120},{16,0},{24,8},{32,16},{40,24},{48,32},{56,40},{64,... | collective-permute-start | bytes 786440 | tf_op jit(solution)/shard_map/ppermute | solution.py:34
  41.2 8.2 %collective-permute-start.11 = (bf16[128,1024]{1,0:T(8,128)(2,1)S(1)}, bf16[128,1024]{1,0:T(8,128)(2,1)S(1)}, u32[]{:S(2)}, u32[]{:S(2)}) collective-permute-start(bf16[128,1024]{1,0:T(8,128)(2,1)S(1)} %collective-permute-done.10.refs_0_), channel_id=1, source_target_pairs={{0,16},{8,24},{16,32},{24,40},{32,48},{40,56},{48,64},{56,72},{64,... | collective-permute-start | bytes 786440 | tf_op jit(solution)/shard_map/ppermute | solution.py:34
  41.2 8.3 %collective-permute-start.14 = (bf16[128,1024]{1,0:T(8,128)(2,1)S(1)}, bf16[128,1024]{1,0:T(8,128)(2,1)S(1)}, u32[]{:S(2)}, u32[]{:S(2)}) collective-permute-start(bf16[128,1024]{1,0:T(8,128)(2,1)S(1)} %collective-permute-done.13.refs_1_), channel_id=1, source_target_pairs={{0,112},{8,120},{16,0},{24,8},{32,16},{40,24},{48,32},{56,40},{64,... | collective-permute-start | bytes 786440 | tf_op jit(solution)/shard_map/ppermute | solution.py:34
  49.4 7.7 %collective-permute-start.12 = (bf16[128,1024]{1,0:T(8,128)(2,1)S(1)}, bf16[128,1024]{1,0:T(8,128)(2,1)S(1)}, u32[]{:S(2)}, u32[]{:S(2)}) collective-permute-start(bf16[128,1024]{1,0:T(8,128)(2,1)S(1)} %collective-permute-done.11.refs_0_), channel_id=1, source_target_pairs={{0,16},{8,24},{16,32},{24,40},{32,48},{40,56},{48,64},{56,72},{64,... | collective-permute-start | bytes 786440 | tf_op jit(solution)/shard_map/ppermute | solution.py:34
  58.9 6.9 %collective-permute-start.16 = (bf16[80,512]{1,0:T(8,128)(2,1)S(1)}, bf16[80,512]{1,0:T(8,128)(2,1)S(1)}, u32[]{:S(2)}, u32[]{:S(2)}) collective-permute-start(bf16[80,512]{1,0:T(8,128)(2,1)S(1)} %get-tuple-element.77), channel_id=1, source_target_pairs={{0,128},{8,136},{16,144},{24,152},{32,160},{40,168},{48,176},{56,1... | collective-permute-start | bytes 245768 | tf_op jit(solution)/shard_map/ppermute | solution.py:34
  61.3 5.4 %collective-permute-start.18 = (bf16[80,512]{1,0:T(8,128)(2,1)S(1)}, bf16[80,512]{1,0:T(8,128)(2,1)S(1)}, u32[]{:S(2)}, u32[]{:S(2)}) collective-permute-start(bf16[80,512]{1,0:T(8,128)(2,1)S(1)} %get-tuple-element.79), channel_id=1, source_target_pairs={{0,136},{8,128},{16,152},{24,144},{32,168},{40,160},{48,184},{56,1... | collective-permute-start | bytes 245768 | tf_op jit(solution)/shard_map/ppermute | solution.py:34
  64.3 2.4 %collective-permute-start.17 = (bf16[80,512]{1,0:T(8,128)(2,1)S(1)}, bf16[80,512]{1,0:T(8,128)(2,1)S(1)}, u32[]{:S(2)}, u32[]{:S(2)}) collective-permute-start(bf16[80,512]{1,0:T(8,128)(2,1)S(1)} %get-tuple-element.78), channel_id=1, source_target_pairs={{0,8},{8,0},{16,24},{24,16},{32,40},{40,32},{48,56},{56,48},{64,72... | collective-permute-start | bytes 245768 | tf_op jit(solution)/shard_map/ppermute | solution.py:34
  67.2 7.8 %collective-permute-start.22 = (bf16[512,128]{1,0:T(8,128)(2,1)S(1)}, bf16[512,128]{1,0:T(8,128)(2,1)S(1)}, u32[]{:S(2)}, u32[]{:S(2)}) collective-permute-start(bf16[512,128]{1,0:T(8,128)(2,1)S(1)} %get-tuple-element.85), channel_id=1, source_target_pairs={{0,1},{1,0},{2,3},{3,2},{4,5},{5,4},{6,7},{7,6},{8,9},{9,8},{10,11... | collective-permute-start | bytes 393224 | tf_op jit(solution)/shard_map/ppermute | solution.py:48
  68.6 6.6 %collective-permute-start.19 = (bf16[512,128]{1,0:T(8,128)(2,1)S(1)}, bf16[512,128]{1,0:T(8,128)(2,1)S(1)}, u32[]{:S(2)}, u32[]{:S(2)}) collective-permute-start(bf16[512,128]{1,0:T(8,128)(2,1)S(1)} %get-tuple-element.82), channel_id=1, source_target_pairs={{0,2},{1,3},{2,4},{3,5},{4,6},{5,7},{6,0},{7,1},{8,10},{9,11},{10,... | collective-permute-start | bytes 393224 | tf_op jit(solution)/shard_map/ppermute | solution.py:48
  68.6 6.7 %collective-permute-start.20 = (bf16[512,128]{1,0:T(8,128)(2,1)S(1)}, bf16[512,128]{1,0:T(8,128)(2,1)S(1)}, u32[]{:S(2)}, u32[]{:S(2)}) collective-permute-start(bf16[512,128]{1,0:T(8,128)(2,1)S(1)} %get-tuple-element.83), channel_id=1, source_target_pairs={{0,6},{1,7},{2,0},{3,1},{4,2},{5,3},{6,4},{7,5},{8,14},{9,15},{10,... | collective-permute-start | bytes 393224 | tf_op jit(solution)/shard_map/ppermute | solution.py:48
  71.8 7.6 %collective-permute-start.24 = (bf16[512,128]{1,0:T(8,128)(2,1)S(1)}, bf16[512,128]{1,0:T(8,128)(2,1)S(1)}, u32[]{:S(2)}, u32[]{:S(2)}) collective-permute-start(bf16[512,128]{1,0:T(8,128)(2,1)S(1)} %get-tuple-element.86), channel_id=1, source_target_pairs={{0,2},{1,3},{2,4},{3,5},{4,6},{5,7},{6,0},{7,1},{8,10},{9,11},{10,... | collective-permute-start | bytes 393224 | tf_op jit(solution)/shard_map/ppermute | solution.py:48
  71.8 8.1 %collective-permute-start.25 = (bf16[512,128]{1,0:T(8,128)(2,1)S(1)}, bf16[512,128]{1,0:T(8,128)(2,1)S(1)}, u32[]{:S(2)}, u32[]{:S(2)}) collective-permute-start(bf16[512,128]{1,0:T(8,128)(2,1)S(1)} %get-tuple-element.87), channel_id=1, source_target_pairs={{0,6},{1,7},{2,0},{3,1},{4,2},{5,3},{6,4},{7,5},{8,14},{9,15},{10,... | collective-permute-start | bytes 393224 | tf_op jit(solution)/shard_map/ppermute | solution.py:48
  75.1 6.6 %collective-permute-start.23 = (bf16[512,128]{1,0:T(8,128)(2,1)S(1)}, bf16[512,128]{1,0:T(8,128)(2,1)S(1)}, u32[]{:S(2)}, u32[]{:S(2)}) collective-permute-start(bf16[512,128]{1,0:T(8,128)(2,1)S(1)} %add.126), channel_id=1, source_target_pairs={{0,4},{1,5},{2,6},{3,7},{4,0},{5,1},{6,2},{7,3},{8,12},{9,13},{10,... | collective-permute-start | bytes 393224 | tf_op jit(solution)/shard_map/ppermute | solution.py:48
  75.3 6.3 %collective-permute-start.21 = (bf16[512,128]{1,0:T(8,128)(2,1)S(1)}, bf16[512,128]{1,0:T(8,128)(2,1)S(1)}, u32[]{:S(2)}, u32[]{:S(2)}) collective-permute-start(bf16[512,128]{1,0:T(8,128)(2,1)S(1)} %add.125), channel_id=1, source_target_pairs={{0,1},{1,0},{2,3},{3,2},{4,5},{5,4},{6,7},{7,6},{8,9},{9,8},{10,11... | collective-permute-start | bytes 393224 | tf_op jit(solution)/shard_map/ppermute | solution.py:48
  (2 other events, 1.4 us)

commit v2 on v1

--- a/solution.py
+++ b/solution.py
@@ -57,13 +57,13 @@
 
 
 def prepare_kernel(
-    place_ref, wq_hbm, wk_hbm, wv_hbm, w_out_hbm, gain_hbm, bias_hbm, scale_hbm,
-    w_ref, out_ref, vectors_ref,
-    wq_ref, wk_ref, wv_ref, w_out_ref, gain_ref, bias_ref, scale_ref, flipped_ref, done,
+    place_ref, wq_hbm, wk_hbm, wv_hbm, gain_hbm, bias_hbm,
+    w_ref, vectors_ref,
+    wq_ref, wk_ref, wv_ref, gain_ref, bias_ref, flipped_ref, done,
 ):
     pairs = (
-        (wq_hbm, wq_ref), (wk_hbm, wk_ref), (wv_hbm, wv_ref), (w_out_hbm, w_out_ref),
-        (gain_hbm, gain_ref), (bias_hbm, bias_ref), (scale_hbm, scale_ref),
+        (wq_hbm, wq_ref), (wk_hbm, wk_ref), (wv_hbm, wv_ref),
+        (gain_hbm, gain_ref), (bias_hbm, bias_ref),
     )
     copies = [pltpu.make_async_copy(a, b, done.at[n]) for n, (a, b) in enumerate(pairs)]
     for copy in copies:
@@ -86,39 +86,60 @@
                 w_ref[at : at + HEAD_DIM, n * width : (n + 1) * width] = flipped_ref[
                     rows, columns(1 + n)
                 ]
-    for h, rows in enumerate(heads):
-        for n in range(count):
-            out_ref[h * HEAD_DIM : (h + 1) * HEAD_DIM, n * width : (n + 1) * width] = w_out_ref[
-                rows, columns(1 + count + n)
-            ]
     for n in range(count):
         j = place_ref[1 + n]
         vectors_ref[n : n + 1, :] = gain_ref[pl.ds(j, 1), :]
         vectors_ref[count + n : count + n + 1, :] = bias_ref[pl.ds(j, 1), :]
-    vectors_ref[2 * count : 3 * count, :] = jnp.broadcast_to(scale_ref[...], (count, width))
-
-
-def prepare(place, wq, wk, wv, w_out, gain, bias, scale):
+
+
+def prepare(place, wq, wk, wv, gain, bias):
     return pl.pallas_call(
         prepare_kernel,
         out_shape=(
             jax.ShapeDtypeStruct((6 * HEAD_DIM, FEATURES), jnp.bfloat16),
-            jax.ShapeDtypeStruct((2 * HEAD_DIM, FEATURES), jnp.bfloat16),
-            jax.ShapeDtypeStruct((3 * len(STEPS), FEATURES // len(STEPS)), jnp.float32),
+            jax.ShapeDtypeStruct((2 * len(STEPS), FEATURES // len(STEPS)), jnp.float32),
         ),
         in_specs=[pl.BlockSpec(memory_space=pltpu.SMEM)]
-        + [pl.BlockSpec(memory_space=pltpu.MemorySpace.HBM)] * 7,
-        out_specs=tuple(whole(3)),
-        scratch_shapes=[
-            pltpu.VMEM(a.shape, a.dtype) for a in (wq, wk, wv, w_out, gain, bias, scale)
-        ]
-        + [pltpu.VMEM((2 * HEAD_DIM, FEATURES), jnp.bfloat16), pltpu.SemaphoreType.DMA((7,))],
+        + [pl.BlockSpec(memory_space=pltpu.MemorySpace.HBM)] * 5,
+        out_specs=tuple(whole(2)),
+        scratch_shapes=[pltpu.VMEM(a.shape, a.dtype) for a in (wq, wk, wv, gain, bias)]
+        + [pltpu.VMEM((2 * HEAD_DIM, FEATURES), jnp.bfloat16), pltpu.SemaphoreType.DMA((5,))],
         compiler_params=params(),
         name="prepare",
         cost_estimate=pl.CostEstimate(
             flops=2 * HALF * FEATURES * 384, bytes_accessed=4 * 2**20, transcendentals=0
         ),
-    )(place, wq, wk, wv, w_out, gain, bias, scale)
+    )(place, wq, wk, wv, gain, bias)
+
+
+def arrange_kernel(place_ref, w_ref, scale_ref, after_ref, out_ref, vector_ref):
+    core = place_ref[0]
+    count = len(STEPS)
+    width = FEATURES // count
+    for at, h in enumerate((core, 1 - core)):
+        rows = pl.ds(pl.multiple_of(h * HEAD_DIM, HEAD_DIM), HEAD_DIM)
+        for n in range(count):
+            columns = pl.ds(pl.multiple_of(place_ref[1 + count + n] * width, width), width)
+            out_ref[at * HEAD_DIM : (at + 1) * HEAD_DIM, n * width : (n + 1) * width] = w_ref[
+                rows, columns
+            ]
+    vector_ref[...] = jnp.broadcast_to(scale_ref[...], vector_ref.shape)
+
+
+def arrange(place, w_out, scale, after):
+    return pl.pallas_call(
+        arrange_kernel,
+        out_shape=(
+            jax.ShapeDtypeStruct(w_out.shape, w_out.dtype),
+            jax.ShapeDtypeStruct((8, scale.shape[1]), jnp.float32),
+        ),
+        in_specs=[pl.BlockSpec(memory_space=pltpu.SMEM)]
+        + whole(2)
+        + [pl.BlockSpec(memory_space=pl.ANY)],
+        out_specs=tuple(whole(2)),
+        compiler_params=params(),
+        name="arrange",
+    )(place, w_out, scale, after)
 
 
 def project_kernel(*refs):
@@ -187,7 +208,7 @@
     )(keep, taken)
 
 
-def attend_kernel(*refs, blocks, sets, work, fresh, pack):
+def attend_kernel(*refs, blocks, sets, work, fresh, pack, waits):
     kv = refs[:blocks]
     queries = refs[blocks : blocks + sets]
     at = blocks + sets
@@ -197,6 +218,7 @@
             old[which] = refs[at : at + 3]
             at += 3
     k_ref, s_ref = refs[-2:]
+    at += waits
     packs, new = refs[at : at + len(pack)], refs[at + len(pack) : -2]
     for b in range(blocks):
         k_ref[b * BLOCK : (b + 1) * BLOCK, :] = kv[b][0:HEAD_DIM, :].T
@@ -274,7 +296,7 @@
             top, slot = one_tile(i, here, after, top, slot)
 
 
-def attend(kv, queries, states, work, pack=()):
+def attend(kv, queries, states, work, pack=(), after=()):
     sets = len(queries)
     fresh = tuple(n for n, state in enumerate(states) if state is None)
     width = BLOCK - TILE * len(pack)
@@ -291,10 +313,16 @@
     count = sum(len(chosen) for _, chosen in work)
     return pl.pallas_call(
         functools.partial(
-            attend_kernel, blocks=len(kv), sets=sets, work=work, fresh=fresh, pack=pack
+            attend_kernel,
+            blocks=len(kv),
+            sets=sets,
+            work=work,
+            fresh=fresh,
+            pack=pack,
+            waits=len(after),
         ),
         out_shape=tuple(out_shape),
-        in_specs=whole(len(operands)),
+        in_specs=whole(len(operands)) + [pl.BlockSpec(memory_space=pl.ANY)] * len(after),
         out_specs=tuple(whole(len(out_shape))),
         scratch_shapes=[
             pltpu.VMEM((len(kv) * BLOCK, HEAD_DIM), jnp.bfloat16),
@@ -307,7 +335,7 @@
             bytes_accessed=2**20,
             transcendentals=count * BLOCK * BLOCK,
         ),
-    )(*operands)
+    )(*operands, *after)
 
 
 def unpack(pack_ref):
@@ -351,34 +379,34 @@
     )(*state, mine, core, diagonal, w_out)
 
 
-def add_kernel(*refs):
+def add_kernel(*refs, terms):
     total = refs[0][...].astype(jnp.float32)
-    for ref in refs[1:-1]:
+    for ref in refs[1:terms]:
         total = total + ref[...].astype(jnp.float32)
     refs[-1][...] = total.astype(jnp.bfloat16)
 
 
-def add(*terms):
-    return pl.pallas_call(
-        add_kernel,
+def add(*terms, after=()):
+    return pl.pallas_call(
+        functools.partial(add_kernel, terms=len(terms)),
         out_shape=jax.ShapeDtypeStruct(terms[0].shape, jnp.bfloat16),
-        in_specs=whole(len(terms)),
+        in_specs=whole(len(terms)) + [pl.BlockSpec(memory_space=pl.ANY)] * len(after),
         out_specs=whole(1)[0],
         compiler_params=params(),
         name="add",
-    )(*terms)
-
-
-def finish_kernel(tokens_ref, vectors_ref, *refs):
+    )(*terms, *after)
+
+
+def finish_kernel(tokens_ref, scale_ref, *refs):
     out_ref = refs[-1]
     total = refs[0][...].astype(jnp.float32)
     for part_ref in refs[1:-1]:
         total = total + part_ref[...].astype(jnp.float32)
-    scale = vectors_ref[2 * len(STEPS) : 2 * len(STEPS) + 1, :]
+    scale = scale_ref[0:1, :]
     out_ref[...] = (tokens_ref[...].astype(jnp.float32) + scale * total).astype(jnp.bfloat16)
 
 
-def finish(parts, tokens, vectors):
+def finish(parts, tokens, scale):
     return pl.pallas_call(
         finish_kernel,
         out_shape=jax.ShapeDtypeStruct(tokens.shape, jnp.bfloat16),
@@ -386,7 +414,7 @@
         out_specs=whole(1)[0],
         compiler_params=params(),
         name="finish",
-    )(tokens, vectors, *parts)
+    )(tokens, scale, *parts)
 
 
 def per_device(tokens, norm_gain, norm_bias, w_query, w_key, w_value, w_out, layer_scale):
@@ -402,18 +430,17 @@
     beside = send_heads(tokens, (0, 1))
     blocks = [tokens, beside, send_heads(tokens, (1, 0)), send_heads(tokens, (3, 0)), across]
     blocks += [send_heads(beside, (1, 0)), send_heads(beside, (3, 0)), send_heads(across, (0, 1))]
-    w_all, w_last, vectors = prepare(
+    w_all, vectors = prepare(
         place,
         w_query,
         w_key,
         w_value,
-        w_out,
         norm_gain.reshape(groups, width),
         norm_bias.reshape(groups, width),
-        layer_scale.reshape(1, width),
     )
     keep, give = project(blocks, vectors, w_all)
     queries, own = join(keep, send(give, 0, 0, 1))
+    w_last, scale = arrange(place, w_out, layer_scale.reshape(1, width), own)
     right, left = own, own
     mine, theirs = None, None
     for step in range(4):
@@ -430,12 +457,16 @@
                 blocks, work = (own, *near), ((1, (0, 1, 2)), (0, (1,)))
             else:
                 blocks, work = near, ((0, (0, 1)), (1, (0, 1)))
-            both = attend(blocks, [queries, partner], [mine, theirs], work)
+            both = attend(
+                blocks, [queries, partner], [mine, theirs], work, after=[w_last] if step == 1 else ()
+            )
             mine, theirs = both[:3], both[3:]
     for_mine, for_other = attend([right], [partner], [theirs], ((0, (0,)),), pack=(0, 1))
     from_partner = send(for_mine, 1, 0, 0)
     from_diagonal = send(for_other, 1, 0, 1)
-    for_core, *state = attend([late, right], [queries], [mine], ((0, (0, 1)),), pack=(1,))
+    for_core, *state = attend(
+        [late, right], [queries], [mine], ((0, (0, 1)),), pack=(1,)
+    )
     from_core = send(for_core, 0, 0, 1)
     terms = dict(zip(STEPS, output(state, from_partner, from_core, from_diagonal, w_last)))
     by_column = [send_heads(terms[1, 1], (1, 0)), send_heads(terms[3, 1], (3, 0))]
@@ -443,7 +474,7 @@
     by_partner = send_heads(terms[2, 1], (0, 1))
     parts += [send_heads(add(terms[2, 0], by_partner), (2, 0))]
     parts += [send_heads(terms[1, 0], (1, 0)), send_heads(terms[3, 0], (3, 0)), terms[0, 0]]
-    return finish(parts, tokens, vectors)
+    return finish(parts, tokens, scale)
 
 
 def solution(mesh):

time: 82.8 us -> 82 us (level)
  local copies, waits for them, and re-layouts: 3.62 us -> 2.6 us
    unnamed x16, local copies, waits for them, and re-layouts: 3.53 us -> 2.51 us
  transfers between devices with their start and end apart: 26 -> 26, of which waited for: 8 -> 8; matrix products, arithmetic and copies ran while one was open for 0% -> 0% of each run, Pallas kernels for 25% -> 26%
where the time goes in v2:
time: 82 us; the launch traced here: 81.9 us
  starting transfers between devices  39.2 us (48%)
  Pallas kernels  26.3 us (32%)
  waiting for transfers between devices  13.6 us (17%)
  local copies, waits for them, and re-layouts  2.6 us (3%)
    pallas_call x6, Pallas kernels, attend(): pl.pallas_call(functools.partial(attend_kernel, blocks=len(kv), sets=sets...  21.5 us
    ppermute x14, starting transfers between devices, send_heads(): return lax.ppermute(array, 'heads', heads_shift(*step))  20.4 us
    ppermute x12, starting transfers between devices, send(): return lax.ppermute(array, 'frames', frames_shift(dy, dz, dc))  18.8 us
    ppermute x12, waiting for transfers between devices, send(): return lax.ppermute(array, 'frames', frames_shift(dy, dz, dc))  7.63 us
    ppermute x14, waiting for transfers between devices, send_heads(): return lax.ppermute(array, 'heads', heads_shift(*step))  5.94 us
    unnamed x16, local copies, waits for them, and re-layouts  2.51 us
    pallas_call x1, Pallas kernels, project(): pl.pallas_call(project_kernel, out_shape=(shape, shape), in_specs=whole(1...  1.69 us
  transfers between devices with their start and end apart: 26, of which 8 were waited for; matrix products, arithmetic and copies ran while one was open for 0% of the time, Pallas kernels for 26%

profile of v2, /device:TPU:8, one launch (start us, length us, event | category | flops | bytes accessed | tf_op | source)
XLA Modules:
  0.0 81.9 jit_solution(4078496064752956503)
XLA Ops:
  0.0 2.2 %collective-permute-start = (bf16[512,128]{1,0:T(8,128)(2,1)}, bf16[512,128]{1,0:T(8,128)(2,1)S(1)}, u32[]{:S(2)}, u32[]{:S(2)}) collective-permute-start(bf16[512,128]{1,0:T(8,128)(2,1)} %tokens_ref.1), channel_id=1, source_target_pairs={{0,1},{1,0},{2,3},{3,2},{4,5},{5,4},{6,7},{7,6},{8,9},{9,8},{10,11... | collective-permute-start | bytes 393224 | tf_op jit(solution)/shard_map/ppermute | solution.py:48
  2.2 1.3 %collective-permute-start.3 = (bf16[512,128]{1,0:T(8,128)(2,1)}, bf16[512,128]{1,0:T(8,128)(2,1)S(1)}, u32[]{:S(2)}, u32[]{:S(2)}) collective-permute-start(bf16[512,128]{1,0:T(8,128)(2,1)} %tokens_ref.1), channel_id=1, source_target_pairs={{0,4},{1,5},{2,6},{3,7},{4,0},{5,1},{6,2},{7,3},{8,12},{9,13},{10,... | collective-permute-start | bytes 393224 | tf_op jit(solution)/shard_map/ppermute | solution.py:48
  4.1 2.6 %collective-permute-start.2 = (bf16[512,128]{1,0:T(8,128)(2,1)}, bf16[512,128]{1,0:T(8,128)(2,1)S(1)}, u32[]{:S(2)}, u32[]{:S(2)}) collective-permute-start(bf16[512,128]{1,0:T(8,128)(2,1)} %tokens_ref.1), channel_id=1, source_target_pairs={{0,6},{1,7},{2,0},{3,1},{4,2},{5,3},{6,4},{7,5},{8,14},{9,15},{10,... | collective-permute-start | bytes 393224 | tf_op jit(solution)/shard_map/ppermute | solution.py:48
  6.9 3.0 %collective-permute-start.5 = (bf16[512,128]{1,0:T(8,128)(2,1)S(1)}, bf16[512,128]{1,0:T(8,128)(2,1)S(1)}, u32[]{:S(2)}, u32[]{:S(2)}) collective-permute-start(bf16[512,128]{1,0:T(8,128)(2,1)S(1)} %collective-permute-done.refs_1_), channel_id=1, source_target_pairs={{0,6},{1,7},{2,0},{3,1},{4,2},{5,3},{6,4},{7,5},{8,14},{9,15},{10,... | collective-permute-start | bytes 393224 | tf_op jit(solution)/shard_map/ppermute | solution.py:48
  10.0 1.6 %collective-permute-start.6 = (bf16[512,128]{1,0:T(8,128)(2,1)S(1)}, bf16[512,128]{1,0:T(8,128)(2,1)S(1)}, u32[]{:S(2)}, u32[]{:S(2)}) collective-permute-start(bf16[512,128]{1,0:T(8,128)(2,1)S(1)} %collective-permute-done.3.refs_4_), channel_id=1, source_target_pairs={{0,1},{1,0},{2,3},{3,2},{4,5},{5,4},{6,7},{7,6},{8,9},{9,8},{10,11... | collective-permute-start | bytes 393224 | tf_op jit(solution)/shard_map/ppermute | solution.py:48
  12.2 0.9 %copy-done.4 = bf16[1024,128]{1,0:T(8,128)(2,1)S(1)} copy-done((bf16[1024,128]{1,0:T(8,128)(2,1)S(1)}, bf16[1024,128]{1,0:T(8,128)(2,1)}, u32[]{:S(2)}) %copy-start.4) | copy-done | bytes 262168
  13.2 0.9 %copy-done.5 = bf16[1024,128]{1,0:T(8,128)(2,1)S(1)} copy-done((bf16[1024,128]{1,0:T(8,128)(2,1)S(1)}, bf16[1024,128]{1,0:T(8,128)(2,1)}, u32[]{:S(2)}) %copy-start.5) | copy-done | bytes 262168
  14.1 1.1 %prepare.1 = (bf16[384,1024]{1,0:T(8,128)(2,1)S(1)}, f32[16,128]{1,0:T(8,128)S(1)}) custom-call(s32[17]{0:T(128)S(1)} %stack.65.place_ref, bf16[1024,128]{1,0:T(8,128)(2,1)S(1)} %copy-done.3, bf16[1024,128]{1,0:T(8,128)(2,1)S(1)} %copy-done.4, bf16[1024,128]{1,0:T(8,128)(2,1)S(1)} %copy-done.5, f32[8,128]{1,0:T(8,128)S(1)} %bitcast.19, f32[8,128]{1,0:T(8,128)S(1)} %bitcast.20), custom_call_target="tpu_custom_call" | custom-call | flops 402653184 | bytes 4194304 | tf_op jit(solution)/shard_map/prepare/pallas_call | solution.py:96
  15.3 1.7 %norm_project.1 = (bf16[192,512]{1,0:T(8,128)(2,1)S(1)}, bf16[192,512]{1,0:T(8,128)(2,1)S(1)}) custom-call(bf16[512,128]{1,0:T(8,128)(2,1)S(1)} %copy-done, bf16[512,128]{1,0:T(8,128)(2,1)S(1)} %collective-permute-done.refs_1_, bf16[512,128]{1,0:T(8,128)(2,1)S(1)} %collective-permute-done.1.refs_2_, bf16[512,128]{1,0:T(8,128)(2,1)S(1)} %collective-permute-done.2.refs_3_, ...), custom_call_target="tpu_custom_call" | custom-call | flops 402653184 | bytes 2097152 | tf_op jit(solution)/shard_map/norm_project/pallas_call | solution.py:177
  17.1 1.4 %collective-permute-done.7.taken = bf16[192,512]{1,0:T(8,128)(2,1)S(1)} collective-permute-done((bf16[192,512]{1,0:T(8,128)(2,1)S(1)}, bf16[192,512]{1,0:T(8,128)(2,1)S(1)}, u32[]{:S(2)}, u32[]{:S(2)}) %collective-permute-start.7) | collective-permute-done | bytes 196640 | tf_op jit(solution)/shard_map/ppermute | solution.py:34
  18.6 2.0 %collective-permute-start.9 = (bf16[128,1024]{1,0:T(8,128)(2,1)S(1)}, bf16[128,1024]{1,0:T(8,128)(2,1)S(1)}, u32[]{:S(2)}, u32[]{:S(2)}) collective-permute-start(bf16[128,1024]{1,0:T(8,128)(2,1)S(1)} %get-tuple-element.52.after_ref.refs_0_), channel_id=1, source_target_pairs={{0,16},{8,24},{16,32},{24,40},{32,48},{40,56},{48,64},{56,72},{64,... | collective-permute-start | bytes 786440 | tf_op jit(solution)/shard_map/ppermute | solution.py:34
  20.6 4.0 %collective-permute-start.8 = (bf16[128,1024]{1,0:T(8,128)(2,1)S(1)}, bf16[128,1024]{1,0:T(8,128)(2,1)S(1)}, u32[]{:S(2)}, u32[]{:S(2)}) collective-permute-start(bf16[128,1024]{1,0:T(8,128)(2,1)S(1)} %get-tuple-element.52.after_ref.refs_0_), channel_id=1, source_target_pairs={{0,112},{8,120},{16,0},{24,8},{32,16},{40,24},{48,32},{56,40},{64,... | collective-permute-start | bytes 786440 | tf_op jit(solution)/shard_map/ppermute | solution.py:34
  24.6 2.3 %collective-permute-start.15 = (bf16[64,1024]{1,0:T(8,128)(2,1)S(1)}, bf16[64,1024]{1,0:T(8,128)(2,1)S(1)}, u32[]{:S(2)}, u32[]{:S(2)}) collective-permute-start(bf16[64,1024]{1,0:T(8,128)(2,1)S(1)} %get-tuple-element.54.refs_1_.refs_3_.refs_2_), channel_id=1, source_target_pairs={{0,128},{8,136},{16,144},{24,152},{32,160},{40,168},{48,176},{56,1... | collective-permute-start | bytes 393224 | tf_op jit(solution)/shard_map/ppermute | solution.py:34
  27.5 1.8 %attend.6 = (f32[1,1024]{1,0:T(1,128)S(1)}, f32[1,1024]{1,0:T(1,128)S(1)}, f32[64,1024]{1,0:T(8,128)S(1)}) custom-call(bf16[128,1024]{1,0:T(8,128)(2,1)S(1)} %get-tuple-element.52.after_ref.refs_0_, bf16[64,1024]{1,0:T(8,128)(2,1)S(1)} %get-tuple-element.54.refs_1_.refs_3_.refs_2_), custom_call_target="tpu_custom_call" | custom-call | flops 1073741824 | bytes 1048576 | tf_op jit(solution)/shard_map/attend/pallas_call | solution.py:314
  29.3 1.8 %collective-permute-done.9.refs_1_ = bf16[128,1024]{1,0:T(8,128)(2,1)S(1)} collective-permute-done((bf16[128,1024]{1,0:T(8,128)(2,1)S(1)}, bf16[128,1024]{1,0:T(8,128)(2,1)S(1)}, u32[]{:S(2)}, u32[]{:S(2)}) %collective-permute-start.9) | collective-permute-done | bytes 262176 | tf_op jit(solution)/shard_map/ppermute | solution.py:34
  31.1 3.2 %collective-permute-start.13 = (bf16[128,1024]{1,0:T(8,128)(2,1)S(1)}, bf16[128,1024]{1,0:T(8,128)(2,1)S(1)}, u32[]{:S(2)}, u32[]{:S(2)}) collective-permute-start(bf16[128,1024]{1,0:T(8,128)(2,1)S(1)} %collective-permute-done.8.refs_2_.refs_0_), channel_id=1, source_target_pairs={{0,112},{8,120},{16,0},{24,8},{32,16},{40,24},{48,32},{56,40},{64,... | collective-permute-start | bytes 786440 | tf_op jit(solution)/shard_map/ppermute | solution.py:34
  34.3 4.9 %attend.7 = (f32[1,1024]{1,0:T(1,128)S(1)}, f32[1,1024]{1,0:T(1,128)S(1)}, f32[64,1024]{1,0:T(8,128)S(1)}, f32[1,1024]{1,0:T(1,128)S(1)}, f32[1,1024]{1,0:T(1,128)S(1)}, /*index=5*/f32[64,1024]{1,0:T(8,128)S(1)}) custom-call(bf16[128,1024]{1,0:T(8,128)(2,1)S(1)} %get-tuple-element.52.after_ref.refs_0_, bf16[128,1024]{1,0:T(8,128)(2,1)S(1)} %collective-permute-done.9.refs_1_, ...), custom_call_target="tpu_custom_call" | custom-call | flops 4294967296 | bytes 1048576 | tf_op jit(solution)/shard_map/attend/pallas_call | solution.py:314
  39.3 0.9 %collective-permute-done.10.refs_0_ = bf16[128,1024]{1,0:T(8,128)(2,1)S(1)} collective-permute-done((bf16[128,1024]{1,0:T(8,128)(2,1)S(1)}, bf16[128,1024]{1,0:T(8,128)(2,1)S(1)}, u32[]{:S(2)}, u32[]{:S(2)}) %collective-permute-start.10) | collective-permute-done | bytes 262176 | tf_op jit(solution)/shard_map/ppermute | solution.py:34
  40.2 3.2 %collective-permute-start.14 = (bf16[128,1024]{1,0:T(8,128)(2,1)S(1)}, bf16[128,1024]{1,0:T(8,128)(2,1)S(1)}, u32[]{:S(2)}, u32[]{:S(2)}) collective-permute-start(bf16[128,1024]{1,0:T(8,128)(2,1)S(1)} %collective-permute-done.13.refs_1_), channel_id=1, source_target_pairs={{0,112},{8,120},{16,0},{24,8},{32,16},{40,24},{48,32},{56,40},{64,... | collective-permute-start | bytes 786440 | tf_op jit(solution)/shard_map/ppermute | solution.py:34
  43.4 5.0 %attend.8 = (f32[1,1024]{1,0:T(1,128)S(1)}, f32[1,1024]{1,0:T(1,128)S(1)}, f32[64,1024]{1,0:T(8,128)S(1)}, f32[1,1024]{1,0:T(1,128)S(1)}, f32[1,1024]{1,0:T(1,128)S(1)}, /*index=5*/f32[64,1024]{1,0:T(8,128)S(1)}) custom-call(bf16[128,1024]{1,0:T(8,128)(2,1)S(1)} %collective-permute-done.10.refs_0_, bf16[128,1024]{1,0:T(8,128)(2,1)S(1)} %collective-permute-done.13.refs_1_, ...), custom_call_target="tpu_custom_call" | custom-call | flops 4294967296 | bytes 1048576 | tf_op jit(solution)/shard_map/attend/pallas_call | solution.py:314
  48.5 5.0 %attend.9 = (f32[1,1024]{1,0:T(1,128)S(1)}, f32[1,1024]{1,0:T(1,128)S(1)}, f32[64,1024]{1,0:T(8,128)S(1)}, f32[1,1024]{1,0:T(1,128)S(1)}, f32[1,1024]{1,0:T(1,128)S(1)}, /*index=5*/f32[64,1024]{1,0:T(8,128)S(1)}) custom-call(bf16[128,1024]{1,0:T(8,128)(2,1)S(1)} %collective-permute-done.11.refs_0_, bf16[128,1024]{1,0:T(8,128)(2,1)S(1)} %collective-permute-done.14.refs_1_, ...), custom_call_target="tpu_custom_call" | custom-call | flops 4294967296 | bytes 1048576 | tf_op jit(solution)/shard_map/attend/pallas_call | solution.py:314
  53.5 2.6 %collective-permute-done.12.refs_1_.refs_0_ = bf16[128,1024]{1,0:T(8,128)(2,1)S(1)} collective-permute-done((bf16[128,1024]{1,0:T(8,128)(2,1)S(1)}, bf16[128,1024]{1,0:T(8,128)(2,1)S(1)}, u32[]{:S(2)}, u32[]{:S(2)}) %collective-permute-start.12) | collective-permute-done | bytes 262176 | tf_op jit(solution)/shard_map/ppermute | solution.py:34
  56.1 1.8 %attend.11 = (bf16[80,512]{1,0:T(8,128)(2,1)S(1)}, bf16[80,512]{1,0:T(8,128)(2,1)S(1)}) custom-call(bf16[128,1024]{1,0:T(8,128)(2,1)S(1)} %collective-permute-done.12.refs_1_.refs_0_, bf16[64,1024]{1,0:T(8,128)(2,1)S(1)} %collective-permute-done.15.refs_4_.refs_3_.refs_1_, f32[1,1024]{1,0:T(1,128)S(1)} %get-tuple-element.77.refs_2_, ...), custom_call_target="tpu_custom_call" | custom-call | flops 1073741824 | bytes 1048576 | tf_op jit(solution)/shard_map/attend/pallas_call | solution.py:314
  57.8 2.4 %collective-permute-start.16 = (bf16[80,512]{1,0:T(8,128)(2,1)S(1)}, bf16[80,512]{1,0:T(8,128)(2,1)S(1)}, u32[]{:S(2)}, u32[]{:S(2)}) collective-permute-start(bf16[80,512]{1,0:T(8,128)(2,1)S(1)} %get-tuple-element.80), channel_id=1, source_target_pairs={{0,128},{8,136},{16,144},{24,152},{32,160},{40,168},{48,176},{56,1... | collective-permute-start | bytes 245768 | tf_op jit(solution)/shard_map/ppermute | solution.py:34
  60.2 3.1 %attend.10 = (bf16[80,512]{1,0:T(8,128)(2,1)S(1)}, f32[1,512]{1,0:T(1,128)S(1)}, f32[1,512]{1,0:T(1,128)S(1)}, f32[64,512]{1,0:T(8,128)S(1)}) custom-call(bf16[128,1024]{1,0:T(8,128)(2,1)S(1)} %collective-permute-done.8.refs_2_.refs_0_, bf16[128,1024]{1,0:T(8,128)(2,1)S(1)} %collective-permute-done.12.refs_1_.refs_0_, ...), custom_call_target="tpu_custom_call" | custom-call | flops 2147483648 | bytes 1048576 | tf_op jit(solution)/shard_map/attend/pallas_call | solution.py:314
  63.3 1.4 %collective-permute-start.17 = (bf16[80,512]{1,0:T(8,128)(2,1)S(1)}, bf16[80,512]{1,0:T(8,128)(2,1)S(1)}, u32[]{:S(2)}, u32[]{:S(2)}) collective-permute-start(bf16[80,512]{1,0:T(8,128)(2,1)S(1)} %get-tuple-element.81), channel_id=1, source_target_pairs={{0,8},{8,0},{16,24},{24,16},{32,40},{40,32},{48,56},{56,48},{64,72... | collective-permute-start | bytes 245768 | tf_op jit(solution)/shard_map/ppermute | solution.py:34
  64.7 0.9 %collective-permute-done.18.diagonal_ref = bf16[80,512]{1,0:T(8,128)(2,1)S(1)} collective-permute-done((bf16[80,512]{1,0:T(8,128)(2,1)S(1)}, bf16[80,512]{1,0:T(8,128)(2,1)S(1)}, u32[]{:S(2)}, u32[]{:S(2)}) %collective-permute-start.18) | collective-permute-done | bytes 81952 | tf_op jit(solution)/shard_map/ppermute | solution.py:34
  66.2 1.8 %collective-permute-start.22 = (bf16[512,128]{1,0:T(8,128)(2,1)S(1)}, bf16[512,128]{1,0:T(8,128)(2,1)S(1)}, u32[]{:S(2)}, u32[]{:S(2)}) collective-permute-start(bf16[512,128]{1,0:T(8,128)(2,1)S(1)} %get-tuple-element.87), channel_id=1, source_target_pairs={{0,1},{1,0},{2,3},{3,2},{4,5},{5,4},{6,7},{7,6},{8,9},{9,8},{10,11... | collective-permute-start | bytes 393224 | tf_op jit(solution)/shard_map/ppermute | solution.py:48
  68.0 3.2 %collective-permute-start.20 = (bf16[512,128]{1,0:T(8,128)(2,1)S(1)}, bf16[512,128]{1,0:T(8,128)(2,1)S(1)}, u32[]{:S(2)}, u32[]{:S(2)}) collective-permute-start(bf16[512,128]{1,0:T(8,128)(2,1)S(1)} %get-tuple-element.85), channel_id=1, source_target_pairs={{0,6},{1,7},{2,0},{3,1},{4,2},{5,3},{6,4},{7,5},{8,14},{9,15},{10,... | collective-permute-start | bytes 393224 | tf_op jit(solution)/shard_map/ppermute | solution.py:48
  71.2 3.2 %collective-permute-start.25 = (bf16[512,128]{1,0:T(8,128)(2,1)S(1)}, bf16[512,128]{1,0:T(8,128)(2,1)S(1)}, u32[]{:S(2)}, u32[]{:S(2)}) collective-permute-start(bf16[512,128]{1,0:T(8,128)(2,1)S(1)} %get-tuple-element.89), channel_id=1, source_target_pairs={{0,6},{1,7},{2,0},{3,1},{4,2},{5,3},{6,4},{7,5},{8,14},{9,15},{10,... | collective-permute-start | bytes 393224 | tf_op jit(solution)/shard_map/ppermute | solution.py:48
  75.2 3.7 %collective-permute-done.24.refs_2_ = bf16[512,128]{1,0:T(8,128)(2,1)S(1)} collective-permute-done((bf16[512,128]{1,0:T(8,128)(2,1)S(1)}, bf16[512,128]{1,0:T(8,128)(2,1)S(1)}, u32[]{:S(2)}, u32[]{:S(2)}) %collective-permute-start.24) | collective-permute-done | bytes 131104 | tf_op jit(solution)/shard_map/ppermute | solution.py:48
  79.3 1.7 %collective-permute-done.23.refs_1_ = bf16[512,128]{1,0:T(8,128)(2,1)S(1)} collective-permute-done((bf16[512,128]{1,0:T(8,128)(2,1)S(1)}, bf16[512,128]{1,0:T(8,128)(2,1)S(1)}, u32[]{:S(2)}, u32[]{:S(2)}) %collective-permute-start.23) | collective-permute-done | bytes 131104 | tf_op jit(solution)/shard_map/ppermute | solution.py:48
  (51 shorter events, 4.9 us)
Async XLA Ops:
  0.0 11.6 %copy-start.3 = (bf16[1024,128]{1,0:T(8,128)(2,1)S(1)}, bf16[1024,128]{1,0:T(8,128)(2,1)}, u32[]{:S(2)}) copy-start(bf16[1024,128]{1,0:T(8,128)(2,1)} %wq_hbm.1) | copy-start | bytes 786436
  0.0 6.7 %collective-permute-start = (bf16[512,128]{1,0:T(8,128)(2,1)}, bf16[512,128]{1,0:T(8,128)(2,1)S(1)}, u32[]{:S(2)}, u32[]{:S(2)}) collective-permute-start(bf16[512,128]{1,0:T(8,128)(2,1)} %tokens_ref.1), channel_id=1, source_target_pairs={{0,1},{1,0},{2,3},{3,2},{4,5},{5,4},{6,7},{7,6},{8,9},{9,8},{10,11... | collective-permute-start | bytes 393224 | tf_op jit(solution)/shard_map/ppermute | solution.py:48
  2.2 7.8 %collective-permute-start.3 = (bf16[512,128]{1,0:T(8,128)(2,1)}, bf16[512,128]{1,0:T(8,128)(2,1)S(1)}, u32[]{:S(2)}, u32[]{:S(2)}) collective-permute-start(bf16[512,128]{1,0:T(8,128)(2,1)} %tokens_ref.1), channel_id=1, source_target_pairs={{0,4},{1,5},{2,6},{3,7},{4,0},{5,1},{6,2},{7,3},{8,12},{9,13},{10,... | collective-permute-start | bytes 393224 | tf_op jit(solution)/shard_map/ppermute | solution.py:48
  3.5 11.8 %collective-permute-start.1 = (bf16[512,128]{1,0:T(8,128)(2,1)}, bf16[512,128]{1,0:T(8,128)(2,1)S(1)}, u32[]{:S(2)}, u32[]{:S(2)}) collective-permute-start(bf16[512,128]{1,0:T(8,128)(2,1)} %tokens_ref.1), channel_id=1, source_target_pairs={{0,2},{1,3},{2,4},{3,5},{4,6},{5,7},{6,0},{7,1},{8,10},{9,11},{10,... | collective-permute-start | bytes 393224 | tf_op jit(solution)/shard_map/ppermute | solution.py:48
  4.1 11.2 %collective-permute-start.2 = (bf16[512,128]{1,0:T(8,128)(2,1)}, bf16[512,128]{1,0:T(8,128)(2,1)S(1)}, u32[]{:S(2)}, u32[]{:S(2)}) collective-permute-start(bf16[512,128]{1,0:T(8,128)(2,1)} %tokens_ref.1), channel_id=1, source_target_pairs={{0,6},{1,7},{2,0},{3,1},{4,2},{5,3},{6,4},{7,5},{8,14},{9,15},{10,... | collective-permute-start | bytes 393224 | tf_op jit(solution)/shard_map/ppermute | solution.py:48
  6.7 8.5 %collective-permute-start.4 = (bf16[512,128]{1,0:T(8,128)(2,1)S(1)}, bf16[512,128]{1,0:T(8,128)(2,1)S(1)}, u32[]{:S(2)}, u32[]{:S(2)}) collective-permute-start(bf16[512,128]{1,0:T(8,128)(2,1)S(1)} %collective-permute-done.refs_1_), channel_id=1, source_target_pairs={{0,2},{1,3},{2,4},{3,5},{4,6},{5,7},{6,0},{7,1},{8,10},{9,11},{10,... | collective-permute-start | bytes 393224 | tf_op jit(solution)/shard_map/ppermute | solution.py:48
  6.9 8.3 %collective-permute-start.5 = (bf16[512,128]{1,0:T(8,128)(2,1)S(1)}, bf16[512,128]{1,0:T(8,128)(2,1)S(1)}, u32[]{:S(2)}, u32[]{:S(2)}) collective-permute-start(bf16[512,128]{1,0:T(8,128)(2,1)S(1)} %collective-permute-done.refs_1_), channel_id=1, source_target_pairs={{0,6},{1,7},{2,0},{3,1},{4,2},{5,3},{6,4},{7,5},{8,14},{9,15},{10,... | collective-permute-start | bytes 393224 | tf_op jit(solution)/shard_map/ppermute | solution.py:48
  10.0 5.3 %collective-permute-start.6 = (bf16[512,128]{1,0:T(8,128)(2,1)S(1)}, bf16[512,128]{1,0:T(8,128)(2,1)S(1)}, u32[]{:S(2)}, u32[]{:S(2)}) collective-permute-start(bf16[512,128]{1,0:T(8,128)(2,1)S(1)} %collective-permute-done.3.refs_4_), channel_id=1, source_target_pairs={{0,1},{1,0},{2,3},{3,2},{4,5},{5,4},{6,7},{7,6},{8,9},{9,8},{10,11... | collective-permute-start | bytes 393224 | tf_op jit(solution)/shard_map/ppermute | solution.py:48
  12.2 0.9 %copy-start.4 = (bf16[1024,128]{1,0:T(8,128)(2,1)S(1)}, bf16[1024,128]{1,0:T(8,128)(2,1)}, u32[]{:S(2)}) copy-start(bf16[1024,128]{1,0:T(8,128)(2,1)} %wk_hbm.1) | copy-start | bytes 786436
  13.2 0.9 %copy-start.5 = (bf16[1024,128]{1,0:T(8,128)(2,1)S(1)}, bf16[1024,128]{1,0:T(8,128)(2,1)}, u32[]{:S(2)}) copy-start(bf16[1024,128]{1,0:T(8,128)(2,1)} %wv_hbm.1) | copy-start | bytes 786436
  14.1 1.1 %copy-start = (bf16[512,128]{1,0:T(8,128)(2,1)S(1)}, bf16[512,128]{1,0:T(8,128)(2,1)}, u32[]{:S(2)}) copy-start(bf16[512,128]{1,0:T(8,128)(2,1)} %tokens_ref.1) | copy-start | bytes 393220
  17.0 9.9 %copy-start.1 = (bf16[128,1024]{1,0:T(8,128)(2,1)S(1)}, bf16[128,1024]{1,0:T(8,128)(2,1)}, u32[]{:S(2)}) copy-start(bf16[128,1024]{1,0:T(8,128)(2,1)} %w_ref.1) | copy-start | bytes 786436
  17.0 1.5 %collective-permute-start.7 = (bf16[192,512]{1,0:T(8,128)(2,1)S(1)}, bf16[192,512]{1,0:T(8,128)(2,1)S(1)}, u32[]{:S(2)}, u32[]{:S(2)}) collective-permute-start(bf16[192,512]{1,0:T(8,128)(2,1)S(1)} %get-tuple-element.51), channel_id=1, source_target_pairs={{0,8},{8,0},{16,24},{24,16},{32,40},{40,32},{48,56},{56,48},{64,72... | collective-permute-start | bytes 589832 | tf_op jit(solution)/shard_map/ppermute | solution.py:34
  18.6 12.5 %collective-permute-start.9 = (bf16[128,1024]{1,0:T(8,128)(2,1)S(1)}, bf16[128,1024]{1,0:T(8,128)(2,1)S(1)}, u32[]{:S(2)}, u32[]{:S(2)}) collective-permute-start(bf16[128,1024]{1,0:T(8,128)(2,1)S(1)} %get-tuple-element.52.after_ref.refs_0_), channel_id=1, source_target_pairs={{0,16},{8,24},{16,32},{24,40},{32,48},{40,56},{48,64},{56,72},{64,... | collective-permute-start | bytes 786440 | tf_op jit(solution)/shard_map/ppermute | solution.py:34
  20.6 10.6 %collective-permute-start.8 = (bf16[128,1024]{1,0:T(8,128)(2,1)S(1)}, bf16[128,1024]{1,0:T(8,128)(2,1)S(1)}, u32[]{:S(2)}, u32[]{:S(2)}) collective-permute-start(bf16[128,1024]{1,0:T(8,128)(2,1)S(1)} %get-tuple-element.52.after_ref.refs_0_), channel_id=1, source_target_pairs={{0,112},{8,120},{16,0},{24,8},{32,16},{40,24},{48,32},{56,40},{64,... | collective-permute-start | bytes 786440 | tf_op jit(solution)/shard_map/ppermute | solution.py:34
  24.6 2.3 %copy-start.2 = (f32[128]{0:T(128)S(1)}, f32[128]{0:T(128)}, u32[]{:S(2)}) copy-start(f32[128]{0:T(128)} %param.15) | copy-start | bytes 1540
  24.6 9.8 %collective-permute-start.15 = (bf16[64,1024]{1,0:T(8,128)(2,1)S(1)}, bf16[64,1024]{1,0:T(8,128)(2,1)S(1)}, u32[]{:S(2)}, u32[]{:S(2)}) collective-permute-start(bf16[64,1024]{1,0:T(8,128)(2,1)S(1)} %get-tuple-element.54.refs_1_.refs_3_.refs_2_), channel_id=1, source_target_pairs={{0,128},{8,136},{16,144},{24,152},{32,160},{40,168},{48,176},{56,1... | collective-permute-start | bytes 393224 | tf_op jit(solution)/shard_map/ppermute | solution.py:34
  31.1 9.0 %collective-permute-start.10 = (bf16[128,1024]{1,0:T(8,128)(2,1)S(1)}, bf16[128,1024]{1,0:T(8,128)(2,1)S(1)}, u32[]{:S(2)}, u32[]{:S(2)}) collective-permute-start(bf16[128,1024]{1,0:T(8,128)(2,1)S(1)} %collective-permute-done.9.refs_1_), channel_id=1, source_target_pairs={{0,16},{8,24},{16,32},{24,40},{32,48},{40,56},{48,64},{56,72},{64,... | collective-permute-start | bytes 786440 | tf_op jit(solution)/shard_map/ppermute | solution.py:34
  31.1 9.0 %collective-permute-start.13 = (bf16[128,1024]{1,0:T(8,128)(2,1)S(1)}, bf16[128,1024]{1,0:T(8,128)(2,1)S(1)}, u32[]{:S(2)}, u32[]{:S(2)}) collective-permute-start(bf16[128,1024]{1,0:T(8,128)(2,1)S(1)} %collective-permute-done.8.refs_2_.refs_0_), channel_id=1, source_target_pairs={{0,112},{8,120},{16,0},{24,8},{32,16},{40,24},{48,32},{56,40},{64,... | collective-permute-start | bytes 786440 | tf_op jit(solution)/shard_map/ppermute | solution.py:34
  40.2 8.2 %collective-permute-start.11 = (bf16[128,1024]{1,0:T(8,128)(2,1)S(1)}, bf16[128,1024]{1,0:T(8,128)(2,1)S(1)}, u32[]{:S(2)}, u32[]{:S(2)}) collective-permute-start(bf16[128,1024]{1,0:T(8,128)(2,1)S(1)} %collective-permute-done.10.refs_0_), channel_id=1, source_target_pairs={{0,16},{8,24},{16,32},{24,40},{32,48},{40,56},{48,64},{56,72},{64,... | collective-permute-start | bytes 786440 | tf_op jit(solution)/shard_map/ppermute | solution.py:34
  40.2 8.3 %collective-permute-start.14 = (bf16[128,1024]{1,0:T(8,128)(2,1)S(1)}, bf16[128,1024]{1,0:T(8,128)(2,1)S(1)}, u32[]{:S(2)}, u32[]{:S(2)}) collective-permute-start(bf16[128,1024]{1,0:T(8,128)(2,1)S(1)} %collective-permute-done.13.refs_1_), channel_id=1, source_target_pairs={{0,112},{8,120},{16,0},{24,8},{32,16},{40,24},{48,32},{56,40},{64,... | collective-permute-start | bytes 786440 | tf_op jit(solution)/shard_map/ppermute | solution.py:34
  48.4 7.7 %collective-permute-start.12 = (bf16[128,1024]{1,0:T(8,128)(2,1)S(1)}, bf16[128,1024]{1,0:T(8,128)(2,1)S(1)}, u32[]{:S(2)}, u32[]{:S(2)}) collective-permute-start(bf16[128,1024]{1,0:T(8,128)(2,1)S(1)} %collective-permute-done.11.refs_0_), channel_id=1, source_target_pairs={{0,16},{8,24},{16,32},{24,40},{32,48},{40,56},{48,64},{56,72},{64,... | collective-permute-start | bytes 786440 | tf_op jit(solution)/shard_map/ppermute | solution.py:34
  57.8 6.9 %collective-permute-start.16 = (bf16[80,512]{1,0:T(8,128)(2,1)S(1)}, bf16[80,512]{1,0:T(8,128)(2,1)S(1)}, u32[]{:S(2)}, u32[]{:S(2)}) collective-permute-start(bf16[80,512]{1,0:T(8,128)(2,1)S(1)} %get-tuple-element.80), channel_id=1, source_target_pairs={{0,128},{8,136},{16,144},{24,152},{32,160},{40,168},{48,176},{56,1... | collective-permute-start | bytes 245768 | tf_op jit(solution)/shard_map/ppermute | solution.py:34
  60.2 5.4 %collective-permute-start.18 = (bf16[80,512]{1,0:T(8,128)(2,1)S(1)}, bf16[80,512]{1,0:T(8,128)(2,1)S(1)}, u32[]{:S(2)}, u32[]{:S(2)}) collective-permute-start(bf16[80,512]{1,0:T(8,128)(2,1)S(1)} %get-tuple-element.82), channel_id=1, source_target_pairs={{0,136},{8,128},{16,152},{24,144},{32,168},{40,160},{48,184},{56,1... | collective-permute-start | bytes 245768 | tf_op jit(solution)/shard_map/ppermute | solution.py:34
  63.3 2.4 %collective-permute-start.17 = (bf16[80,512]{1,0:T(8,128)(2,1)S(1)}, bf16[80,512]{1,0:T(8,128)(2,1)S(1)}, u32[]{:S(2)}, u32[]{:S(2)}) collective-permute-start(bf16[80,512]{1,0:T(8,128)(2,1)S(1)} %get-tuple-element.81), channel_id=1, source_target_pairs={{0,8},{8,0},{16,24},{24,16},{32,40},{40,32},{48,56},{56,48},{64,72... | collective-permute-start | bytes 245768 | tf_op jit(solution)/shard_map/ppermute | solution.py:34
  66.2 8.3 %collective-permute-start.22 = (bf16[512,128]{1,0:T(8,128)(2,1)S(1)}, bf16[512,128]{1,0:T(8,128)(2,1)S(1)}, u32[]{:S(2)}, u32[]{:S(2)}) collective-permute-start(bf16[512,128]{1,0:T(8,128)(2,1)S(1)} %get-tuple-element.87), channel_id=1, source_target_pairs={{0,1},{1,0},{2,3},{3,2},{4,5},{5,4},{6,7},{7,6},{8,9},{9,8},{10,11... | collective-permute-start | bytes 393224 | tf_op jit(solution)/shard_map/ppermute | solution.py:48
  68.0 6.6 %collective-permute-start.19 = (bf16[512,128]{1,0:T(8,128)(2,1)S(1)}, bf16[512,128]{1,0:T(8,128)(2,1)S(1)}, u32[]{:S(2)}, u32[]{:S(2)}) collective-permute-start(bf16[512,128]{1,0:T(8,128)(2,1)S(1)} %get-tuple-element.84), channel_id=1, source_target_pairs={{0,2},{1,3},{2,4},{3,5},{4,6},{5,7},{6,0},{7,1},{8,10},{9,11},{10,... | collective-permute-start | bytes 393224 | tf_op jit(solution)/shard_map/ppermute | solution.py:48
  68.0 6.6 %collective-permute-start.20 = (bf16[512,128]{1,0:T(8,128)(2,1)S(1)}, bf16[512,128]{1,0:T(8,128)(2,1)S(1)}, u32[]{:S(2)}, u32[]{:S(2)}) collective-permute-start(bf16[512,128]{1,0:T(8,128)(2,1)S(1)} %get-tuple-element.85), channel_id=1, source_target_pairs={{0,6},{1,7},{2,0},{3,1},{4,2},{5,3},{6,4},{7,5},{8,14},{9,15},{10,... | collective-permute-start | bytes 393224 | tf_op jit(solution)/shard_map/ppermute | solution.py:48
  71.2 7.6 %collective-permute-start.24 = (bf16[512,128]{1,0:T(8,128)(2,1)S(1)}, bf16[512,128]{1,0:T(8,128)(2,1)S(1)}, u32[]{:S(2)}, u32[]{:S(2)}) collective-permute-start(bf16[512,128]{1,0:T(8,128)(2,1)S(1)} %get-tuple-element.88), channel_id=1, source_target_pairs={{0,2},{1,3},{2,4},{3,5},{4,6},{5,7},{6,0},{7,1},{8,10},{9,11},{10,... | collective-permute-start | bytes 393224 | tf_op jit(solution)/shard_map/ppermute | solution.py:48
  71.2 8.1 %collective-permute-start.25 = (bf16[512,128]{1,0:T(8,128)(2,1)S(1)}, bf16[512,128]{1,0:T(8,128)(2,1)S(1)}, u32[]{:S(2)}, u32[]{:S(2)}) collective-permute-start(bf16[512,128]{1,0:T(8,128)(2,1)S(1)} %get-tuple-element.89), channel_id=1, source_target_pairs={{0,6},{1,7},{2,0},{3,1},{4,2},{5,3},{6,4},{7,5},{8,14},{9,15},{10,... | collective-permute-start | bytes 393224 | tf_op jit(solution)/shard_map/ppermute | solution.py:48
  74.5 6.6 %collective-permute-start.23 = (bf16[512,128]{1,0:T(8,128)(2,1)S(1)}, bf16[512,128]{1,0:T(8,128)(2,1)S(1)}, u32[]{:S(2)}, u32[]{:S(2)}) collective-permute-start(bf16[512,128]{1,0:T(8,128)(2,1)S(1)} %add.126), channel_id=1, source_target_pairs={{0,4},{1,5},{2,6},{3,7},{4,0},{5,1},{6,2},{7,3},{8,12},{9,13},{10,... | collective-permute-start | bytes 393224 | tf_op jit(solution)/shard_map/ppermute | solution.py:48
  74.7 6.4 %collective-permute-start.21 = (bf16[512,128]{1,0:T(8,128)(2,1)S(1)}, bf16[512,128]{1,0:T(8,128)(2,1)S(1)}, u32[]{:S(2)}, u32[]{:S(2)}) collective-permute-start(bf16[512,128]{1,0:T(8,128)(2,1)S(1)} %add.125), channel_id=1, source_target_pairs={{0,1},{1,0},{2,3},{3,2},{4,5},{5,4},{6,7},{7,6},{8,9},{9,8},{10,11... | collective-permute-start | bytes 393224 | tf_op jit(solution)/shard_map/ppermute | solution.py:48
  (2 other events, 1.4 us)

commit v3 on v2

--- a/solution.py
+++ b/solution.py
@@ -280,12 +280,13 @@
                 pack_ref[HEAD_DIM:PACK_ROWS, :] = rows.astype(jnp.bfloat16)
         return top, slot
 
-    if len(steps) % 2 == 0 and not pack:
+    if not pack:
 
         def body(i, top):
             here = pl.ds(pl.multiple_of(i * TILE, TILE), TILE)
             after = pl.ds(pl.multiple_of(lax.rem(i + 1, tiles) * TILE, TILE), TILE)
-            return one_tile(-1, here, after, top, 0)[0]
+            slot = 0 if len(steps) % 2 == 0 else lax.rem(i, 2)
+            return one_tile(-1, here, after, top, slot)[0]
 
         lax.fori_loop(0, tiles, body, score(steps[0], slice(0, TILE), 0))
     else:
@@ -445,21 +446,31 @@
     mine, theirs = None, None
     for step in range(4):
         near = (right, left)
+        if step == 2:
+            right, _ = lax.optimization_barrier((right, mine[0]))
+            left, _ = lax.optimization_barrier((left, mine[0]))
         right = send(right, 0, 1, 0)
         if step < 3:
             left = send(left, 0, -1, 0)
         if step == 0:
             partner = send(queries, 1, 0, 0)
             mine = attend([own], [queries], [None], ((0, (0,)),))
+        elif step == 1:
+            late = near[1]
+            both = attend(
+                [own, *near],
+                [queries, partner],
+                [mine, theirs],
+                ((1, (0, 1, 2)), (0, (1,))),
+                after=[w_last],
+            )
+            mine, theirs = both[:3], both[3:]
+        elif step == 2:
+            both = attend(near, [queries, partner], [mine, theirs], ((0, (0, 1)), (1, (0,))))
+            mine, theirs = both[:3], both[3:]
+            theirs = attend(near[1:], [partner], [theirs], ((0, (0,)),), after=[right])
         else:
-            if step == 1:
-                late = near[1]
-                blocks, work = (own, *near), ((1, (0, 1, 2)), (0, (1,)))
-            else:
-                blocks, work = near, ((0, (0, 1)), (1, (0, 1)))
-            both = attend(
-                blocks, [queries, partner], [mine, theirs], work, after=[w_last] if step == 1 else ()
-            )
+            both = attend(near, [queries, partner], [mine, theirs], ((0, (0, 1)), (1, (0, 1))))
             mine, theirs = both[:3], both[3:]
     for_mine, for_other = attend([right], [partner], [theirs], ((0, (0,)),), pack=(0, 1))
     from_partner = send(for_mine, 1, 0, 0)

time: 82 us -> 85.4 us (1.041)
  Pallas kernels: 26.3 us -> 33.3 us
  waiting for transfers between devices: 13.6 us -> 9.58 us
    pallas_call x6 -> x7, Pallas kernels: 21.5 us -> 28.5 us  [attend(): pl.pallas_call(functools.partial(attend_kernel, blocks=len(kv), sets=sets...]
    ppermute x12, waiting for transfers between devices: 7.63 us -> 3.72 us  [send(): return lax.ppermute(array, 'frames', frames_shift(dy, dz, dc))]
  transfers between devices with their start and end apart: 26 -> 26, of which waited for: 8 -> 7; matrix products, arithmetic and copies ran while one was open for 0% -> 0% of each run, Pallas kernels for 26% -> 33%
where the time goes in v3:
time: 85.4 us; the launch traced here: 85.2 us
  starting transfers between devices  39.5 us (46%)
  Pallas kernels  33.3 us (39%)
  waiting for transfers between devices  9.58 us (11%)
  local copies, waits for them, and re-layouts  2.6 us (3%)
    pallas_call x7, Pallas kernels, attend(): pl.pallas_call(functools.partial(attend_kernel, blocks=len(kv), sets=sets...  28.5 us
    ppermute x14, starting transfers between devices, send_heads(): return lax.ppermute(array, 'heads', heads_shift(*step))  20.5 us
    ppermute x12, starting transfers between devices, send(): return lax.ppermute(array, 'frames', frames_shift(dy, dz, dc))  19 us
    ppermute x14, waiting for transfers between devices, send_heads(): return lax.ppermute(array, 'heads', heads_shift(*step))  5.85 us
    ppermute x12, waiting for transfers between devices, send(): return lax.ppermute(array, 'frames', frames_shift(dy, dz, dc))  3.72 us
    unnamed x16, local copies, waits for them, and re-layouts  2.51 us
  transfers between devices with their start and end apart: 26, of which 7 were waited for; matrix products, arithmetic and copies ran while one was open for 0% of the time, Pallas kernels for 33%

profile of v3, /device:TPU:8, one launch (start us, length us, event | category | flops | bytes accessed | tf_op | source)
XLA Modules:
  0.0 85.2 jit_solution(6105927522363490460)
XLA Ops:
  0.0 2.2 %collective-permute-start = (bf16[512,128]{1,0:T(8,128)(2,1)}, bf16[512,128]{1,0:T(8,128)(2,1)S(1)}, u32[]{:S(2)}, u32[]{:S(2)}) collective-permute-start(bf16[512,128]{1,0:T(8,128)(2,1)} %tokens_ref.1), channel_id=1, source_target_pairs={{0,1},{1,0},{2,3},{3,2},{4,5},{5,4},{6,7},{7,6},{8,9},{9,8},{10,11... | collective-permute-start | bytes 393224 | tf_op jit(solution)/shard_map/ppermute | solution.py:48
  2.2 1.3 %collective-permute-start.3 = (bf16[512,128]{1,0:T(8,128)(2,1)}, bf16[512,128]{1,0:T(8,128)(2,1)S(1)}, u32[]{:S(2)}, u32[]{:S(2)}) collective-permute-start(bf16[512,128]{1,0:T(8,128)(2,1)} %tokens_ref.1), channel_id=1, source_target_pairs={{0,4},{1,5},{2,6},{3,7},{4,0},{5,1},{6,2},{7,3},{8,12},{9,13},{10,... | collective-permute-start | bytes 393224 | tf_op jit(solution)/shard_map/ppermute | solution.py:48
  4.1 2.6 %collective-permute-start.2 = (bf16[512,128]{1,0:T(8,128)(2,1)}, bf16[512,128]{1,0:T(8,128)(2,1)S(1)}, u32[]{:S(2)}, u32[]{:S(2)}) collective-permute-start(bf16[512,128]{1,0:T(8,128)(2,1)} %tokens_ref.1), channel_id=1, source_target_pairs={{0,6},{1,7},{2,0},{3,1},{4,2},{5,3},{6,4},{7,5},{8,14},{9,15},{10,... | collective-permute-start | bytes 393224 | tf_op jit(solution)/shard_map/ppermute | solution.py:48
  6.9 3.0 %collective-permute-start.5 = (bf16[512,128]{1,0:T(8,128)(2,1)S(1)}, bf16[512,128]{1,0:T(8,128)(2,1)S(1)}, u32[]{:S(2)}, u32[]{:S(2)}) collective-permute-start(bf16[512,128]{1,0:T(8,128)(2,1)S(1)} %collective-permute-done.refs_1_), channel_id=1, source_target_pairs={{0,6},{1,7},{2,0},{3,1},{4,2},{5,3},{6,4},{7,5},{8,14},{9,15},{10,... | collective-permute-start | bytes 393224 | tf_op jit(solution)/shard_map/ppermute | solution.py:48
  10.0 1.6 %collective-permute-start.6 = (bf16[512,128]{1,0:T(8,128)(2,1)S(1)}, bf16[512,128]{1,0:T(8,128)(2,1)S(1)}, u32[]{:S(2)}, u32[]{:S(2)}) collective-permute-start(bf16[512,128]{1,0:T(8,128)(2,1)S(1)} %collective-permute-done.3.refs_4_), channel_id=1, source_target_pairs={{0,1},{1,0},{2,3},{3,2},{4,5},{5,4},{6,7},{7,6},{8,9},{9,8},{10,11... | collective-permute-start | bytes 393224 | tf_op jit(solution)/shard_map/ppermute | solution.py:48
  12.2 0.9 %copy-done.4 = bf16[1024,128]{1,0:T(8,128)(2,1)S(1)} copy-done((bf16[1024,128]{1,0:T(8,128)(2,1)S(1)}, bf16[1024,128]{1,0:T(8,128)(2,1)}, u32[]{:S(2)}) %copy-start.4) | copy-done | bytes 262168
  13.2 0.9 %copy-done.5 = bf16[1024,128]{1,0:T(8,128)(2,1)S(1)} copy-done((bf16[1024,128]{1,0:T(8,128)(2,1)S(1)}, bf16[1024,128]{1,0:T(8,128)(2,1)}, u32[]{:S(2)}) %copy-start.5) | copy-done | bytes 262168
  14.1 1.1 %prepare.1 = (bf16[384,1024]{1,0:T(8,128)(2,1)S(1)}, f32[16,128]{1,0:T(8,128)S(1)}) custom-call(s32[17]{0:T(128)S(1)} %stack.65.place_ref, bf16[1024,128]{1,0:T(8,128)(2,1)S(1)} %copy-done.3, bf16[1024,128]{1,0:T(8,128)(2,1)S(1)} %copy-done.4, bf16[1024,128]{1,0:T(8,128)(2,1)S(1)} %copy-done.5, f32[8,128]{1,0:T(8,128)S(1)} %bitcast.19, f32[8,128]{1,0:T(8,128)S(1)} %bitcast.20), custom_call_target="tpu_custom_call" | custom-call | flops 402653184 | bytes 4194304 | tf_op jit(solution)/shard_map/prepare/pallas_call | solution.py:96
  15.3 1.7 %norm_project.1 = (bf16[192,512]{1,0:T(8,128)(2,1)S(1)}, bf16[192,512]{1,0:T(8,128)(2,1)S(1)}) custom-call(bf16[512,128]{1,0:T(8,128)(2,1)S(1)} %copy-done, bf16[512,128]{1,0:T(8,128)(2,1)S(1)} %collective-permute-done.refs_1_, bf16[512,128]{1,0:T(8,128)(2,1)S(1)} %collective-permute-done.1.refs_2_, bf16[512,128]{1,0:T(8,128)(2,1)S(1)} %collective-permute-done.2.refs_3_, ...), custom_call_target="tpu_custom_call" | custom-call | flops 402653184 | bytes 2097152 | tf_op jit(solution)/shard_map/norm_project/pallas_call | solution.py:177
  17.1 1.4 %collective-permute-done.7.taken = bf16[192,512]{1,0:T(8,128)(2,1)S(1)} collective-permute-done((bf16[192,512]{1,0:T(8,128)(2,1)S(1)}, bf16[192,512]{1,0:T(8,128)(2,1)S(1)}, u32[]{:S(2)}, u32[]{:S(2)}) %collective-permute-start.7) | collective-permute-done | bytes 196640 | tf_op jit(solution)/shard_map/ppermute | solution.py:34
  18.6 2.0 %collective-permute-start.9 = (bf16[128,1024]{1,0:T(8,128)(2,1)S(1)}, bf16[128,1024]{1,0:T(8,128)(2,1)S(1)}, u32[]{:S(2)}, u32[]{:S(2)}) collective-permute-start(bf16[128,1024]{1,0:T(8,128)(2,1)S(1)} %get-tuple-element.57.after_ref.refs_0_), channel_id=1, source_target_pairs={{0,16},{8,24},{16,32},{24,40},{32,48},{40,56},{48,64},{56,72},{64,... | collective-permute-start | bytes 786440 | tf_op jit(solution)/shard_map/ppermute | solution.py:34
  20.6 4.0 %collective-permute-start.8 = (bf16[128,1024]{1,0:T(8,128)(2,1)S(1)}, bf16[128,1024]{1,0:T(8,128)(2,1)S(1)}, u32[]{:S(2)}, u32[]{:S(2)}) collective-permute-start(bf16[128,1024]{1,0:T(8,128)(2,1)S(1)} %get-tuple-element.57.after_ref.refs_0_), channel_id=1, source_target_pairs={{0,112},{8,120},{16,0},{24,8},{32,16},{40,24},{48,32},{56,40},{64,... | collective-permute-start | bytes 786440 | tf_op jit(solution)/shard_map/ppermute | solution.py:34
  24.6 2.3 %collective-permute-start.11 = (bf16[64,1024]{1,0:T(8,128)(2,1)S(1)}, bf16[64,1024]{1,0:T(8,128)(2,1)S(1)}, u32[]{:S(2)}, u32[]{:S(2)}) collective-permute-start(bf16[64,1024]{1,0:T(8,128)(2,1)S(1)} %get-tuple-element.59.refs_1_.refs_3_.refs_2_), channel_id=1, source_target_pairs={{0,128},{8,136},{16,144},{24,152},{32,160},{40,168},{48,176},{56,1... | collective-permute-start | bytes 393224 | tf_op jit(solution)/shard_map/ppermute | solution.py:34
  27.5 3.1 %attend.7 = (f32[1,1024]{1,0:T(1,128)S(1)}, f32[1,1024]{1,0:T(1,128)S(1)}, f32[64,1024]{1,0:T(8,128)S(1)}) custom-call(bf16[128,1024]{1,0:T(8,128)(2,1)S(1)} %get-tuple-element.57.after_ref.refs_0_, bf16[64,1024]{1,0:T(8,128)(2,1)S(1)} %get-tuple-element.59.refs_1_.refs_3_.refs_2_), custom_call_target="tpu_custom_call" | custom-call | flops 1073741824 | bytes 1048576 | tf_op jit(solution)/shard_map/attend/pallas_call | solution.py:315
  31.1 3.2 %collective-permute-start.14 = (bf16[128,1024]{1,0:T(8,128)(2,1)S(1)}, bf16[128,1024]{1,0:T(8,128)(2,1)S(1)}, u32[]{:S(2)}, u32[]{:S(2)}) collective-permute-start(bf16[128,1024]{1,0:T(8,128)(2,1)S(1)} %collective-permute-done.8.refs_2_.refs_0_), channel_id=1, source_target_pairs={{0,112},{8,120},{16,0},{24,8},{32,16},{40,24},{48,32},{56,40},{64,... | collective-permute-start | bytes 786440 | tf_op jit(solution)/shard_map/ppermute | solution.py:34
  34.3 4.9 %attend.8 = (f32[1,1024]{1,0:T(1,128)S(1)}, f32[1,1024]{1,0:T(1,128)S(1)}, f32[64,1024]{1,0:T(8,128)S(1)}, f32[1,1024]{1,0:T(1,128)S(1)}, f32[1,1024]{1,0:T(1,128)S(1)}, /*index=5*/f32[64,1024]{1,0:T(8,128)S(1)}) custom-call(bf16[128,1024]{1,0:T(8,128)(2,1)S(1)} %get-tuple-element.57.after_ref.refs_0_, bf16[128,1024]{1,0:T(8,128)(2,1)S(1)} %collective-permute-done.9.refs_1_, ...), custom_call_target="tpu_custom_call" | custom-call | flops 4294967296 | bytes 1048576 | tf_op jit(solution)/shard_map/attend/pallas_call | solution.py:315
  39.3 0.9 %collective-permute-done.10.refs_0_ = bf16[128,1024]{1,0:T(8,128)(2,1)S(1)} collective-permute-done((bf16[128,1024]{1,0:T(8,128)(2,1)S(1)}, bf16[128,1024]{1,0:T(8,128)(2,1)S(1)}, u32[]{:S(2)}, u32[]{:S(2)}) %collective-permute-start.10) | collective-permute-done | bytes 262176 | tf_op jit(solution)/shard_map/ppermute | solution.py:34
  40.2 3.2 %collective-permute-start.15 = (bf16[128,1024]{1,0:T(8,128)(2,1)S(1)}, bf16[128,1024]{1,0:T(8,128)(2,1)S(1)}, u32[]{:S(2)}, u32[]{:S(2)}) collective-permute-start(bf16[128,1024]{1,0:T(8,128)(2,1)S(1)} %collective-permute-done.14.refs_1_.refs_0_), channel_id=1, source_target_pairs={{0,112},{8,120},{16,0},{24,8},{32,16},{40,24},{48,32},{56,40},{64,... | collective-permute-start | bytes 786440 | tf_op jit(solution)/shard_map/ppermute | solution.py:34
  43.4 7.5 %attend.9 = (f32[1,1024]{1,0:T(1,128)S(1)}, f32[1,1024]{1,0:T(1,128)S(1)}, f32[64,1024]{1,0:T(8,128)S(1)}, f32[1,1024]{1,0:T(1,128)S(1)}, f32[1,1024]{1,0:T(1,128)S(1)}, /*index=5*/f32[64,1024]{1,0:T(8,128)S(1)}) custom-call(bf16[128,1024]{1,0:T(8,128)(2,1)S(1)} %collective-permute-done.10.refs_0_, ...), custom_call_target="tpu_custom_call" | custom-call | flops 3221225472 | bytes 1048576 | tf_op jit(solution)/shard_map/attend/pallas_call | solution.py:315
  51.2 3.2 %attend.10 = (f32[1,1024]{1,0:T(1,128)S(1)}, f32[1,1024]{1,0:T(1,128)S(1)}, f32[64,1024]{1,0:T(8,128)S(1)}) custom-call(bf16[128,1024]{1,0:T(8,128)(2,1)S(1)} %collective-permute-done.14.refs_1_.refs_0_, bf16[64,1024]{1,0:T(8,128)(2,1)S(1)} %collective-permute-done.11.refs_4_.refs_3_.refs_1_, f32[1,1024]{1,0:T(1,128)S(1)} %get-tuple-element.75.refs_2_, ...), custom_call_target="tpu_custom_call" | custom-call | flops 1073741824 | bytes 1048576 | tf_op jit(solution)/shard_map/attend/pallas_call | solution.py:315
  54.4 5.0 %attend.11 = (f32[1,1024]{1,0:T(1,128)S(1)}, f32[1,1024]{1,0:T(1,128)S(1)}, f32[64,1024]{1,0:T(8,128)S(1)}, f32[1,1024]{1,0:T(1,128)S(1)}, f32[1,1024]{1,0:T(1,128)S(1)}, /*index=5*/f32[64,1024]{1,0:T(8,128)S(1)}) custom-call(bf16[128,1024]{1,0:T(8,128)(2,1)S(1)} %collective-permute-done.12.refs_5_.refs_0_, ...), custom_call_target="tpu_custom_call" | custom-call | flops 4294967296 | bytes 1048576 | tf_op jit(solution)/shard_map/attend/pallas_call | solution.py:315
  59.4 1.8 %attend.13 = (bf16[80,512]{1,0:T(8,128)(2,1)S(1)}, bf16[80,512]{1,0:T(8,128)(2,1)S(1)}) custom-call(bf16[128,1024]{1,0:T(8,128)(2,1)S(1)} %collective-permute-done.13.refs_1_.refs_0_, bf16[64,1024]{1,0:T(8,128)(2,1)S(1)} %collective-permute-done.11.refs_4_.refs_3_.refs_1_, f32[1,1024]{1,0:T(1,128)S(1)} %get-tuple-element.87.refs_2_, ...), custom_call_target="tpu_custom_call" | custom-call | flops 1073741824 | bytes 1048576 | tf_op jit(solution)/shard_map/attend/pallas_call | solution.py:315
  61.2 2.4 %collective-permute-start.16 = (bf16[80,512]{1,0:T(8,128)(2,1)S(1)}, bf16[80,512]{1,0:T(8,128)(2,1)S(1)}, u32[]{:S(2)}, u32[]{:S(2)}) collective-permute-start(bf16[80,512]{1,0:T(8,128)(2,1)S(1)} %get-tuple-element.90), channel_id=1, source_target_pairs={{0,128},{8,136},{16,144},{24,152},{32,160},{40,168},{48,176},{56,1... | collective-permute-start | bytes 245768 | tf_op jit(solution)/shard_map/ppermute | solution.py:34
  63.6 3.1 %attend.12 = (bf16[80,512]{1,0:T(8,128)(2,1)S(1)}, f32[1,512]{1,0:T(1,128)S(1)}, f32[1,512]{1,0:T(1,128)S(1)}, f32[64,512]{1,0:T(8,128)S(1)}) custom-call(bf16[128,1024]{1,0:T(8,128)(2,1)S(1)} %collective-permute-done.8.refs_2_.refs_0_, bf16[128,1024]{1,0:T(8,128)(2,1)S(1)} %collective-permute-done.13.refs_1_.refs_0_, ...), custom_call_target="tpu_custom_call" | custom-call | flops 2147483648 | bytes 1048576 | tf_op jit(solution)/shard_map/attend/pallas_call | solution.py:315
  66.7 1.4 %collective-permute-start.17 = (bf16[80,512]{1,0:T(8,128)(2,1)S(1)}, bf16[80,512]{1,0:T(8,128)(2,1)S(1)}, u32[]{:S(2)}, u32[]{:S(2)}) collective-permute-start(bf16[80,512]{1,0:T(8,128)(2,1)S(1)} %get-tuple-element.91), channel_id=1, source_target_pairs={{0,8},{8,0},{16,24},{24,16},{32,40},{40,32},{48,56},{56,48},{64,72... | collective-permute-start | bytes 245768 | tf_op jit(solution)/shard_map/ppermute | solution.py:34
  68.1 0.9 %collective-permute-done.18.diagonal_ref = bf16[80,512]{1,0:T(8,128)(2,1)S(1)} collective-permute-done((bf16[80,512]{1,0:T(8,128)(2,1)S(1)}, bf16[80,512]{1,0:T(8,128)(2,1)S(1)}, u32[]{:S(2)}, u32[]{:S(2)}) %collective-permute-start.18) | collective-permute-done | bytes 81952 | tf_op jit(solution)/shard_map/ppermute | solution.py:34
  69.5 1.9 %collective-permute-start.22 = (bf16[512,128]{1,0:T(8,128)(2,1)S(1)}, bf16[512,128]{1,0:T(8,128)(2,1)S(1)}, u32[]{:S(2)}, u32[]{:S(2)}) collective-permute-start(bf16[512,128]{1,0:T(8,128)(2,1)S(1)} %get-tuple-element.97), channel_id=1, source_target_pairs={{0,1},{1,0},{2,3},{3,2},{4,5},{5,4},{6,7},{7,6},{8,9},{9,8},{10,11... | collective-permute-start | bytes 393224 | tf_op jit(solution)/shard_map/ppermute | solution.py:48
  71.4 3.2 %collective-permute-start.20 = (bf16[512,128]{1,0:T(8,128)(2,1)S(1)}, bf16[512,128]{1,0:T(8,128)(2,1)S(1)}, u32[]{:S(2)}, u32[]{:S(2)}) collective-permute-start(bf16[512,128]{1,0:T(8,128)(2,1)S(1)} %get-tuple-element.95), channel_id=1, source_target_pairs={{0,6},{1,7},{2,0},{3,1},{4,2},{5,3},{6,4},{7,5},{8,14},{9,15},{10,... | collective-permute-start | bytes 393224 | tf_op jit(solution)/shard_map/ppermute | solution.py:48
  74.6 3.2 %collective-permute-start.25 = (bf16[512,128]{1,0:T(8,128)(2,1)S(1)}, bf16[512,128]{1,0:T(8,128)(2,1)S(1)}, u32[]{:S(2)}, u32[]{:S(2)}) collective-permute-start(bf16[512,128]{1,0:T(8,128)(2,1)S(1)} %get-tuple-element.99), channel_id=1, source_target_pairs={{0,6},{1,7},{2,0},{3,1},{4,2},{5,3},{6,4},{7,5},{8,14},{9,15},{10,... | collective-permute-start | bytes 393224 | tf_op jit(solution)/shard_map/ppermute | solution.py:48
  78.6 3.6 %collective-permute-done.24.refs_2_ = bf16[512,128]{1,0:T(8,128)(2,1)S(1)} collective-permute-done((bf16[512,128]{1,0:T(8,128)(2,1)S(1)}, bf16[512,128]{1,0:T(8,128)(2,1)S(1)}, u32[]{:S(2)}, u32[]{:S(2)}) %collective-permute-start.24) | collective-permute-done | bytes 131104 | tf_op jit(solution)/shard_map/ppermute | solution.py:48
  82.7 1.7 %collective-permute-done.23.refs_1_ = bf16[512,128]{1,0:T(8,128)(2,1)S(1)} collective-permute-done((bf16[512,128]{1,0:T(8,128)(2,1)S(1)}, bf16[512,128]{1,0:T(8,128)(2,1)S(1)}, u32[]{:S(2)}, u32[]{:S(2)}) %collective-permute-start.23) | collective-permute-done | bytes 131104 | tf_op jit(solution)/shard_map/ppermute | solution.py:48
  84.5 0.8 finish.1
  (52 shorter events, 4.9 us)
Async XLA Ops:
  0.0 11.6 %copy-start.3 = (bf16[1024,128]{1,0:T(8,128)(2,1)S(1)}, bf16[1024,128]{1,0:T(8,128)(2,1)}, u32[]{:S(2)}) copy-start(bf16[1024,128]{1,0:T(8,128)(2,1)} %wq_hbm.1) | copy-start | bytes 786436
  0.0 6.7 %collective-permute-start = (bf16[512,128]{1,0:T(8,128)(2,1)}, bf16[512,128]{1,0:T(8,128)(2,1)S(1)}, u32[]{:S(2)}, u32[]{:S(2)}) collective-permute-start(bf16[512,128]{1,0:T(8,128)(2,1)} %tokens_ref.1), channel_id=1, source_target_pairs={{0,1},{1,0},{2,3},{3,2},{4,5},{5,4},{6,7},{7,6},{8,9},{9,8},{10,11... | collective-permute-start | bytes 393224 | tf_op jit(solution)/shard_map/ppermute | solution.py:48
  2.2 7.8 %collective-permute-start.3 = (bf16[512,128]{1,0:T(8,128)(2,1)}, bf16[512,128]{1,0:T(8,128)(2,1)S(1)}, u32[]{:S(2)}, u32[]{:S(2)}) collective-permute-start(bf16[512,128]{1,0:T(8,128)(2,1)} %tokens_ref.1), channel_id=1, source_target_pairs={{0,4},{1,5},{2,6},{3,7},{4,0},{5,1},{6,2},{7,3},{8,12},{9,13},{10,... | collective-permute-start | bytes 393224 | tf_op jit(solution)/shard_map/ppermute | solution.py:48
  3.5 11.8 %collective-permute-start.1 = (bf16[512,128]{1,0:T(8,128)(2,1)}, bf16[512,128]{1,0:T(8,128)(2,1)S(1)}, u32[]{:S(2)}, u32[]{:S(2)}) collective-permute-start(bf16[512,128]{1,0:T(8,128)(2,1)} %tokens_ref.1), channel_id=1, source_target_pairs={{0,2},{1,3},{2,4},{3,5},{4,6},{5,7},{6,0},{7,1},{8,10},{9,11},{10,... | collective-permute-start | bytes 393224 | tf_op jit(solution)/shard_map/ppermute | solution.py:48
  4.1 11.2 %collective-permute-start.2 = (bf16[512,128]{1,0:T(8,128)(2,1)}, bf16[512,128]{1,0:T(8,128)(2,1)S(1)}, u32[]{:S(2)}, u32[]{:S(2)}) collective-permute-start(bf16[512,128]{1,0:T(8,128)(2,1)} %tokens_ref.1), channel_id=1, source_target_pairs={{0,6},{1,7},{2,0},{3,1},{4,2},{5,3},{6,4},{7,5},{8,14},{9,15},{10,... | collective-permute-start | bytes 393224 | tf_op jit(solution)/shard_map/ppermute | solution.py:48
  6.7 8.5 %collective-permute-start.4 = (bf16[512,128]{1,0:T(8,128)(2,1)S(1)}, bf16[512,128]{1,0:T(8,128)(2,1)S(1)}, u32[]{:S(2)}, u32[]{:S(2)}) collective-permute-start(bf16[512,128]{1,0:T(8,128)(2,1)S(1)} %collective-permute-done.refs_1_), channel_id=1, source_target_pairs={{0,2},{1,3},{2,4},{3,5},{4,6},{5,7},{6,0},{7,1},{8,10},{9,11},{10,... | collective-permute-start | bytes 393224 | tf_op jit(solution)/shard_map/ppermute | solution.py:48
  6.9 8.3 %collective-permute-start.5 = (bf16[512,128]{1,0:T(8,128)(2,1)S(1)}, bf16[512,128]{1,0:T(8,128)(2,1)S(1)}, u32[]{:S(2)}, u32[]{:S(2)}) collective-permute-start(bf16[512,128]{1,0:T(8,128)(2,1)S(1)} %collective-permute-done.refs_1_), channel_id=1, source_target_pairs={{0,6},{1,7},{2,0},{3,1},{4,2},{5,3},{6,4},{7,5},{8,14},{9,15},{10,... | collective-permute-start | bytes 393224 | tf_op jit(solution)/shard_map/ppermute | solution.py:48
  10.0 5.3 %collective-permute-start.6 = (bf16[512,128]{1,0:T(8,128)(2,1)S(1)}, bf16[512,128]{1,0:T(8,128)(2,1)S(1)}, u32[]{:S(2)}, u32[]{:S(2)}) collective-permute-start(bf16[512,128]{1,0:T(8,128)(2,1)S(1)} %collective-permute-done.3.refs_4_), channel_id=1, source_target_pairs={{0,1},{1,0},{2,3},{3,2},{4,5},{5,4},{6,7},{7,6},{8,9},{9,8},{10,11... | collective-permute-start | bytes 393224 | tf_op jit(solution)/shard_map/ppermute | solution.py:48
  12.2 0.9 %copy-start.4 = (bf16[1024,128]{1,0:T(8,128)(2,1)S(1)}, bf16[1024,128]{1,0:T(8,128)(2,1)}, u32[]{:S(2)}) copy-start(bf16[1024,128]{1,0:T(8,128)(2,1)} %wk_hbm.1) | copy-start | bytes 786436
  13.2 0.9 %copy-start.5 = (bf16[1024,128]{1,0:T(8,128)(2,1)S(1)}, bf16[1024,128]{1,0:T(8,128)(2,1)}, u32[]{:S(2)}) copy-start(bf16[1024,128]{1,0:T(8,128)(2,1)} %wv_hbm.1) | copy-start | bytes 786436
  14.1 1.1 %copy-start = (bf16[512,128]{1,0:T(8,128)(2,1)S(1)}, bf16[512,128]{1,0:T(8,128)(2,1)}, u32[]{:S(2)}) copy-start(bf16[512,128]{1,0:T(8,128)(2,1)} %tokens_ref.1) | copy-start | bytes 393220
  17.0 9.9 %copy-start.1 = (bf16[128,1024]{1,0:T(8,128)(2,1)S(1)}, bf16[128,1024]{1,0:T(8,128)(2,1)}, u32[]{:S(2)}) copy-start(bf16[128,1024]{1,0:T(8,128)(2,1)} %w_ref.1) | copy-start | bytes 786436
  17.0 1.5 %collective-permute-start.7 = (bf16[192,512]{1,0:T(8,128)(2,1)S(1)}, bf16[192,512]{1,0:T(8,128)(2,1)S(1)}, u32[]{:S(2)}, u32[]{:S(2)}) collective-permute-start(bf16[192,512]{1,0:T(8,128)(2,1)S(1)} %get-tuple-element.56), channel_id=1, source_target_pairs={{0,8},{8,0},{16,24},{24,16},{32,40},{40,32},{48,56},{56,48},{64,72... | collective-permute-start | bytes 589832 | tf_op jit(solution)/shard_map/ppermute | solution.py:34
  18.6 12.5 %collective-permute-start.9 = (bf16[128,1024]{1,0:T(8,128)(2,1)S(1)}, bf16[128,1024]{1,0:T(8,128)(2,1)S(1)}, u32[]{:S(2)}, u32[]{:S(2)}) collective-permute-start(bf16[128,1024]{1,0:T(8,128)(2,1)S(1)} %get-tuple-element.57.after_ref.refs_0_), channel_id=1, source_target_pairs={{0,16},{8,24},{16,32},{24,40},{32,48},{40,56},{48,64},{56,72},{64,... | collective-permute-start | bytes 786440 | tf_op jit(solution)/shard_map/ppermute | solution.py:34
  20.6 10.6 %collective-permute-start.8 = (bf16[128,1024]{1,0:T(8,128)(2,1)S(1)}, bf16[128,1024]{1,0:T(8,128)(2,1)S(1)}, u32[]{:S(2)}, u32[]{:S(2)}) collective-permute-start(bf16[128,1024]{1,0:T(8,128)(2,1)S(1)} %get-tuple-element.57.after_ref.refs_0_), channel_id=1, source_target_pairs={{0,112},{8,120},{16,0},{24,8},{32,16},{40,24},{48,32},{56,40},{64,... | collective-permute-start | bytes 786440 | tf_op jit(solution)/shard_map/ppermute | solution.py:34
  24.6 2.3 %copy-start.2 = (f32[128]{0:T(128)S(1)}, f32[128]{0:T(128)}, u32[]{:S(2)}) copy-start(f32[128]{0:T(128)} %param.15) | copy-start | bytes 1540
  24.6 9.8 %collective-permute-start.11 = (bf16[64,1024]{1,0:T(8,128)(2,1)S(1)}, bf16[64,1024]{1,0:T(8,128)(2,1)S(1)}, u32[]{:S(2)}, u32[]{:S(2)}) collective-permute-start(bf16[64,1024]{1,0:T(8,128)(2,1)S(1)} %get-tuple-element.59.refs_1_.refs_3_.refs_2_), channel_id=1, source_target_pairs={{0,128},{8,136},{16,144},{24,152},{32,160},{40,168},{48,176},{56,1... | collective-permute-start | bytes 393224 | tf_op jit(solution)/shard_map/ppermute | solution.py:34
  31.1 9.0 %collective-permute-start.10 = (bf16[128,1024]{1,0:T(8,128)(2,1)S(1)}, bf16[128,1024]{1,0:T(8,128)(2,1)S(1)}, u32[]{:S(2)}, u32[]{:S(2)}) collective-permute-start(bf16[128,1024]{1,0:T(8,128)(2,1)S(1)} %collective-permute-done.9.refs_1_), channel_id=1, source_target_pairs={{0,16},{8,24},{16,32},{24,40},{32,48},{40,56},{48,64},{56,72},{64,... | collective-permute-start | bytes 786440 | tf_op jit(solution)/shard_map/ppermute | solution.py:34
  31.1 9.0 %collective-permute-start.14 = (bf16[128,1024]{1,0:T(8,128)(2,1)S(1)}, bf16[128,1024]{1,0:T(8,128)(2,1)S(1)}, u32[]{:S(2)}, u32[]{:S(2)}) collective-permute-start(bf16[128,1024]{1,0:T(8,128)(2,1)S(1)} %collective-permute-done.8.refs_2_.refs_0_), channel_id=1, source_target_pairs={{0,112},{8,120},{16,0},{24,8},{32,16},{40,24},{48,32},{56,40},{64,... | collective-permute-start | bytes 786440 | tf_op jit(solution)/shard_map/ppermute | solution.py:34
  40.2 10.8 %collective-permute-start.12 = (bf16[128,1024]{1,0:T(8,128)(2,1)S(1)}, bf16[128,1024]{1,0:T(8,128)(2,1)S(1)}, u32[]{:S(2)}, u32[]{:S(2)}) collective-permute-start(bf16[128,1024]{1,0:T(8,128)(2,1)S(1)} %collective-permute-done.10.refs_0_), channel_id=1, source_target_pairs={{0,16},{8,24},{16,32},{24,40},{32,48},{40,56},{48,64},{56,72},{64,... | collective-permute-start | bytes 786440 | tf_op jit(solution)/shard_map/ppermute | solution.py:34
  40.2 14.2 %collective-permute-start.15 = (bf16[128,1024]{1,0:T(8,128)(2,1)S(1)}, bf16[128,1024]{1,0:T(8,128)(2,1)S(1)}, u32[]{:S(2)}, u32[]{:S(2)}) collective-permute-start(bf16[128,1024]{1,0:T(8,128)(2,1)S(1)} %collective-permute-done.14.refs_1_.refs_0_), channel_id=1, source_target_pairs={{0,112},{8,120},{16,0},{24,8},{32,16},{40,24},{48,32},{56,40},{64,... | collective-permute-start | bytes 786440 | tf_op jit(solution)/shard_map/ppermute | solution.py:34
  50.9 8.5 %collective-permute-start.13 = (bf16[128,1024]{1,0:T(8,128)(2,1)S(1)}, bf16[128,1024]{1,0:T(8,128)(2,1)S(1)}, u32[]{:S(2)}, u32[]{:S(2)}) collective-permute-start(bf16[128,1024]{1,0:T(8,128)(2,1)S(1)} %collective-permute-done.12.refs_5_.refs_0_), channel_id=1, source_target_pairs={{0,16},{8,24},{16,32},{24,40},{32,48},{40,56},{48,64},{56,72},{64,... | collective-permute-start | bytes 786440 | tf_op jit(solution)/shard_map/ppermute | solution.py:34
  61.2 6.9 %collective-permute-start.16 = (bf16[80,512]{1,0:T(8,128)(2,1)S(1)}, bf16[80,512]{1,0:T(8,128)(2,1)S(1)}, u32[]{:S(2)}, u32[]{:S(2)}) collective-permute-start(bf16[80,512]{1,0:T(8,128)(2,1)S(1)} %get-tuple-element.90), channel_id=1, source_target_pairs={{0,128},{8,136},{16,144},{24,152},{32,160},{40,168},{48,176},{56,1... | collective-permute-start | bytes 245768 | tf_op jit(solution)/shard_map/ppermute | solution.py:34
  63.6 5.4 %collective-permute-start.18 = (bf16[80,512]{1,0:T(8,128)(2,1)S(1)}, bf16[80,512]{1,0:T(8,128)(2,1)S(1)}, u32[]{:S(2)}, u32[]{:S(2)}) collective-permute-start(bf16[80,512]{1,0:T(8,128)(2,1)S(1)} %get-tuple-element.92), channel_id=1, source_target_pairs={{0,136},{8,128},{16,152},{24,144},{32,168},{40,160},{48,184},{56,1... | collective-permute-start | bytes 245768 | tf_op jit(solution)/shard_map/ppermute | solution.py:34
  66.7 2.3 %collective-permute-start.17 = (bf16[80,512]{1,0:T(8,128)(2,1)S(1)}, bf16[80,512]{1,0:T(8,128)(2,1)S(1)}, u32[]{:S(2)}, u32[]{:S(2)}) collective-permute-start(bf16[80,512]{1,0:T(8,128)(2,1)S(1)} %get-tuple-element.91), channel_id=1, source_target_pairs={{0,8},{8,0},{16,24},{24,16},{32,40},{40,32},{48,56},{56,48},{64,72... | collective-permute-start | bytes 245768 | tf_op jit(solution)/shard_map/ppermute | solution.py:34
  69.5 8.4 %collective-permute-start.22 = (bf16[512,128]{1,0:T(8,128)(2,1)S(1)}, bf16[512,128]{1,0:T(8,128)(2,1)S(1)}, u32[]{:S(2)}, u32[]{:S(2)}) collective-permute-start(bf16[512,128]{1,0:T(8,128)(2,1)S(1)} %get-tuple-element.97), channel_id=1, source_target_pairs={{0,1},{1,0},{2,3},{3,2},{4,5},{5,4},{6,7},{7,6},{8,9},{9,8},{10,11... | collective-permute-start | bytes 393224 | tf_op jit(solution)/shard_map/ppermute | solution.py:48
  71.4 6.6 %collective-permute-start.19 = (bf16[512,128]{1,0:T(8,128)(2,1)S(1)}, bf16[512,128]{1,0:T(8,128)(2,1)S(1)}, u32[]{:S(2)}, u32[]{:S(2)}) collective-permute-start(bf16[512,128]{1,0:T(8,128)(2,1)S(1)} %get-tuple-element.94), channel_id=1, source_target_pairs={{0,2},{1,3},{2,4},{3,5},{4,6},{5,7},{6,0},{7,1},{8,10},{9,11},{10,... | collective-permute-start | bytes 393224 | tf_op jit(solution)/shard_map/ppermute | solution.py:48
  71.4 6.6 %collective-permute-start.20 = (bf16[512,128]{1,0:T(8,128)(2,1)S(1)}, bf16[512,128]{1,0:T(8,128)(2,1)S(1)}, u32[]{:S(2)}, u32[]{:S(2)}) collective-permute-start(bf16[512,128]{1,0:T(8,128)(2,1)S(1)} %get-tuple-element.95), channel_id=1, source_target_pairs={{0,6},{1,7},{2,0},{3,1},{4,2},{5,3},{6,4},{7,5},{8,14},{9,15},{10,... | collective-permute-start | bytes 393224 | tf_op jit(solution)/shard_map/ppermute | solution.py:48
  74.6 7.6 %collective-permute-start.24 = (bf16[512,128]{1,0:T(8,128)(2,1)S(1)}, bf16[512,128]{1,0:T(8,128)(2,1)S(1)}, u32[]{:S(2)}, u32[]{:S(2)}) collective-permute-start(bf16[512,128]{1,0:T(8,128)(2,1)S(1)} %get-tuple-element.98), channel_id=1, source_target_pairs={{0,2},{1,3},{2,4},{3,5},{4,6},{5,7},{6,0},{7,1},{8,10},{9,11},{10,... | collective-permute-start | bytes 393224 | tf_op jit(solution)/shard_map/ppermute | solution.py:48
  74.6 8.1 %collective-permute-start.25 = (bf16[512,128]{1,0:T(8,128)(2,1)S(1)}, bf16[512,128]{1,0:T(8,128)(2,1)S(1)}, u32[]{:S(2)}, u32[]{:S(2)}) collective-permute-start(bf16[512,128]{1,0:T(8,128)(2,1)S(1)} %get-tuple-element.99), channel_id=1, source_target_pairs={{0,6},{1,7},{2,0},{3,1},{4,2},{5,3},{6,4},{7,5},{8,14},{9,15},{10,... | collective-permute-start | bytes 393224 | tf_op jit(solution)/shard_map/ppermute | solution.py:48
  77.9 6.6 %collective-permute-start.23 = (bf16[512,128]{1,0:T(8,128)(2,1)S(1)}, bf16[512,128]{1,0:T(8,128)(2,1)S(1)}, u32[]{:S(2)}, u32[]{:S(2)}) collective-permute-start(bf16[512,128]{1,0:T(8,128)(2,1)S(1)} %add.126), channel_id=1, source_target_pairs={{0,4},{1,5},{2,6},{3,7},{4,0},{5,1},{6,2},{7,3},{8,12},{9,13},{10,... | collective-permute-start | bytes 393224 | tf_op jit(solution)/shard_map/ppermute | solution.py:48
  78.1 6.4 %collective-permute-start.21 = (bf16[512,128]{1,0:T(8,128)(2,1)S(1)}, bf16[512,128]{1,0:T(8,128)(2,1)S(1)}, u32[]{:S(2)}, u32[]{:S(2)}) collective-permute-start(bf16[512,128]{1,0:T(8,128)(2,1)S(1)} %add.125), channel_id=1, source_target_pairs={{0,1},{1,0},{2,3},{3,2},{4,5},{5,4},{6,7},{7,6},{8,9},{9,8},{10,11... | collective-permute-start | bytes 393224 | tf_op jit(solution)/shard_map/ppermute | solution.py:48
  (2 other events, 1.4 us)

commit v4 on v3

--- a/solution.py
+++ b/solution.py
@@ -280,13 +280,12 @@
                 pack_ref[HEAD_DIM:PACK_ROWS, :] = rows.astype(jnp.bfloat16)
         return top, slot
 
-    if not pack:
+    if len(steps) % 2 == 0 and not pack:
 
         def body(i, top):
             here = pl.ds(pl.multiple_of(i * TILE, TILE), TILE)
             after = pl.ds(pl.multiple_of(lax.rem(i + 1, tiles) * TILE, TILE), TILE)
-            slot = 0 if len(steps) % 2 == 0 else lax.rem(i, 2)
-            return one_tile(-1, here, after, top, slot)[0]
+            return one_tile(-1, here, after, top, 0)[0]
 
         lax.fori_loop(0, tiles, body, score(steps[0], slice(0, TILE), 0))
     else:

time: 85.4 us -> 81.9 us (0.959)
  Pallas kernels: 33.3 us -> 27.3 us
  waiting for transfers between devices: 9.58 us -> 12.5 us
    pallas_call x7, Pallas kernels: 28.5 us -> 22.5 us  [attend(): pl.pallas_call(functools.partial(attend_kernel, blocks=len(kv), sets=sets...]
    ppermute x12, waiting for transfers between devices: 3.72 us -> 6.58 us  [send(): return lax.ppermute(array, 'frames', frames_shift(dy, dz, dc))]
  transfers between devices with their start and end apart: 26 -> 26, of which waited for: 7 -> 9; matrix products, arithmetic and copies ran while one was open for 0% -> 0% of each run, Pallas kernels for 33% -> 28%
where the time goes in v4:
time: 81.9 us; the launch traced here: 81.7 us
  starting transfers between devices  39.1 us (48%)
  Pallas kernels  27.3 us (33%)
  waiting for transfers between devices  12.5 us (15%)
  local copies, waits for them, and re-layouts  2.6 us (3%)
    pallas_call x7, Pallas kernels, attend(): pl.pallas_call(functools.partial(attend_kernel, blocks=len(kv), sets=sets...  22.5 us
    ppermute x14, starting transfers between devices, send_heads(): return lax.ppermute(array, 'heads', heads_shift(*step))  20.4 us
    ppermute x12, starting transfers between devices, send(): return lax.ppermute(array, 'frames', frames_shift(dy, dz, dc))  18.7 us
    ppermute x12, waiting for transfers between devices, send(): return lax.ppermute(array, 'frames', frames_shift(dy, dz, dc))  6.58 us
    ppermute x14, waiting for transfers between devices, send_heads(): return lax.ppermute(array, 'heads', heads_shift(*step))  5.94 us
    unnamed x16, local copies, waits for them, and re-layouts  2.51 us
    pallas_call x1, Pallas kernels, project(): pl.pallas_call(project_kernel, out_shape=(shape, shape), in_specs=whole(1...  1.69 us
  transfers between devices with their start and end apart: 26, of which 9 were waited for; matrix products, arithmetic and copies ran while one was open for 0% of the time, Pallas kernels for 28%

profile of v4, /device:TPU:8, one launch (start us, length us, event | category | flops | bytes accessed | tf_op | source)
XLA Modules:
  0.0 81.7 jit_solution(16673221963218698561)
XLA Ops:
  0.0 2.2 %collective-permute-start = (bf16[512,128]{1,0:T(8,128)(2,1)}, bf16[512,128]{1,0:T(8,128)(2,1)S(1)}, u32[]{:S(2)}, u32[]{:S(2)}) collective-permute-start(bf16[512,128]{1,0:T(8,128)(2,1)} %tokens_ref.1), channel_id=1, source_target_pairs={{0,1},{1,0},{2,3},{3,2},{4,5},{5,4},{6,7},{7,6},{8,9},{9,8},{10,11... | collective-permute-start | bytes 393224 | tf_op jit(solution)/shard_map/ppermute | solution.py:48
  2.2 1.3 %collective-permute-start.3 = (bf16[512,128]{1,0:T(8,128)(2,1)}, bf16[512,128]{1,0:T(8,128)(2,1)S(1)}, u32[]{:S(2)}, u32[]{:S(2)}) collective-permute-start(bf16[512,128]{1,0:T(8,128)(2,1)} %tokens_ref.1), channel_id=1, source_target_pairs={{0,4},{1,5},{2,6},{3,7},{4,0},{5,1},{6,2},{7,3},{8,12},{9,13},{10,... | collective-permute-start | bytes 393224 | tf_op jit(solution)/shard_map/ppermute | solution.py:48
  4.1 2.6 %collective-permute-start.2 = (bf16[512,128]{1,0:T(8,128)(2,1)}, bf16[512,128]{1,0:T(8,128)(2,1)S(1)}, u32[]{:S(2)}, u32[]{:S(2)}) collective-permute-start(bf16[512,128]{1,0:T(8,128)(2,1)} %tokens_ref.1), channel_id=1, source_target_pairs={{0,6},{1,7},{2,0},{3,1},{4,2},{5,3},{6,4},{7,5},{8,14},{9,15},{10,... | collective-permute-start | bytes 393224 | tf_op jit(solution)/shard_map/ppermute | solution.py:48
  6.9 3.0 %collective-permute-start.5 = (bf16[512,128]{1,0:T(8,128)(2,1)S(1)}, bf16[512,128]{1,0:T(8,128)(2,1)S(1)}, u32[]{:S(2)}, u32[]{:S(2)}) collective-permute-start(bf16[512,128]{1,0:T(8,128)(2,1)S(1)} %collective-permute-done.refs_1_), channel_id=1, source_target_pairs={{0,6},{1,7},{2,0},{3,1},{4,2},{5,3},{6,4},{7,5},{8,14},{9,15},{10,... | collective-permute-start | bytes 393224 | tf_op jit(solution)/shard_map/ppermute | solution.py:48
  10.0 1.6 %collective-permute-start.6 = (bf16[512,128]{1,0:T(8,128)(2,1)S(1)}, bf16[512,128]{1,0:T(8,128)(2,1)S(1)}, u32[]{:S(2)}, u32[]{:S(2)}) collective-permute-start(bf16[512,128]{1,0:T(8,128)(2,1)S(1)} %collective-permute-done.3.refs_4_), channel_id=1, source_target_pairs={{0,1},{1,0},{2,3},{3,2},{4,5},{5,4},{6,7},{7,6},{8,9},{9,8},{10,11... | collective-permute-start | bytes 393224 | tf_op jit(solution)/shard_map/ppermute | solution.py:48
  12.2 0.9 %copy-done.4 = bf16[1024,128]{1,0:T(8,128)(2,1)S(1)} copy-done((bf16[1024,128]{1,0:T(8,128)(2,1)S(1)}, bf16[1024,128]{1,0:T(8,128)(2,1)}, u32[]{:S(2)}) %copy-start.4) | copy-done | bytes 262168
  13.2 0.9 %copy-done.5 = bf16[1024,128]{1,0:T(8,128)(2,1)S(1)} copy-done((bf16[1024,128]{1,0:T(8,128)(2,1)S(1)}, bf16[1024,128]{1,0:T(8,128)(2,1)}, u32[]{:S(2)}) %copy-start.5) | copy-done | bytes 262168
  14.1 1.1 %prepare.1 = (bf16[384,1024]{1,0:T(8,128)(2,1)S(1)}, f32[16,128]{1,0:T(8,128)S(1)}) custom-call(s32[17]{0:T(128)S(1)} %stack.65.place_ref, bf16[1024,128]{1,0:T(8,128)(2,1)S(1)} %copy-done.3, bf16[1024,128]{1,0:T(8,128)(2,1)S(1)} %copy-done.4, bf16[1024,128]{1,0:T(8,128)(2,1)S(1)} %copy-done.5, f32[8,128]{1,0:T(8,128)S(1)} %bitcast.19, f32[8,128]{1,0:T(8,128)S(1)} %bitcast.20), custom_call_target="tpu_custom_call" | custom-call | flops 402653184 | bytes 4194304 | tf_op jit(solution)/shard_map/prepare/pallas_call | solution.py:96
  15.3 1.7 %norm_project.1 = (bf16[192,512]{1,0:T(8,128)(2,1)S(1)}, bf16[192,512]{1,0:T(8,128)(2,1)S(1)}) custom-call(bf16[512,128]{1,0:T(8,128)(2,1)S(1)} %copy-done, bf16[512,128]{1,0:T(8,128)(2,1)S(1)} %collective-permute-done.refs_1_, bf16[512,128]{1,0:T(8,128)(2,1)S(1)} %collective-permute-done.1.refs_2_, bf16[512,128]{1,0:T(8,128)(2,1)S(1)} %collective-permute-done.2.refs_3_, ...), custom_call_target="tpu_custom_call" | custom-call | flops 402653184 | bytes 2097152 | tf_op jit(solution)/shard_map/norm_project/pallas_call | solution.py:177
  17.1 1.4 %collective-permute-done.7.taken = bf16[192,512]{1,0:T(8,128)(2,1)S(1)} collective-permute-done((bf16[192,512]{1,0:T(8,128)(2,1)S(1)}, bf16[192,512]{1,0:T(8,128)(2,1)S(1)}, u32[]{:S(2)}, u32[]{:S(2)}) %collective-permute-start.7) | collective-permute-done | bytes 196640 | tf_op jit(solution)/shard_map/ppermute | solution.py:34
  18.6 2.0 %collective-permute-start.9 = (bf16[128,1024]{1,0:T(8,128)(2,1)S(1)}, bf16[128,1024]{1,0:T(8,128)(2,1)S(1)}, u32[]{:S(2)}, u32[]{:S(2)}) collective-permute-start(bf16[128,1024]{1,0:T(8,128)(2,1)S(1)} %get-tuple-element.57.after_ref.refs_0_), channel_id=1, source_target_pairs={{0,16},{8,24},{16,32},{24,40},{32,48},{40,56},{48,64},{56,72},{64,... | collective-permute-start | bytes 786440 | tf_op jit(solution)/shard_map/ppermute | solution.py:34
  20.6 4.0 %collective-permute-start.8 = (bf16[128,1024]{1,0:T(8,128)(2,1)S(1)}, bf16[128,1024]{1,0:T(8,128)(2,1)S(1)}, u32[]{:S(2)}, u32[]{:S(2)}) collective-permute-start(bf16[128,1024]{1,0:T(8,128)(2,1)S(1)} %get-tuple-element.57.after_ref.refs_0_), channel_id=1, source_target_pairs={{0,112},{8,120},{16,0},{24,8},{32,16},{40,24},{48,32},{56,40},{64,... | collective-permute-start | bytes 786440 | tf_op jit(solution)/shard_map/ppermute | solution.py:34
  24.6 2.3 %collective-permute-start.11 = (bf16[64,1024]{1,0:T(8,128)(2,1)S(1)}, bf16[64,1024]{1,0:T(8,128)(2,1)S(1)}, u32[]{:S(2)}, u32[]{:S(2)}) collective-permute-start(bf16[64,1024]{1,0:T(8,128)(2,1)S(1)} %get-tuple-element.59.refs_1_.refs_3_.refs_2_), channel_id=1, source_target_pairs={{0,128},{8,136},{16,144},{24,152},{32,160},{40,168},{48,176},{56,1... | collective-permute-start | bytes 393224 | tf_op jit(solution)/shard_map/ppermute | solution.py:34
  27.5 1.8 %attend.7 = (f32[1,1024]{1,0:T(1,128)S(1)}, f32[1,1024]{1,0:T(1,128)S(1)}, f32[64,1024]{1,0:T(8,128)S(1)}) custom-call(bf16[128,1024]{1,0:T(8,128)(2,1)S(1)} %get-tuple-element.57.after_ref.refs_0_, bf16[64,1024]{1,0:T(8,128)(2,1)S(1)} %get-tuple-element.59.refs_1_.refs_3_.refs_2_), custom_call_target="tpu_custom_call" | custom-call | flops 1073741824 | bytes 1048576 | tf_op jit(solution)/shard_map/attend/pallas_call | solution.py:314
  29.3 1.8 %collective-permute-done.9.refs_1_ = bf16[128,1024]{1,0:T(8,128)(2,1)S(1)} collective-permute-done((bf16[128,1024]{1,0:T(8,128)(2,1)S(1)}, bf16[128,1024]{1,0:T(8,128)(2,1)S(1)}, u32[]{:S(2)}, u32[]{:S(2)}) %collective-permute-start.9) | collective-permute-done | bytes 262176 | tf_op jit(solution)/shard_map/ppermute | solution.py:34
  31.1 3.2 %collective-permute-start.14 = (bf16[128,1024]{1,0:T(8,128)(2,1)S(1)}, bf16[128,1024]{1,0:T(8,128)(2,1)S(1)}, u32[]{:S(2)}, u32[]{:S(2)}) collective-permute-start(bf16[128,1024]{1,0:T(8,128)(2,1)S(1)} %collective-permute-done.8.refs_2_.refs_0_), channel_id=1, source_target_pairs={{0,112},{8,120},{16,0},{24,8},{32,16},{40,24},{48,32},{56,40},{64,... | collective-permute-start | bytes 786440 | tf_op jit(solution)/shard_map/ppermute | solution.py:34
  34.3 4.9 %attend.8 = (f32[1,1024]{1,0:T(1,128)S(1)}, f32[1,1024]{1,0:T(1,128)S(1)}, f32[64,1024]{1,0:T(8,128)S(1)}, f32[1,1024]{1,0:T(1,128)S(1)}, f32[1,1024]{1,0:T(1,128)S(1)}, /*index=5*/f32[64,1024]{1,0:T(8,128)S(1)}) custom-call(bf16[128,1024]{1,0:T(8,128)(2,1)S(1)} %get-tuple-element.57.after_ref.refs_0_, bf16[128,1024]{1,0:T(8,128)(2,1)S(1)} %collective-permute-done.9.refs_1_, ...), custom_call_target="tpu_custom_call" | custom-call | flops 4294967296 | bytes 1048576 | tf_op jit(solution)/shard_map/attend/pallas_call | solution.py:314
  39.3 0.9 %collective-permute-done.10.refs_0_ = bf16[128,1024]{1,0:T(8,128)(2,1)S(1)} collective-permute-done((bf16[128,1024]{1,0:T(8,128)(2,1)S(1)}, bf16[128,1024]{1,0:T(8,128)(2,1)S(1)}, u32[]{:S(2)}, u32[]{:S(2)}) %collective-permute-start.10) | collective-permute-done | bytes 262176 | tf_op jit(solution)/shard_map/ppermute | solution.py:34
  40.2 3.2 %collective-permute-start.15 = (bf16[128,1024]{1,0:T(8,128)(2,1)S(1)}, bf16[128,1024]{1,0:T(8,128)(2,1)S(1)}, u32[]{:S(2)}, u32[]{:S(2)}) collective-permute-start(bf16[128,1024]{1,0:T(8,128)(2,1)S(1)} %collective-permute-done.14.refs_1_.refs_0_), channel_id=1, source_target_pairs={{0,112},{8,120},{16,0},{24,8},{32,16},{40,24},{48,32},{56,40},{64,... | collective-permute-start | bytes 786440 | tf_op jit(solution)/shard_map/ppermute | solution.py:34
  43.4 4.2 %attend.9 = (f32[1,1024]{1,0:T(1,128)S(1)}, f32[1,1024]{1,0:T(1,128)S(1)}, f32[64,1024]{1,0:T(8,128)S(1)}, f32[1,1024]{1,0:T(1,128)S(1)}, f32[1,1024]{1,0:T(1,128)S(1)}, /*index=5*/f32[64,1024]{1,0:T(8,128)S(1)}) custom-call(bf16[128,1024]{1,0:T(8,128)(2,1)S(1)} %collective-permute-done.10.refs_0_, ...), custom_call_target="tpu_custom_call" | custom-call | flops 3221225472 | bytes 1048576 | tf_op jit(solution)/shard_map/attend/pallas_call | solution.py:314
  48.3 1.7 %attend.10 = (f32[1,1024]{1,0:T(1,128)S(1)}, f32[1,1024]{1,0:T(1,128)S(1)}, f32[64,1024]{1,0:T(8,128)S(1)}) custom-call(bf16[128,1024]{1,0:T(8,128)(2,1)S(1)} %collective-permute-done.14.refs_1_.refs_0_, bf16[64,1024]{1,0:T(8,128)(2,1)S(1)} %collective-permute-done.11.refs_4_.refs_3_.refs_1_, f32[1,1024]{1,0:T(1,128)S(1)} %get-tuple-element.75.refs_2_, ...), custom_call_target="tpu_custom_call" | custom-call | flops 1073741824 | bytes 1048576 | tf_op jit(solution)/shard_map/attend/pallas_call | solution.py:314
  50.1 5.0 %attend.11 = (f32[1,1024]{1,0:T(1,128)S(1)}, f32[1,1024]{1,0:T(1,128)S(1)}, f32[64,1024]{1,0:T(8,128)S(1)}, f32[1,1024]{1,0:T(1,128)S(1)}, f32[1,1024]{1,0:T(1,128)S(1)}, /*index=5*/f32[64,1024]{1,0:T(8,128)S(1)}) custom-call(bf16[128,1024]{1,0:T(8,128)(2,1)S(1)} %collective-permute-done.12.refs_5_.refs_0_, ...), custom_call_target="tpu_custom_call" | custom-call | flops 4294967296 | bytes 1048576 | tf_op jit(solution)/shard_map/attend/pallas_call | solution.py:314
  55.9 1.8 %attend.13 = (bf16[80,512]{1,0:T(8,128)(2,1)S(1)}, bf16[80,512]{1,0:T(8,128)(2,1)S(1)}) custom-call(bf16[128,1024]{1,0:T(8,128)(2,1)S(1)} %collective-permute-done.13.refs_1_.refs_0_, bf16[64,1024]{1,0:T(8,128)(2,1)S(1)} %collective-permute-done.11.refs_4_.refs_3_.refs_1_, f32[1,1024]{1,0:T(1,128)S(1)} %get-tuple-element.87.refs_2_, ...), custom_call_target="tpu_custom_call" | custom-call | flops 1073741824 | bytes 1048576 | tf_op jit(solution)/shard_map/attend/pallas_call | solution.py:314
  57.7 2.4 %collective-permute-start.16 = (bf16[80,512]{1,0:T(8,128)(2,1)S(1)}, bf16[80,512]{1,0:T(8,128)(2,1)S(1)}, u32[]{:S(2)}, u32[]{:S(2)}) collective-permute-start(bf16[80,512]{1,0:T(8,128)(2,1)S(1)} %get-tuple-element.90), channel_id=1, source_target_pairs={{0,128},{8,136},{16,144},{24,152},{32,160},{40,168},{48,176},{56,1... | collective-permute-start | bytes 245768 | tf_op jit(solution)/shard_map/ppermute | solution.py:34
  60.0 3.1 %attend.12 = (bf16[80,512]{1,0:T(8,128)(2,1)S(1)}, f32[1,512]{1,0:T(1,128)S(1)}, f32[1,512]{1,0:T(1,128)S(1)}, f32[64,512]{1,0:T(8,128)S(1)}) custom-call(bf16[128,1024]{1,0:T(8,128)(2,1)S(1)} %collective-permute-done.8.refs_2_.refs_0_, bf16[128,1024]{1,0:T(8,128)(2,1)S(1)} %collective-permute-done.13.refs_1_.refs_0_, ...), custom_call_target="tpu_custom_call" | custom-call | flops 2147483648 | bytes 1048576 | tf_op jit(solution)/shard_map/attend/pallas_call | solution.py:314
  63.1 1.4 %collective-permute-start.17 = (bf16[80,512]{1,0:T(8,128)(2,1)S(1)}, bf16[80,512]{1,0:T(8,128)(2,1)S(1)}, u32[]{:S(2)}, u32[]{:S(2)}) collective-permute-start(bf16[80,512]{1,0:T(8,128)(2,1)S(1)} %get-tuple-element.91), channel_id=1, source_target_pairs={{0,8},{8,0},{16,24},{24,16},{32,40},{40,32},{48,56},{56,48},{64,72... | collective-permute-start | bytes 245768 | tf_op jit(solution)/shard_map/ppermute | solution.py:34
  64.6 0.9 %collective-permute-done.18.diagonal_ref = bf16[80,512]{1,0:T(8,128)(2,1)S(1)} collective-permute-done((bf16[80,512]{1,0:T(8,128)(2,1)S(1)}, bf16[80,512]{1,0:T(8,128)(2,1)S(1)}, u32[]{:S(2)}, u32[]{:S(2)}) %collective-permute-start.18) | collective-permute-done | bytes 81952 | tf_op jit(solution)/shard_map/ppermute | solution.py:34
  66.0 1.8 %collective-permute-start.22 = (bf16[512,128]{1,0:T(8,128)(2,1)S(1)}, bf16[512,128]{1,0:T(8,128)(2,1)S(1)}, u32[]{:S(2)}, u32[]{:S(2)}) collective-permute-start(bf16[512,128]{1,0:T(8,128)(2,1)S(1)} %get-tuple-element.97), channel_id=1, source_target_pairs={{0,1},{1,0},{2,3},{3,2},{4,5},{5,4},{6,7},{7,6},{8,9},{9,8},{10,11... | collective-permute-start | bytes 393224 | tf_op jit(solution)/shard_map/ppermute | solution.py:48
  67.8 3.2 %collective-permute-start.20 = (bf16[512,128]{1,0:T(8,128)(2,1)S(1)}, bf16[512,128]{1,0:T(8,128)(2,1)S(1)}, u32[]{:S(2)}, u32[]{:S(2)}) collective-permute-start(bf16[512,128]{1,0:T(8,128)(2,1)S(1)} %get-tuple-element.95), channel_id=1, source_target_pairs={{0,6},{1,7},{2,0},{3,1},{4,2},{5,3},{6,4},{7,5},{8,14},{9,15},{10,... | collective-permute-start | bytes 393224 | tf_op jit(solution)/shard_map/ppermute | solution.py:48
  71.1 3.2 %collective-permute-start.25 = (bf16[512,128]{1,0:T(8,128)(2,1)S(1)}, bf16[512,128]{1,0:T(8,128)(2,1)S(1)}, u32[]{:S(2)}, u32[]{:S(2)}) collective-permute-start(bf16[512,128]{1,0:T(8,128)(2,1)S(1)} %get-tuple-element.99), channel_id=1, source_target_pairs={{0,6},{1,7},{2,0},{3,1},{4,2},{5,3},{6,4},{7,5},{8,14},{9,15},{10,... | collective-permute-start | bytes 393224 | tf_op jit(solution)/shard_map/ppermute | solution.py:48
  75.0 3.7 %collective-permute-done.24.refs_2_ = bf16[512,128]{1,0:T(8,128)(2,1)S(1)} collective-permute-done((bf16[512,128]{1,0:T(8,128)(2,1)S(1)}, bf16[512,128]{1,0:T(8,128)(2,1)S(1)}, u32[]{:S(2)}, u32[]{:S(2)}) %collective-permute-start.24) | collective-permute-done | bytes 131104 | tf_op jit(solution)/shard_map/ppermute | solution.py:48
  79.2 1.7 %collective-permute-done.23.refs_1_ = bf16[512,128]{1,0:T(8,128)(2,1)S(1)} collective-permute-done((bf16[512,128]{1,0:T(8,128)(2,1)S(1)}, bf16[512,128]{1,0:T(8,128)(2,1)S(1)}, u32[]{:S(2)}, u32[]{:S(2)}) %collective-permute-start.23) | collective-permute-done | bytes 131104 | tf_op jit(solution)/shard_map/ppermute | solution.py:48
  (52 shorter events, 6.3 us)
Async XLA Ops:
  0.0 11.6 %copy-start.3 = (bf16[1024,128]{1,0:T(8,128)(2,1)S(1)}, bf16[1024,128]{1,0:T(8,128)(2,1)}, u32[]{:S(2)}) copy-start(bf16[1024,128]{1,0:T(8,128)(2,1)} %wq_hbm.1) | copy-start | bytes 786436
  0.0 6.7 %collective-permute-start = (bf16[512,128]{1,0:T(8,128)(2,1)}, bf16[512,128]{1,0:T(8,128)(2,1)S(1)}, u32[]{:S(2)}, u32[]{:S(2)}) collective-permute-start(bf16[512,128]{1,0:T(8,128)(2,1)} %tokens_ref.1), channel_id=1, source_target_pairs={{0,1},{1,0},{2,3},{3,2},{4,5},{5,4},{6,7},{7,6},{8,9},{9,8},{10,11... | collective-permute-start | bytes 393224 | tf_op jit(solution)/shard_map/ppermute | solution.py:48
  2.2 7.8 %collective-permute-start.3 = (bf16[512,128]{1,0:T(8,128)(2,1)}, bf16[512,128]{1,0:T(8,128)(2,1)S(1)}, u32[]{:S(2)}, u32[]{:S(2)}) collective-permute-start(bf16[512,128]{1,0:T(8,128)(2,1)} %tokens_ref.1), channel_id=1, source_target_pairs={{0,4},{1,5},{2,6},{3,7},{4,0},{5,1},{6,2},{7,3},{8,12},{9,13},{10,... | collective-permute-start | bytes 393224 | tf_op jit(solution)/shard_map/ppermute | solution.py:48
  3.5 11.8 %collective-permute-start.1 = (bf16[512,128]{1,0:T(8,128)(2,1)}, bf16[512,128]{1,0:T(8,128)(2,1)S(1)}, u32[]{:S(2)}, u32[]{:S(2)}) collective-permute-start(bf16[512,128]{1,0:T(8,128)(2,1)} %tokens_ref.1), channel_id=1, source_target_pairs={{0,2},{1,3},{2,4},{3,5},{4,6},{5,7},{6,0},{7,1},{8,10},{9,11},{10,... | collective-permute-start | bytes 393224 | tf_op jit(solution)/shard_map/ppermute | solution.py:48
  4.1 11.2 %collective-permute-start.2 = (bf16[512,128]{1,0:T(8,128)(2,1)}, bf16[512,128]{1,0:T(8,128)(2,1)S(1)}, u32[]{:S(2)}, u32[]{:S(2)}) collective-permute-start(bf16[512,128]{1,0:T(8,128)(2,1)} %tokens_ref.1), channel_id=1, source_target_pairs={{0,6},{1,7},{2,0},{3,1},{4,2},{5,3},{6,4},{7,5},{8,14},{9,15},{10,... | collective-permute-start | bytes 393224 | tf_op jit(solution)/shard_map/ppermute | solution.py:48
  6.7 8.5 %collective-permute-start.4 = (bf16[512,128]{1,0:T(8,128)(2,1)S(1)}, bf16[512,128]{1,0:T(8,128)(2,1)S(1)}, u32[]{:S(2)}, u32[]{:S(2)}) collective-permute-start(bf16[512,128]{1,0:T(8,128)(2,1)S(1)} %collective-permute-done.refs_1_), channel_id=1, source_target_pairs={{0,2},{1,3},{2,4},{3,5},{4,6},{5,7},{6,0},{7,1},{8,10},{9,11},{10,... | collective-permute-start | bytes 393224 | tf_op jit(solution)/shard_map/ppermute | solution.py:48
  6.9 8.3 %collective-permute-start.5 = (bf16[512,128]{1,0:T(8,128)(2,1)S(1)}, bf16[512,128]{1,0:T(8,128)(2,1)S(1)}, u32[]{:S(2)}, u32[]{:S(2)}) collective-permute-start(bf16[512,128]{1,0:T(8,128)(2,1)S(1)} %collective-permute-done.refs_1_), channel_id=1, source_target_pairs={{0,6},{1,7},{2,0},{3,1},{4,2},{5,3},{6,4},{7,5},{8,14},{9,15},{10,... | collective-permute-start | bytes 393224 | tf_op jit(solution)/shard_map/ppermute | solution.py:48
  10.0 5.3 %collective-permute-start.6 = (bf16[512,128]{1,0:T(8,128)(2,1)S(1)}, bf16[512,128]{1,0:T(8,128)(2,1)S(1)}, u32[]{:S(2)}, u32[]{:S(2)}) collective-permute-start(bf16[512,128]{1,0:T(8,128)(2,1)S(1)} %collective-permute-done.3.refs_4_), channel_id=1, source_target_pairs={{0,1},{1,0},{2,3},{3,2},{4,5},{5,4},{6,7},{7,6},{8,9},{9,8},{10,11... | collective-permute-start | bytes 393224 | tf_op jit(solution)/shard_map/ppermute | solution.py:48
  12.2 0.9 %copy-start.4 = (bf16[1024,128]{1,0:T(8,128)(2,1)S(1)}, bf16[1024,128]{1,0:T(8,128)(2,1)}, u32[]{:S(2)}) copy-start(bf16[1024,128]{1,0:T(8,128)(2,1)} %wk_hbm.1) | copy-start | bytes 786436
  13.2 0.9 %copy-start.5 = (bf16[1024,128]{1,0:T(8,128)(2,1)S(1)}, bf16[1024,128]{1,0:T(8,128)(2,1)}, u32[]{:S(2)}) copy-start(bf16[1024,128]{1,0:T(8,128)(2,1)} %wv_hbm.1) | copy-start | bytes 786436
  14.1 1.1 %copy-start = (bf16[512,128]{1,0:T(8,128)(2,1)S(1)}, bf16[512,128]{1,0:T(8,128)(2,1)}, u32[]{:S(2)}) copy-start(bf16[512,128]{1,0:T(8,128)(2,1)} %tokens_ref.1) | copy-start | bytes 393220
  17.0 9.9 %copy-start.1 = (bf16[128,1024]{1,0:T(8,128)(2,1)S(1)}, bf16[128,1024]{1,0:T(8,128)(2,1)}, u32[]{:S(2)}) copy-start(bf16[128,1024]{1,0:T(8,128)(2,1)} %w_ref.1) | copy-start | bytes 786436
  17.0 1.5 %collective-permute-start.7 = (bf16[192,512]{1,0:T(8,128)(2,1)S(1)}, bf16[192,512]{1,0:T(8,128)(2,1)S(1)}, u32[]{:S(2)}, u32[]{:S(2)}) collective-permute-start(bf16[192,512]{1,0:T(8,128)(2,1)S(1)} %get-tuple-element.56), channel_id=1, source_target_pairs={{0,8},{8,0},{16,24},{24,16},{32,40},{40,32},{48,56},{56,48},{64,72... | collective-permute-start | bytes 589832 | tf_op jit(solution)/shard_map/ppermute | solution.py:34
  18.6 12.5 %collective-permute-start.9 = (bf16[128,1024]{1,0:T(8,128)(2,1)S(1)}, bf16[128,1024]{1,0:T(8,128)(2,1)S(1)}, u32[]{:S(2)}, u32[]{:S(2)}) collective-permute-start(bf16[128,1024]{1,0:T(8,128)(2,1)S(1)} %get-tuple-element.57.after_ref.refs_0_), channel_id=1, source_target_pairs={{0,16},{8,24},{16,32},{24,40},{32,48},{40,56},{48,64},{56,72},{64,... | collective-permute-start | bytes 786440 | tf_op jit(solution)/shard_map/ppermute | solution.py:34
  20.6 10.6 %collective-permute-start.8 = (bf16[128,1024]{1,0:T(8,128)(2,1)S(1)}, bf16[128,1024]{1,0:T(8,128)(2,1)S(1)}, u32[]{:S(2)}, u32[]{:S(2)}) collective-permute-start(bf16[128,1024]{1,0:T(8,128)(2,1)S(1)} %get-tuple-element.57.after_ref.refs_0_), channel_id=1, source_target_pairs={{0,112},{8,120},{16,0},{24,8},{32,16},{40,24},{48,32},{56,40},{64,... | collective-permute-start | bytes 786440 | tf_op jit(solution)/shard_map/ppermute | solution.py:34
  24.6 2.3 %copy-start.2 = (f32[128]{0:T(128)S(1)}, f32[128]{0:T(128)}, u32[]{:S(2)}) copy-start(f32[128]{0:T(128)} %param.15) | copy-start | bytes 1540
  24.6 9.8 %collective-permute-start.11 = (bf16[64,1024]{1,0:T(8,128)(2,1)S(1)}, bf16[64,1024]{1,0:T(8,128)(2,1)S(1)}, u32[]{:S(2)}, u32[]{:S(2)}) collective-permute-start(bf16[64,1024]{1,0:T(8,128)(2,1)S(1)} %get-tuple-element.59.refs_1_.refs_3_.refs_2_), channel_id=1, source_target_pairs={{0,128},{8,136},{16,144},{24,152},{32,160},{40,168},{48,176},{56,1... | collective-permute-start | bytes 393224 | tf_op jit(solution)/shard_map/ppermute | solution.py:34
  31.1 9.0 %collective-permute-start.10 = (bf16[128,1024]{1,0:T(8,128)(2,1)S(1)}, bf16[128,1024]{1,0:T(8,128)(2,1)S(1)}, u32[]{:S(2)}, u32[]{:S(2)}) collective-permute-start(bf16[128,1024]{1,0:T(8,128)(2,1)S(1)} %collective-permute-done.9.refs_1_), channel_id=1, source_target_pairs={{0,16},{8,24},{16,32},{24,40},{32,48},{40,56},{48,64},{56,72},{64,... | collective-permute-start | bytes 786440 | tf_op jit(solution)/shard_map/ppermute | solution.py:34
  31.1 9.0 %collective-permute-start.14 = (bf16[128,1024]{1,0:T(8,128)(2,1)S(1)}, bf16[128,1024]{1,0:T(8,128)(2,1)S(1)}, u32[]{:S(2)}, u32[]{:S(2)}) collective-permute-start(bf16[128,1024]{1,0:T(8,128)(2,1)S(1)} %collective-permute-done.8.refs_2_.refs_0_), channel_id=1, source_target_pairs={{0,112},{8,120},{16,0},{24,8},{32,16},{40,24},{48,32},{56,40},{64,... | collective-permute-start | bytes 786440 | tf_op jit(solution)/shard_map/ppermute | solution.py:34
  40.2 8.1 %collective-permute-start.12 = (bf16[128,1024]{1,0:T(8,128)(2,1)S(1)}, bf16[128,1024]{1,0:T(8,128)(2,1)S(1)}, u32[]{:S(2)}, u32[]{:S(2)}) collective-permute-start(bf16[128,1024]{1,0:T(8,128)(2,1)S(1)} %collective-permute-done.10.refs_0_), channel_id=1, source_target_pairs={{0,16},{8,24},{16,32},{24,40},{32,48},{40,56},{48,64},{56,72},{64,... | collective-permute-start | bytes 786440 | tf_op jit(solution)/shard_map/ppermute | solution.py:34
  40.2 9.9 %collective-permute-start.15 = (bf16[128,1024]{1,0:T(8,128)(2,1)S(1)}, bf16[128,1024]{1,0:T(8,128)(2,1)S(1)}, u32[]{:S(2)}, u32[]{:S(2)}) collective-permute-start(bf16[128,1024]{1,0:T(8,128)(2,1)S(1)} %collective-permute-done.14.refs_1_.refs_0_), channel_id=1, source_target_pairs={{0,112},{8,120},{16,0},{24,8},{32,16},{40,24},{48,32},{56,40},{64,... | collective-permute-start | bytes 786440 | tf_op jit(solution)/shard_map/ppermute | solution.py:34
  48.3 7.6 %collective-permute-start.13 = (bf16[128,1024]{1,0:T(8,128)(2,1)S(1)}, bf16[128,1024]{1,0:T(8,128)(2,1)S(1)}, u32[]{:S(2)}, u32[]{:S(2)}) collective-permute-start(bf16[128,1024]{1,0:T(8,128)(2,1)S(1)} %collective-permute-done.12.refs_5_.refs_0_), channel_id=1, source_target_pairs={{0,16},{8,24},{16,32},{24,40},{32,48},{40,56},{48,64},{56,72},{64,... | collective-permute-start | bytes 786440 | tf_op jit(solution)/shard_map/ppermute | solution.py:34
  57.7 6.9 %collective-permute-start.16 = (bf16[80,512]{1,0:T(8,128)(2,1)S(1)}, bf16[80,512]{1,0:T(8,128)(2,1)S(1)}, u32[]{:S(2)}, u32[]{:S(2)}) collective-permute-start(bf16[80,512]{1,0:T(8,128)(2,1)S(1)} %get-tuple-element.90), channel_id=1, source_target_pairs={{0,128},{8,136},{16,144},{24,152},{32,160},{40,168},{48,176},{56,1... | collective-permute-start | bytes 245768 | tf_op jit(solution)/shard_map/ppermute | solution.py:34
  60.0 5.4 %collective-permute-start.18 = (bf16[80,512]{1,0:T(8,128)(2,1)S(1)}, bf16[80,512]{1,0:T(8,128)(2,1)S(1)}, u32[]{:S(2)}, u32[]{:S(2)}) collective-permute-start(bf16[80,512]{1,0:T(8,128)(2,1)S(1)} %get-tuple-element.92), channel_id=1, source_target_pairs={{0,136},{8,128},{16,152},{24,144},{32,168},{40,160},{48,184},{56,1... | collective-permute-start | bytes 245768 | tf_op jit(solution)/shard_map/ppermute | solution.py:34
  63.1 2.4 %collective-permute-start.17 = (bf16[80,512]{1,0:T(8,128)(2,1)S(1)}, bf16[80,512]{1,0:T(8,128)(2,1)S(1)}, u32[]{:S(2)}, u32[]{:S(2)}) collective-permute-start(bf16[80,512]{1,0:T(8,128)(2,1)S(1)} %get-tuple-element.91), channel_id=1, source_target_pairs={{0,8},{8,0},{16,24},{24,16},{32,40},{40,32},{48,56},{56,48},{64,72... | collective-permute-start | bytes 245768 | tf_op jit(solution)/shard_map/ppermute | solution.py:34
  66.0 8.3 %collective-permute-start.22 = (bf16[512,128]{1,0:T(8,128)(2,1)S(1)}, bf16[512,128]{1,0:T(8,128)(2,1)S(1)}, u32[]{:S(2)}, u32[]{:S(2)}) collective-permute-start(bf16[512,128]{1,0:T(8,128)(2,1)S(1)} %get-tuple-element.97), channel_id=1, source_target_pairs={{0,1},{1,0},{2,3},{3,2},{4,5},{5,4},{6,7},{7,6},{8,9},{9,8},{10,11... | collective-permute-start | bytes 393224 | tf_op jit(solution)/shard_map/ppermute | solution.py:48
  67.8 6.6 %collective-permute-start.19 = (bf16[512,128]{1,0:T(8,128)(2,1)S(1)}, bf16[512,128]{1,0:T(8,128)(2,1)S(1)}, u32[]{:S(2)}, u32[]{:S(2)}) collective-permute-start(bf16[512,128]{1,0:T(8,128)(2,1)S(1)} %get-tuple-element.94), channel_id=1, source_target_pairs={{0,2},{1,3},{2,4},{3,5},{4,6},{5,7},{6,0},{7,1},{8,10},{9,11},{10,... | collective-permute-start | bytes 393224 | tf_op jit(solution)/shard_map/ppermute | solution.py:48
  67.8 6.6 %collective-permute-start.20 = (bf16[512,128]{1,0:T(8,128)(2,1)S(1)}, bf16[512,128]{1,0:T(8,128)(2,1)S(1)}, u32[]{:S(2)}, u32[]{:S(2)}) collective-permute-start(bf16[512,128]{1,0:T(8,128)(2,1)S(1)} %get-tuple-element.95), channel_id=1, source_target_pairs={{0,6},{1,7},{2,0},{3,1},{4,2},{5,3},{6,4},{7,5},{8,14},{9,15},{10,... | collective-permute-start | bytes 393224 | tf_op jit(solution)/shard_map/ppermute | solution.py:48
  71.1 7.6 %collective-permute-start.24 = (bf16[512,128]{1,0:T(8,128)(2,1)S(1)}, bf16[512,128]{1,0:T(8,128)(2,1)S(1)}, u32[]{:S(2)}, u32[]{:S(2)}) collective-permute-start(bf16[512,128]{1,0:T(8,128)(2,1)S(1)} %get-tuple-element.98), channel_id=1, source_target_pairs={{0,2},{1,3},{2,4},{3,5},{4,6},{5,7},{6,0},{7,1},{8,10},{9,11},{10,... | collective-permute-start | bytes 393224 | tf_op jit(solution)/shard_map/ppermute | solution.py:48
  71.1 8.1 %collective-permute-start.25 = (bf16[512,128]{1,0:T(8,128)(2,1)S(1)}, bf16[512,128]{1,0:T(8,128)(2,1)S(1)}, u32[]{:S(2)}, u32[]{:S(2)}) collective-permute-start(bf16[512,128]{1,0:T(8,128)(2,1)S(1)} %get-tuple-element.99), channel_id=1, source_target_pairs={{0,6},{1,7},{2,0},{3,1},{4,2},{5,3},{6,4},{7,5},{8,14},{9,15},{10,... | collective-permute-start | bytes 393224 | tf_op jit(solution)/shard_map/ppermute | solution.py:48
  74.4 6.6 %collective-permute-start.23 = (bf16[512,128]{1,0:T(8,128)(2,1)S(1)}, bf16[512,128]{1,0:T(8,128)(2,1)S(1)}, u32[]{:S(2)}, u32[]{:S(2)}) collective-permute-start(bf16[512,128]{1,0:T(8,128)(2,1)S(1)} %add.126), channel_id=1, source_target_pairs={{0,4},{1,5},{2,6},{3,7},{4,0},{5,1},{6,2},{7,3},{8,12},{9,13},{10,... | collective-permute-start | bytes 393224 | tf_op jit(solution)/shard_map/ppermute | solution.py:48
  74.5 6.4 %collective-permute-start.21 = (bf16[512,128]{1,0:T(8,128)(2,1)S(1)}, bf16[512,128]{1,0:T(8,128)(2,1)S(1)}, u32[]{:S(2)}, u32[]{:S(2)}) collective-permute-start(bf16[512,128]{1,0:T(8,128)(2,1)S(1)} %add.125), channel_id=1, source_target_pairs={{0,1},{1,0},{2,3},{3,2},{4,5},{5,4},{6,7},{7,6},{8,9},{9,8},{10,11... | collective-permute-start | bytes 393224 | tf_op jit(solution)/shard_map/ppermute | solution.py:48
  (2 other events, 1.4 us)
